TPU v7x, 32 devices: a whole 2x2x4 slice. The times are simulated.
32 devices in a mesh: pipe: 8 (over z, y), cross: 4 (over x, core).
Axes of the slice: x: 2, y: 2, z: 4, core: 2. Of those that a mesh axis runs over, the one named last changes fastest.
Arguments:
- state: float32 [5, 128, 9216], P(None, 'pipe', 'cross')
- face_diffusion: float32 [128, 9216], P('pipe', 'cross')
- courant: float32 [128, 9216], P('pipe', 'cross'), may hold values from -0.5 to 0.5
- cell_mask: int32 [128, 9216], P('pipe', 'cross'), may hold values from 0 to 1, as said below
- ghost_cell: int32 [4096], P(('pipe', 'cross')), may hold values from 0 to 36863, as said below
- ghost_owner: int32 [4096], P(('pipe', 'cross')), may hold values from 0 to 31, as said below
- ghost_image: int32 [4096], P(('pipe', 'cross')), may hold values from 0 to 255
- image_base: int32 [8192], P(('pipe', 'cross')), may hold values from 0 to 34462, as said below
- image_weight: float32 [8, 8192], P(None, ('pipe', 'cross')), may hold values from 0 to 0.25
Outputs:
- derivative: float32 [5, 128, 9216], P(None, 'pipe', 'cross')
- segment: float32 [5, 128, 9216], P(None, 'pipe', 'cross')
Inputs may be any that keep to these rules, and one draw needn't show every extreme that they name: `ghost_cell`: within one device's 128 entries the places are distinct, each a place of that device's block, and cell_mask is 1 at each of them. `ghost_owner`: A device number. Among one device's 128 ghost cells at most 8 name the same owner; one owner, the same for every device, is named by exactly 8 ghost cells of every device. `image_base`: the base row is at most 14, and the base pencil q has q + 97 inside the device's pencils and q + 1 on the same line of 96 pencils. `cell_mask`: 1 marks a solid cell.
All inputs are finite; a program needn't handle non-finite values.
Results may differ from a plain program's by a relative error of at most 0.0003.
Values sent between devices are 32-bit elements; how exact they have to be, the bound alone decides.
No kernel may reach another device: no remote copies, remote signals or barrier semaphores. Data moves between devices by JAX's collectives and lax.ppermute only.
A program may use at most 128 MiB of HBM per device.

v0:
```python
import jax
import jax.numpy as jnp
from jax import lax
from jax.sharding import PartitionSpec as P

LINE = 96


REFLECT = (1.0, -1.0, -1.0, -1.0, 1.0)


def with_halo(x, sides, width):
    for axis, dim in sides:
        count, length = (lax.axis_size(axis), x.shape[dim])
        up = [(i, (i + 1) % count) for i in range(count - 1)]
        down = [(j, i) for i, j in up]
        last = lax.slice_in_dim(x, length - width, length, axis=dim)
        first = lax.slice_in_dim(x, 0, width, axis=dim)
        before = lax.ppermute(last, axis, up)
        after = lax.ppermute(first, axis, down)
        x = jnp.concatenate([before, x, after], axis=dim)
    return x


def passed_along(block, axis, distance):
    devices = range(lax.axis_size(axis))
    route = [(i - distance, i) for i in devices if i - distance in devices]
    return lax.ppermute(block, axis, route)


def corner_offsets(pencils):
    return jnp.array(
        [0, 1, LINE, LINE + 1, pencils, pencils + 1, pencils + LINE, pencils + LINE + 1], jnp.int32
    )


def combine(panels, lower_rows, upper_rows, has_lower, has_upper):
    lower_diag = jnp.where(has_lower, lower_rows[1], 1.0)
    upper_diag = jnp.where(has_upper, upper_rows[1], 1.0)
    lower_ratio = panels[0] / lower_diag
    upper_ratio = panels[2] / upper_diag
    new_lower = -lower_ratio * lower_rows[0]
    new_upper = -upper_ratio * upper_rows[2]
    new_margin = panels[3] - lower_ratio * lower_rows[3] - upper_ratio * upper_rows[3]
    new_diag = new_margin - new_lower - new_upper
    new_rhs = panels[4:] - lower_ratio * lower_rows[4:] - upper_ratio * upper_rows[4:]
    return jnp.concatenate(
        [jnp.stack([new_lower, new_diag, new_upper, new_margin]), new_rhs], axis=0
    )


def explicit_terms(padded, row_index, row_total):
    centre = padded[:, 2:-2]
    minus_one = padded[:, 1:-3]
    plus_one = padded[:, 3:-1]
    minus_two = padded[:, :-4]
    plus_two = padded[:, 4:]
    inner_terms = 7.0 / 9.0 * (plus_one - minus_one) + 1.0 / 36.0 * (plus_two - minus_two)
    near_terms = 0.75 * (plus_one - minus_one)
    first_terms = -1.5 * centre + 2.0 * plus_one - 0.5 * plus_two
    final_terms = 1.5 * centre - 2.0 * minus_one + 0.5 * minus_two
    edge_rows = (row_index == 1) | (row_index == row_total - 2)
    return jnp.where(
        row_index == 0,
        first_terms,
        jnp.where(
            row_index == row_total - 1, final_terms, jnp.where(edge_rows, near_terms, inner_terms)
        ),
    )


def derivative_panels(row_index, row_total, pencils, stencil_terms):
    edge_rows = (row_index == 1) | (row_index == row_total - 2)
    end_rows = (row_index == 0) | (row_index == row_total - 1)
    side_coef = jnp.where(end_rows, 0.0, jnp.where(edge_rows, 0.25, 1.0 / 3.0)) * jnp.ones(
        (1, pencils), jnp.float32
    )
    margin = 1.0 + side_coef + side_coef
    return jnp.concatenate(
        [jnp.stack([side_coef, jnp.ones_like(side_coef), side_coef, margin]), stencil_terms], axis=0
    )


def diffusion_panels(face_low, face_here, row_index, row_total, right_terms):
    lower_side = -face_low
    upper_side = -jnp.where(row_index == row_total - 1, 0.0, face_here)
    margin = jnp.ones_like(face_here)
    diagonal = margin - lower_side - upper_side
    return jnp.concatenate(
        [jnp.stack([lower_side, diagonal, upper_side, margin]), right_terms], axis=0
    )


def slab_solve(panels, row_index, row_total):
    row_count = panels.shape[1]
    stride = 1
    while stride < row_count:
        rimmed = with_halo(panels, (("pipe", 1),), stride)
        panels = combine(
            panels,
            rimmed[:, :row_count],
            rimmed[:, 2 * stride :],
            row_index >= stride,
            row_index < row_total - stride,
        )
        stride = stride * 2
    device_hops = 1
    while device_hops < lax.axis_size("pipe"):
        lower_rows = passed_along(panels, "pipe", device_hops)
        upper_rows = passed_along(panels, "pipe", -device_hops)
        stride = device_hops * row_count
        panels = combine(
            panels, lower_rows, upper_rows, row_index >= stride, row_index < row_total - stride
        )
        device_hops = device_hops * 2
    return panels[4:] / panels[1]


def local(
    state,
    face_diffusion,
    courant,
    cell_mask,
    ghost_cell,
    ghost_owner,
    ghost_image,
    image_base,
    image_weight,
):
    var_count, row_count, pencils = state.shape
    flat_state = state.reshape(var_count, row_count * pencils)
    corners = image_base[None, :] + corner_offsets(pencils)[:, None]
    image_values = jnp.sum(flat_state[:, corners] * image_weight[None], axis=1)
    images_here = image_values.shape[1]
    all_images = lax.all_gather(image_values, ("pipe", "cross"), axis=1, tiled=True)
    picked = all_images[:, ghost_owner * images_here + ghost_image]
    reflection = jnp.array(REFLECT, jnp.float32)[:, None]
    cleared = jnp.where(cell_mask.reshape(1, -1) == 1, 0.0, flat_state)
    filled = (
        cleared.at[:, ghost_cell].set(reflection * picked).reshape(var_count, row_count, pencils)
    )
    stacked = jnp.concatenate([filled, face_diffusion[None]], axis=0)
    rimmed = with_halo(stacked, (("pipe", 1),), 2)
    row_total = row_count * lax.axis_size("pipe")
    row_index = lax.axis_index("pipe") * row_count + lax.broadcasted_iota(
        jnp.int32, (row_count, 1), 0
    )
    stencil_terms = explicit_terms(rimmed[:var_count], row_index, row_total)
    face_low = rimmed[var_count, 1:-3]
    derivative = slab_solve(
        derivative_panels(row_index, row_total, pencils, stencil_terms), row_index, row_total
    )
    rhs_two = filled - courant[None] * derivative
    segment = slab_solve(
        diffusion_panels(face_low, face_diffusion, row_index, row_total, rhs_two),
        row_index,
        row_total,
    )
    return (derivative, segment)


def solution(mesh):
    in_specs = (
        P(None, "pipe", "cross"),
        P("pipe", "cross"),
        P("pipe", "cross"),
        P("pipe", "cross"),
        P(("pipe", "cross")),
        P(("pipe", "cross")),
        P(("pipe", "cross")),
        P(("pipe", "cross")),
        P(None, ("pipe", "cross")),
    )
    out_specs = (P(None, "pipe", "cross"), P(None, "pipe", "cross"))
    return jax.shard_map(local, mesh=mesh, in_specs=in_specs, out_specs=out_specs, check_vma=False)
```

profile of v0, /device:TPU:0, one launch (start us, length us, event | category | flops | bytes accessed | tf_op | source)
XLA Modules:
  0.0 634.4 jit_solution(1203281852547131816)
XLA Ops:
  1.7 10.7 %copy.38 = f32[5,16,2304]{0,2,1:T(8,128)} copy(f32[5,16,2304]{2,1,0:T(8,128)} %param.11) | data formatting | bytes 1474560 | tf_op args[0]
  12.5 21.1 %broadcast_select_fusion = f32[5,36864]{0,1:T(8,128)} fusion(pred[36864]{0:T(1024)(128)(4,1)S(1)} %eq.64, f32[5,16,2304]{0,2,1:T(8,128)} %copy.38), kind=kLoop, calls=%fused_computation.3 | loop fusion | flops 184320 | bytes 1511424 | tf_op jit(solution)/shard_map/jit(_where)/select_n | solution.py:138
  33.6 11.8 %gather_fusion = f32[2048,5]{1,0:T(8,128)S(1)} fusion(f32[5,36864]{0,1:T(8,128)} %bitcast.405, s32[2048]{0:T(1024)S(1)} %broadcast_clamp_fusion), kind=kCustom, calls=%fused_computation | custom fusion | bytes 90112 | tf_op jit(solution)/shard_map/gather | solution.py:133
  45.8 59.4 %all_gather.3 = f32[5,8192]{0,1:T(8,128)} all-gather(f32[5,256]{0,1:T(8,128)S(1)} %bitcast.423), channel_id=1, replica_groups=mesh['pipe'=8,'cross'=4] {'pipe','cross'}, dimensions={1}, use_global_device_ids=true | all-gather | bytes 168960 | tf_op jit(solution)/shard_map/all_gather | solution.py:135
  105.3 14.8 %scatter_custom_fusion = f32[5,36864]{0,1:T(8,128)} fusion(f32[5,36864]{0,1:T(8,128)} %broadcast_select_fusion, s32[128]{0:T(128)S(1)} %compare_select_fusion.2, f32[5]{0:T(128)S(1)} %copy-done.5, f32[5,8192]{0,1:T(8,128)} %all_gather.3, s32[1024]{0:T(1024)S(1)} %pad_clamp_fusion), kind=kCustom, calls=%fused_computation.468 | custom fusion | flops 640 | bytes 4936192 | tf_op jit(solution)/shard_map/scatter | solution.py:140
  120.0 11.1 %copy.39 = f32[5,16,2304]{2,1,0:T(8,128)S(1)} copy(f32[5,16,2304]{0,2,1:T(8,128)} %bitcast.406) | data formatting | bytes 1474560 | tf_op jit(solution)/shard_map/reshape | solution.py:140
  131.2 4.6 collective-permute-start.1
  138.7 5.8 collective-permute-done
  145.4 4.5 collective-permute-start.2
  152.1 4.5 collective-permute-done.3
  174.3 10.1 %collective-permute-done.6 = f32[9,4,2304]{2,1,0:T(4,128)S(1)} collective-permute-done((f32[9,4,2304]{2,1,0:T(4,128)S(1)}, f32[9,4,2304]{2,1,0:T(4,128)S(1)}, u32[]{:S(2)}, u32[]{:S(2)}) %collective-permute-start.6) | collective-permute-done | bytes 331808 | tf_op jit(solution)/shard_map/ppermute | solution.py:19
  185.4 4.4 collective-permute-start.8
  191.4 22.3 %collective-permute-done.8 = f32[9,8,2304]{2,1,0:T(8,128)S(1)} collective-permute-done((f32[9,8,2304]{2,1,0:T(8,128)S(1)}, f32[9,8,2304]{2,1,0:T(8,128)S(1)}, u32[]{:S(2)}, u32[]{:S(2)}) %collective-permute-start.8) | collective-permute-done | bytes 663584 | tf_op jit(solution)/shard_map/ppermute | solution.py:19
  214.5 4.5 collective-permute-start.10
  220.3 50.3 %collective-permute-done.10 = f32[9,16,2304]{2,1,0:T(8,128)S(1)} collective-permute-done((f32[9,16,2304]{2,1,0:T(8,128)S(1)}, f32[9,16,2304]{2,1,0:T(8,128)S(1)}, u32[]{:S(2)}, u32[]{:S(2)}) %collective-permute-start.10) | collective-permute-done | bytes 1327136 | tf_op jit(solution)/shard_map/ppermute | solution.py:28
  271.2 17.4 %collective-permute-start.12 = (f32[9,16,2304]{2,1,0:T(8,128)S(1)}, f32[9,16,2304]{2,1,0:T(8,128)S(1)}, u32[]{:S(2)}, u32[]{:S(2)}) collective-permute-start(f32[9,16,2304]{2,1,0:T(8,128)S(1)} %get-tuple-element.75), channel_id=1, source_target_pairs={{0,8},{4,12},{8,16},{12,20},{16,24},{20,28},{1,9},{5,13},{9,17},{1... | collective-permute-start | bytes 3981320 | tf_op jit(solution)/shard_map/ppermute | solution.py:28
  290.0 27.1 %collective-permute-done.12 = f32[9,16,2304]{2,1,0:T(8,128)S(1)} collective-permute-done((f32[9,16,2304]{2,1,0:T(8,128)S(1)}, f32[9,16,2304]{2,1,0:T(8,128)S(1)}, u32[]{:S(2)}, u32[]{:S(2)}) %collective-permute-start.12) | collective-permute-done | bytes 1327136 | tf_op jit(solution)/shard_map/ppermute | solution.py:28
  317.2 4.1 collective-permute-done.13
  322.9 5.8 collective-permute-start.14
  328.9 53.6 %collective-permute-done.15 = f32[9,16,2304]{2,1,0:T(8,128)S(1)} collective-permute-done((f32[9,16,2304]{2,1,0:T(8,128)S(1)}, f32[9,16,2304]{2,1,0:T(8,128)S(1)}, u32[]{:S(2)}, u32[]{:S(2)}) %collective-permute-start.15) | collective-permute-done | bytes 1327136 | tf_op jit(solution)/shard_map/ppermute | solution.py:28
  386.7 5.9 collective-permute-done.17
  393.5 4.8 collective-permute-start.18
  410.5 20.3 %collective-permute-done.20 = f32[9,4,2304]{2,0,1:T(8,128)S(1)} collective-permute-done((f32[9,4,2304]{2,0,1:T(8,128)S(1)}, f32[9,4,2304]{2,0,1:T(8,128)S(1)}, u32[]{:S(2)}, u32[]{:S(2)}) %collective-permute-start.20) | collective-permute-done | bytes 331808 | tf_op jit(solution)/shard_map/ppermute | solution.py:19
  432.0 4.4 collective-permute-start.22
  437.7 22.6 %collective-permute-done.22 = f32[9,8,2304]{2,1,0:T(8,128)S(1)} collective-permute-done((f32[9,8,2304]{2,1,0:T(8,128)S(1)}, f32[9,8,2304]{2,1,0:T(8,128)S(1)}, u32[]{:S(2)}, u32[]{:S(2)}) %collective-permute-start.22) | collective-permute-done | bytes 663584 | tf_op jit(solution)/shard_map/ppermute | solution.py:19
  460.8 4.5 collective-permute-start.24
  466.6 51.3 %collective-permute-done.24 = f32[9,16,2304]{2,1,0:T(8,128)S(1)} collective-permute-done((f32[9,16,2304]{2,1,0:T(8,128)S(1)}, f32[9,16,2304]{2,1,0:T(8,128)S(1)}, u32[]{:S(2)}, u32[]{:S(2)}) %collective-permute-start.24) | collective-permute-done | bytes 1327136 | tf_op jit(solution)/shard_map/ppermute | solution.py:28
  518.5 17.5 %collective-permute-start.26 = (f32[9,16,2304]{2,1,0:T(8,128)S(1)}, f32[9,16,2304]{2,1,0:T(8,128)S(1)}, u32[]{:S(2)}, u32[]{:S(2)}) collective-permute-start(f32[9,16,2304]{2,1,0:T(8,128)S(1)} %get-tuple-element.12), channel_id=1, source_target_pairs={{0,8},{4,12},{8,16},{12,20},{16,24},{20,28},{1,9},{5,13},{9,17},{1... | collective-permute-start | bytes 3981320 | tf_op jit(solution)/shard_map/ppermute | solution.py:28
  537.2 27.2 %collective-permute-done.26 = f32[9,16,2304]{2,1,0:T(8,128)S(1)} collective-permute-done((f32[9,16,2304]{2,1,0:T(8,128)S(1)}, f32[9,16,2304]{2,1,0:T(8,128)S(1)}, u32[]{:S(2)}, u32[]{:S(2)}) %collective-permute-start.26) | collective-permute-done | bytes 1327136 | tf_op jit(solution)/shard_map/ppermute | solution.py:28
  564.5 4.6 collective-permute-done.27
  574.3 26.1 %collective-permute-done.28 = f32[9,16,2304]{2,1,0:T(8,128)S(1)} collective-permute-done((f32[9,16,2304]{2,1,0:T(8,128)S(1)}, f32[9,16,2304]{2,1,0:T(8,128)S(1)}, u32[]{:S(2)}, u32[]{:S(2)}) %collective-permute-start.28) | collective-permute-done | bytes 1327136 | tf_op jit(solution)/shard_map/ppermute | solution.py:28
  600.5 32.7 %collective-permute-done.29 = f32[9,16,2304]{2,1,0:T(8,128)S(1)} collective-permute-done((f32[9,16,2304]{2,1,0:T(8,128)S(1)}, f32[9,16,2304]{2,1,0:T(8,128)S(1)}, u32[]{:S(2)}, u32[]{:S(2)}) %collective-permute-start.29) | collective-permute-done | bytes 1327136 | tf_op jit(solution)/shard_map/ppermute | solution.py:28
  (176 shorter events, 62.8 us)
Async XLA Ops:
  45.8 59.4 %copy-start.8 = (s32[128]{0:T(128)S(1)}, s32[128]{0:T(128)}, u32[]{:S(2)}) copy-start(s32[128]{0:T(128)} %param.17) | copy-start | bytes 1540
  45.8 59.4 %copy-start.5 = (f32[5]{0:T(128)S(1)}, f32[5]{0:T(128)}, u32[]{:S(2)}) copy-start(f32[5]{0:T(128)} %constant.28.clone) | copy-start | bytes 64
  131.2 7.4 %collective-permute-start.1 = (f32[6,2,2304]{2,1,0:T(2,128)S(1)}, f32[6,2,2304]{2,1,0:T(2,128)S(1)}, u32[]{:S(2)}, u32[]{:S(2)}) collective-permute-start(f32[6,2,2304]{2,1,0:T(2,128)S(1)} %get-tuple-element.158), channel_id=1, source_target_pairs={{0,4},{4,8},{8,12},{12,16},{16,20},{20,24},{24,28},{1,5},{5,9},{9,... | collective-permute-start | bytes 331784 | tf_op jit(solution)/shard_map/ppermute | solution.py:19
  135.9 8.6 %collective-permute-start = (f32[6,2,2304]{2,1,0:T(2,128)S(1)}, f32[6,2,2304]{2,1,0:T(2,128)S(1)}, u32[]{:S(2)}, u32[]{:S(2)}) collective-permute-start(f32[6,2,2304]{2,1,0:T(2,128)S(1)} %get-tuple-element.157), channel_id=1, source_target_pairs={{4,0},{8,4},{12,8},{16,12},{20,16},{24,20},{28,24},{5,1},{9,5},{13... | collective-permute-start | bytes 331784 | tf_op jit(solution)/shard_map/ppermute | solution.py:20
  145.4 6.6 %collective-permute-start.2 = (f32[9,1,2304]{2,1,0:T(1,128)S(1)}, f32[9,1,2304]{2,1,0:T(1,128)S(1)}, u32[]{:S(2)}, u32[]{:S(2)}) collective-permute-start(f32[9,1,2304]{2,1,0:T(1,128)S(1)} %get-tuple-element.154), channel_id=1, source_target_pairs={{0,4},{4,8},{8,12},{12,16},{16,20},{20,24},{24,28},{1,5},{5,9},{9,... | collective-permute-start | bytes 248840 | tf_op jit(solution)/shard_map/ppermute | solution.py:19
  150.3 6.3 %collective-permute-start.3 = (f32[9,1,2304]{2,1,0:T(1,128)S(1)}, f32[9,1,2304]{2,1,0:T(1,128)S(1)}, u32[]{:S(2)}, u32[]{:S(2)}) collective-permute-start(f32[9,1,2304]{2,1,0:T(1,128)S(1)} %get-tuple-element.153), channel_id=1, source_target_pairs={{4,0},{8,4},{12,8},{16,12},{20,16},{24,20},{28,24},{5,1},{9,5},{13... | collective-permute-start | bytes 248840 | tf_op jit(solution)/shard_map/ppermute | solution.py:20
  157.4 8.3 %collective-permute-start.4 = (f32[9,2,2304]{2,1,0:T(2,128)S(1)}, f32[9,2,2304]{2,1,0:T(2,128)S(1)}, u32[]{:S(2)}, u32[]{:S(2)}) collective-permute-start(f32[9,2,2304]{2,1,0:T(2,128)S(1)} %get-tuple-element.150), channel_id=1, source_target_pairs={{0,4},{4,8},{8,12},{12,16},{16,20},{20,24},{24,28},{1,5},{5,9},{9,... | collective-permute-start | bytes 497672 | tf_op jit(solution)/shard_map/ppermute | solution.py:19
  161.3 7.2 %collective-permute-start.5 = (f32[9,2,2304]{2,1,0:T(2,128)S(1)}, f32[9,2,2304]{2,1,0:T(2,128)S(1)}, u32[]{:S(2)}, u32[]{:S(2)}) collective-permute-start(f32[9,2,2304]{2,1,0:T(2,128)S(1)} %get-tuple-element.149), channel_id=1, source_target_pairs={{4,0},{8,4},{12,8},{16,12},{20,16},{24,20},{28,24},{5,1},{9,5},{13... | collective-permute-start | bytes 497672 | tf_op jit(solution)/shard_map/ppermute | solution.py:20
  169.2 15.2 %collective-permute-start.6 = (f32[9,4,2304]{2,1,0:T(4,128)S(1)}, f32[9,4,2304]{2,1,0:T(4,128)S(1)}, u32[]{:S(2)}, u32[]{:S(2)}) collective-permute-start(f32[9,4,2304]{2,1,0:T(4,128)S(1)} %get-tuple-element.146), channel_id=1, source_target_pairs={{0,4},{4,8},{8,12},{12,16},{16,20},{20,24},{24,28},{1,5},{5,9},{9,... | collective-permute-start | bytes 995336 | tf_op jit(solution)/shard_map/ppermute | solution.py:19
  172.7 11.9 %collective-permute-start.7 = (f32[9,4,2304]{2,1,0:T(4,128)S(1)}, f32[9,4,2304]{2,1,0:T(4,128)S(1)}, u32[]{:S(2)}, u32[]{:S(2)}) collective-permute-start(f32[9,4,2304]{2,1,0:T(4,128)S(1)} %get-tuple-element.145), channel_id=1, source_target_pairs={{4,0},{8,4},{12,8},{16,12},{20,16},{24,20},{28,24},{5,1},{9,5},{13... | collective-permute-start | bytes 995336 | tf_op jit(solution)/shard_map/ppermute | solution.py:20
  185.4 28.4 %collective-permute-start.8 = (f32[9,8,2304]{2,1,0:T(8,128)S(1)}, f32[9,8,2304]{2,1,0:T(8,128)S(1)}, u32[]{:S(2)}, u32[]{:S(2)}) collective-permute-start(f32[9,8,2304]{2,1,0:T(8,128)S(1)} %get-tuple-element.142), channel_id=1, source_target_pairs={{0,4},{4,8},{8,12},{12,16},{16,20},{20,24},{24,28},{1,5},{5,9},{9,... | collective-permute-start | bytes 1990664 | tf_op jit(solution)/shard_map/ppermute | solution.py:19
  189.8 24.1 %collective-permute-start.9 = (f32[9,8,2304]{2,1,0:T(8,128)S(1)}, f32[9,8,2304]{2,1,0:T(8,128)S(1)}, u32[]{:S(2)}, u32[]{:S(2)}) collective-permute-start(f32[9,8,2304]{2,1,0:T(8,128)S(1)} %get-tuple-element.141), channel_id=1, source_target_pairs={{4,0},{8,4},{12,8},{16,12},{20,16},{24,20},{28,24},{5,1},{9,5},{13... | collective-permute-start | bytes 1990664 | tf_op jit(solution)/shard_map/ppermute | solution.py:20
  214.5 56.1 %collective-permute-start.10 = (f32[9,16,2304]{2,1,0:T(8,128)S(1)}, f32[9,16,2304]{2,1,0:T(8,128)S(1)}, u32[]{:S(2)}, u32[]{:S(2)}) collective-permute-start(f32[9,16,2304]{2,1,0:T(8,128)S(1)} %get-tuple-element.82), channel_id=1, source_target_pairs={{0,4},{4,8},{8,12},{12,16},{16,20},{20,24},{24,28},{1,5},{5,9},{9,... | collective-permute-start | bytes 3981320 | tf_op jit(solution)/shard_map/ppermute | solution.py:28
  219.0 51.7 %collective-permute-start.11 = (f32[9,16,2304]{2,1,0:T(8,128)S(1)}, f32[9,16,2304]{2,1,0:T(8,128)S(1)}, u32[]{:S(2)}, u32[]{:S(2)}) collective-permute-start(f32[9,16,2304]{2,1,0:T(8,128)S(1)} %get-tuple-element.82), channel_id=1, source_target_pairs={{4,0},{8,4},{12,8},{16,12},{20,16},{24,20},{28,24},{5,1},{9,5},{13... | collective-permute-start | bytes 3981320 | tf_op jit(solution)/shard_map/ppermute | solution.py:28
  271.2 45.9 %collective-permute-start.12 = (f32[9,16,2304]{2,1,0:T(8,128)S(1)}, f32[9,16,2304]{2,1,0:T(8,128)S(1)}, u32[]{:S(2)}, u32[]{:S(2)}) collective-permute-start(f32[9,16,2304]{2,1,0:T(8,128)S(1)} %get-tuple-element.75), channel_id=1, source_target_pairs={{0,8},{4,12},{8,16},{12,20},{16,24},{20,28},{1,9},{5,13},{9,17},{1... | collective-permute-start | bytes 3981320 | tf_op jit(solution)/shard_map/ppermute | solution.py:28
  288.6 32.7 %collective-permute-start.13 = (f32[9,16,2304]{2,1,0:T(8,128)S(1)}, f32[9,16,2304]{2,1,0:T(8,128)S(1)}, u32[]{:S(2)}, u32[]{:S(2)}) collective-permute-start(f32[9,16,2304]{2,1,0:T(8,128)S(1)} %get-tuple-element.75), channel_id=1, source_target_pairs={{8,0},{12,4},{16,8},{20,12},{24,16},{28,20},{9,1},{13,5},{17,9},{2... | collective-permute-start | bytes 3981320 | tf_op jit(solution)/shard_map/ppermute | solution.py:28
  321.6 60.9 %collective-permute-start.15 = (f32[9,16,2304]{2,1,0:T(8,128)S(1)}, f32[9,16,2304]{2,1,0:T(8,128)S(1)}, u32[]{:S(2)}, u32[]{:S(2)}) collective-permute-start(f32[9,16,2304]{2,1,0:T(8,128)S(1)} %get-tuple-element.68), channel_id=1, source_target_pairs={{16,0},{20,4},{24,8},{28,12},{17,1},{21,5},{25,9},{29,13},{18,2},{... | collective-permute-start | bytes 3981320 | tf_op jit(solution)/shard_map/ppermute | solution.py:28
  322.9 59.6 %collective-permute-start.14 = (f32[9,16,2304]{2,1,0:T(8,128)S(1)}, f32[9,16,2304]{2,1,0:T(8,128)S(1)}, u32[]{:S(2)}, u32[]{:S(2)}) collective-permute-start(f32[9,16,2304]{2,1,0:T(8,128)S(1)} %get-tuple-element.68), channel_id=1, source_target_pairs={{0,16},{4,20},{8,24},{12,28},{1,17},{5,21},{9,25},{13,29},{2,18},{... | collective-permute-start | bytes 3981320 | tf_op jit(solution)/shard_map/ppermute | solution.py:28
  383.1 3.5 collective-permute-start.16
  384.6 8.1 %collective-permute-start.17 = (f32[9,1,2304]{2,1,0:T(1,128)S(1)}, f32[9,1,2304]{2,1,0:T(1,128)S(1)}, u32[]{:S(2)}, u32[]{:S(2)}) collective-permute-start(f32[9,1,2304]{2,1,0:T(1,128)S(1)} %get-tuple-element.137), channel_id=1, source_target_pairs={{4,0},{8,4},{12,8},{16,12},{20,16},{24,20},{28,24},{5,1},{9,5},{13... | collective-permute-start | bytes 248840 | tf_op jit(solution)/shard_map/ppermute | solution.py:20
  393.5 8.7 %collective-permute-start.18 = (f32[9,2,2304]{2,1,0:T(2,128)S(1)}, f32[9,2,2304]{2,1,0:T(2,128)S(1)}, u32[]{:S(2)}, u32[]{:S(2)}) collective-permute-start(f32[9,2,2304]{2,1,0:T(2,128)S(1)} %get-tuple-element.136), channel_id=1, source_target_pairs={{0,4},{4,8},{8,12},{12,16},{16,20},{20,24},{24,28},{1,5},{5,9},{9,... | collective-permute-start | bytes 497672 | tf_op jit(solution)/shard_map/ppermute | solution.py:19
  398.3 7.2 %collective-permute-start.19 = (f32[9,2,2304]{2,1,0:T(2,128)S(1)}, f32[9,2,2304]{2,1,0:T(2,128)S(1)}, u32[]{:S(2)}, u32[]{:S(2)}) collective-permute-start(f32[9,2,2304]{2,1,0:T(2,128)S(1)} %get-tuple-element.135), channel_id=1, source_target_pairs={{4,0},{8,4},{12,8},{16,12},{20,16},{24,20},{28,24},{5,1},{9,5},{13... | collective-permute-start | bytes 497672 | tf_op jit(solution)/shard_map/ppermute | solution.py:20
  406.3 24.5 %collective-permute-start.20 = (f32[9,4,2304]{2,0,1:T(8,128)S(1)}, f32[9,4,2304]{2,0,1:T(8,128)S(1)}, u32[]{:S(2)}, u32[]{:S(2)}) collective-permute-start(f32[9,4,2304]{2,0,1:T(8,128)S(1)} %copy.43), channel_id=1, source_target_pairs={{0,4},{4,8},{8,12},{12,16},{16,20},{20,24},{24,28},{1,5},{5,9},{9,... | collective-permute-start | bytes 995336 | tf_op jit(solution)/shard_map/ppermute | solution.py:19
  409.2 21.9 %collective-permute-start.21 = (f32[9,4,2304]{2,0,1:T(8,128)S(1)}, f32[9,4,2304]{2,0,1:T(8,128)S(1)}, u32[]{:S(2)}, u32[]{:S(2)}) collective-permute-start(f32[9,4,2304]{2,0,1:T(8,128)S(1)} %copy.45), channel_id=1, source_target_pairs={{4,0},{8,4},{12,8},{16,12},{20,16},{24,20},{28,24},{5,1},{9,5},{13... | collective-permute-start | bytes 995336 | tf_op jit(solution)/shard_map/ppermute | solution.py:20
  432.0 28.4 %collective-permute-start.22 = (f32[9,8,2304]{2,1,0:T(8,128)S(1)}, f32[9,8,2304]{2,1,0:T(8,128)S(1)}, u32[]{:S(2)}, u32[]{:S(2)}) collective-permute-start(f32[9,8,2304]{2,1,0:T(8,128)S(1)} %get-tuple-element.132), channel_id=1, source_target_pairs={{0,4},{4,8},{8,12},{12,16},{16,20},{20,24},{24,28},{1,5},{5,9},{9,... | collective-permute-start | bytes 1990664 | tf_op jit(solution)/shard_map/ppermute | solution.py:19
  436.4 24.0 %collective-permute-start.23 = (f32[9,8,2304]{2,1,0:T(8,128)S(1)}, f32[9,8,2304]{2,1,0:T(8,128)S(1)}, u32[]{:S(2)}, u32[]{:S(2)}) collective-permute-start(f32[9,8,2304]{2,1,0:T(8,128)S(1)} %get-tuple-element.131), channel_id=1, source_target_pairs={{4,0},{8,4},{12,8},{16,12},{20,16},{24,20},{28,24},{5,1},{9,5},{13... | collective-permute-start | bytes 1990664 | tf_op jit(solution)/shard_map/ppermute | solution.py:20
  460.8 57.1 %collective-permute-start.24 = (f32[9,16,2304]{2,1,0:T(8,128)S(1)}, f32[9,16,2304]{2,1,0:T(8,128)S(1)}, u32[]{:S(2)}, u32[]{:S(2)}) collective-permute-start(f32[9,16,2304]{2,1,0:T(8,128)S(1)} %get-tuple-element.20), channel_id=1, source_target_pairs={{0,4},{4,8},{8,12},{12,16},{16,20},{20,24},{24,28},{1,5},{5,9},{9,... | collective-permute-start | bytes 3981320 | tf_op jit(solution)/shard_map/ppermute | solution.py:28
  465.3 52.7 %collective-permute-start.25 = (f32[9,16,2304]{2,1,0:T(8,128)S(1)}, f32[9,16,2304]{2,1,0:T(8,128)S(1)}, u32[]{:S(2)}, u32[]{:S(2)}) collective-permute-start(f32[9,16,2304]{2,1,0:T(8,128)S(1)} %get-tuple-element.20), channel_id=1, source_target_pairs={{4,0},{8,4},{12,8},{16,12},{20,16},{24,20},{28,24},{5,1},{9,5},{13... | collective-permute-start | bytes 3981320 | tf_op jit(solution)/shard_map/ppermute | solution.py:28
  518.5 45.9 %collective-permute-start.26 = (f32[9,16,2304]{2,1,0:T(8,128)S(1)}, f32[9,16,2304]{2,1,0:T(8,128)S(1)}, u32[]{:S(2)}, u32[]{:S(2)}) collective-permute-start(f32[9,16,2304]{2,1,0:T(8,128)S(1)} %get-tuple-element.12), channel_id=1, source_target_pairs={{0,8},{4,12},{8,16},{12,20},{16,24},{20,28},{1,9},{5,13},{9,17},{1... | collective-permute-start | bytes 3981320 | tf_op jit(solution)/shard_map/ppermute | solution.py:28
  535.9 33.2 %collective-permute-start.27 = (f32[9,16,2304]{2,1,0:T(8,128)S(1)}, f32[9,16,2304]{2,1,0:T(8,128)S(1)}, u32[]{:S(2)}, u32[]{:S(2)}) collective-permute-start(f32[9,16,2304]{2,1,0:T(8,128)S(1)} %get-tuple-element.12), channel_id=1, source_target_pairs={{8,0},{12,4},{16,8},{20,12},{24,16},{28,20},{9,1},{13,5},{17,9},{2... | collective-permute-start | bytes 3981320 | tf_op jit(solution)/shard_map/ppermute | solution.py:28
  569.5 30.9 %collective-permute-start.28 = (f32[9,16,2304]{2,1,0:T(8,128)S(1)}, f32[9,16,2304]{2,1,0:T(8,128)S(1)}, u32[]{:S(2)}, u32[]{:S(2)}) collective-permute-start(f32[9,16,2304]{2,1,0:T(8,128)S(1)} %get-tuple-element.4), channel_id=1, source_target_pairs={{0,16},{4,20},{8,24},{12,28},{1,17},{5,21},{9,25},{13,29},{2,18},{... | collective-permute-start | bytes 3981320 | tf_op jit(solution)/shard_map/ppermute | solution.py:28
  573.0 60.2 %collective-permute-start.29 = (f32[9,16,2304]{2,1,0:T(8,128)S(1)}, f32[9,16,2304]{2,1,0:T(8,128)S(1)}, u32[]{:S(2)}, u32[]{:S(2)}) collective-permute-start(f32[9,16,2304]{2,1,0:T(8,128)S(1)} %get-tuple-element.4), channel_id=1, source_target_pairs={{16,0},{20,4},{24,8},{28,12},{17,1},{21,5},{25,9},{29,13},{18,2},{... | collective-permute-start | bytes 3981320 | tf_op jit(solution)/shard_map/ppermute | solution.py:28
  (8 other events, 199.5 us)
where the time goes:
time: 636 us; the launch traced here: 634 us
  waiting for transfers between devices  382 us (60%)
  starting transfers between devices  107 us (17%)
  blocking collectives  59.4 us (9%)
  other arithmetic  47.2 us (7%)
  local copies, waits for them, and re-layouts  36.9 us (6%)
    ppermute x12, waiting for transfers between devices, passed_along(): return lax.ppermute(block, axis, route)  277 us
    ppermute x9, waiting for transfers between devices, with_halo(): before = lax.ppermute(last, axis, up)  83.3 us
    ppermute x12, starting transfers between devices, passed_along(): return lax.ppermute(block, axis, route)  60.9 us
    all_gather x1, blocking collectives, local(): lax.all_gather(image_values, ('pipe', 'cross'), axis=1, tiled=True)  59.4 us
    ppermute x9, starting transfers between devices, with_halo(): before = lax.ppermute(last, axis, up)  34.2 us
    ppermute x9, waiting for transfers between devices, with_halo(): after = lax.ppermute(first, axis, down)  22.1 us
    select_n x1, other arithmetic, local(): cleared = jnp.where(cell_mask.reshape(1, -1) == 1, 0.0, flat_state)  21.1 us
    scatter x1, other arithmetic, local(): cleared.at[:, ghost_cell].set(reflection * picked)  14.8 us
  transfers between devices with their start and end apart: 30, of which 23 were waited for; matrix products, arithmetic and copies ran while one was open for 1% of the time, Pallas kernels for 0%

commit v1 on v0

v1 whole, which is shorter than its diff:
```python
import functools

import numpy as np
import jax
import jax.numpy as jnp
from jax import lax
from jax.experimental import pallas as pl
from jax.experimental.pallas import tpu as pltpu
from jax.sharding import PartitionSpec as P

LINE = 96
LANES = 128
REFLECT = (1.0, -1.0, -1.0, -1.0, 1.0)

Z_UP, Z_DOWN, ROW_FIRST, ROW_LAST, RIGHT_FIRST, RIGHT_LAST = range(6)
LINK_IN, MARGIN_FIRST, MARGIN_LAST, LINK_UP, FIRST_LO, FIRST_HI, LAST_LO, LAST_HI, FIRST_EDGE, LAST_EDGE = range(10)
COEFFICIENTS = 10
PENCIL, ROW, OWNER, IMAGE, WEIGHT_UP, WEIGHT_DOWN, WEIGHT_FIRST, WEIGHT_LAST = range(8)


def derivative_tables(slabs, rows, var_count):
    total = slabs * rows
    A = np.eye(total)
    B = np.zeros((total, total))
    for i in range(2, total - 2):
        A[i, i - 1] = A[i, i + 1] = 1.0 / 3.0
        B[i, i + 1], B[i, i - 1] = 7.0 / 9.0, -7.0 / 9.0
        B[i, i + 2], B[i, i - 2] = 1.0 / 36.0, -1.0 / 36.0
    for i in (1, total - 2):
        A[i, i - 1] = A[i, i + 1] = 0.25
        B[i, i + 1], B[i, i - 1] = 0.75, -0.75
    B[0, :3] = (-1.5, 2.0, -0.5)
    B[-1, -3:] = (0.5, -2.0, 1.5)
    inverse = np.linalg.inv(A)
    M = inverse @ B

    cells = var_count * rows
    own_at, reduce_at, adjoint_at, profile_at, weight_at = 0, cells, cells + 16, cells + 56, cells + 96
    tables = np.zeros((slabs, cells + 112, LANES))
    carry_up, carry_down = np.zeros(slabs), np.zeros(slabs)
    for p in range(slabs):
        table = tables[p]
        base = p * rows
        here = slice(base, base + rows)
        own = M[here, here]
        lo, hi, lo_edge, hi_edge = (np.zeros(rows) for _ in range(4))
        weight_up, weight_down = np.zeros(rows), np.zeros(rows)
        if p > 0:
            lo = inverse[here, base - 8] / inverse[base + 1, base - 8]
            lo_edge[0] = M[base, base - 1] - lo[0] * M[base + 1, base - 1]
            weight_down = M[base - 2, here]
        if p > 1:
            k = base - rows - 8
            carry_up[p] = inverse[base + 1, k] / inverse[base - rows + 1, k]
        if p < slabs - 1:
            k = base + rows + 8
            hi = inverse[here, k] / inverse[base + rows - 2, k]
            hi_edge[-1] = M[base + rows - 1, base + rows] - hi[-1] * M[base + rows - 2, base + rows]
            weight_up = M[base + rows + 1, here]
        if p < slabs - 2:
            k = base + 2 * rows + 8
            carry_down[p] = inverse[base + rows - 2, k] / inverse[base + 2 * rows - 2, k]
        for v in range(var_count):
            at = slice(v * rows, (v + 1) * rows)
            table[own_at + v * rows : own_at + (v + 1) * rows, at] = own
            table[reduce_at + v, at] = weight_up
            table[reduce_at + var_count + v, at] = weight_down
        table[adjoint_at : adjoint_at + rows, :rows] = own.T
        table[adjoint_at + rows : adjoint_at + 2 * rows, rows : 2 * rows] = own.T
        more = adjoint_at + 2 * rows
        table[more, :rows] = lo
        table[more + 1, :rows] = hi
        table[more + 2, rows : 2 * rows] = lo
        table[more + 3, rows : 2 * rows] = hi
        table[more + 4, 0] = lo_edge[0]
        table[more + 5, 2 * rows - 1] = hi_edge[-1]
        table[profile_at : profile_at + rows] = lo[:, None]
        table[profile_at + rows : profile_at + 2 * rows] = hi[:, None]
        table[profile_at + 2 * rows] = lo_edge[0]
        table[profile_at + 2 * rows + 1] = hi_edge[-1]
        table[weight_at, :rows] = weight_up
        table[weight_at + 1, :rows] = weight_down
    at = (own_at, reduce_at, adjoint_at, profile_at, weight_at)
    return tables.astype(np.float32), at, carry_up, carry_down


def split(x, parts):
    pieces = []
    for _ in range(parts):
        piece = x.astype(jnp.bfloat16)
        pieces.append(piece)
        x = x - piece.astype(jnp.float32)
    return pieces


def exact_dot(x, one_hot, contract):
    found = lax.dot_general(
        jnp.concatenate(split(x, 3), axis=0),
        one_hot,
        (contract, ((), ())),
        preferred_element_type=jnp.float32,
    )
    size = x.shape[0]
    return found[:size] + (found[size : 2 * size] + found[2 * size :])


def full_dot(a, b):
    return jnp.dot(a, b, precision=lax.Precision.HIGHEST, preferred_element_type=jnp.float32)


def marks(shape, axis, values):
    return jnp.where(lax.broadcasted_iota(jnp.int32, shape, axis) == values, 1.0, 0.0).astype(
        jnp.bfloat16
    )


def place_of(cell, rows, pencils):
    row = jnp.zeros_like(cell)
    for k in range(1, rows):
        row += (cell >= k * pencils).astype(jnp.int32)
    return row, cell - row * pencils


def tile(t):
    return slice(t * LANES, (t + 1) * LANES)


def turn(ref, x):
    height, pencils = x.shape
    for t in range(pencils // LANES):
        ref[t * height : (t + 1) * height, :] = x[:, tile(t)]


def slab_at(ref, row, height, count):
    return ref[pl.ds(row, count, stride=height), :]


def put_slab(ref, row, height, count, value):
    ref[pl.ds(row, count, stride=height), :] = value


def kept_at(which, i, rows, count):
    return (which * rows + i) * (-(-count // 8) * 8)


def fetch(sources, targets, sems):
    copies = [
        pltpu.make_async_copy(source, target, sems.at[k])
        for k, (source, target) in enumerate(zip(sources, targets))
    ]
    for copy in copies:
        copy.start()
    return copies


class Slices:
    def __init__(self, slabs, count, var_count):
        rest = count % slabs
        self.slabs, self.count, self.var_count = slabs, count, var_count
        shared = rest > 0 and slabs % rest == 0 and LANES % (slabs // rest) == 0
        self.full = count // slabs if shared else -(-count // slabs)
        self.rest = rest if shared else 0
        self.per = slabs // rest if shared else 1
        self.width = LANES // self.per
        self.chunk = self.full + (1 if shared else 0)
        self.lines, self.back_lines = 6 * var_count + COEFFICIENTS, 4 * var_count
        self.groups, self.back_groups = (self.group_count(n) for n in (self.lines, self.back_lines))
        self.meta_at = self.lines * self.full
        self.packed_at = self.meta_at + 8
        self.height = -(-(self.packed_at + self.groups) // 8) * 8
        self.back_packed_at = self.back_lines * self.full
        self.back_height = -(-(self.back_packed_at + self.back_groups) // 8) * 8

    def group_count(self, lines):
        return -(-lines // self.per) if self.rest else 0

    def tiles_at(self, t):
        return t * self.slabs, min(self.count, (t + 1) * self.slabs)


def lane_block(rows, width):
    return lax.broadcasted_iota(jnp.int32, (rows, LANES), 1) // width


def moved_lanes(x, by):
    by %= LANES
    return x if by == 0 else pltpu.roll(x, by, 1)


def image_kernel(state_hbm, base_hbm, weight_hbm, out_ref, state_ref, base_ref, weight_ref, sems):
    var_count, rows, pencils = state_ref.shape
    images = base_ref.shape[0]
    copies = fetch(
        (state_hbm, base_hbm, weight_hbm), (state_ref, base_ref, weight_ref), sems
    )
    for copy in copies[1:]:
        copy.wait()
    row, pencil = place_of(base_ref[...].reshape(1, images), rows, pencils)
    pick = marks((pencils, images), 0, pencil)
    row_at = lax.broadcasted_iota(jnp.int32, (rows, images), 0)
    lower, upper = row_at == row, row_at == row + 1
    total = [jnp.zeros((rows, images), jnp.float32) for _ in range(var_count)]
    copies[0].wait()
    x = state_ref[...].reshape(var_count * rows, pencils)
    for corner, shift in enumerate((0, 1, LINE, LINE + 1)):
        moved = x if shift == 0 else pltpu.roll(x, pencils - shift, 1)
        pieces = jnp.concatenate(split(moved, 2), axis=0)
        found = jnp.dot(pieces, pick, preferred_element_type=jnp.float32)
        found = found[: var_count * rows] + found[var_count * rows :]
        weight = jnp.where(lower, weight_ref[corner : corner + 1], 0.0) + jnp.where(
            upper, weight_ref[corner + 4 : corner + 5], 0.0
        )
        for v in range(var_count):
            total[v] += found[v * rows : (v + 1) * rows] * weight
    lines = []
    for v in range(var_count):
        value = jnp.sum(total[v], axis=0, keepdims=True)
        lines += [value[:, tile(t)] for t in range(images // LANES)]
    lines = jnp.concatenate(lines, axis=0)
    for k in range(out_ref.shape[0]):
        out_ref[k] = lines


def ghost_values(blocks, owner, image):
    cross = len(blocks)
    slabs, lines, _ = blocks[0].shape
    per = lines // len(REFLECT)
    ghosts = owner.shape[1]
    me = lax.axis_index("cross")
    values = [
        jnp.concatenate(
            [
                jnp.concatenate([block[:, v * per + t, :] for t in range(per)], axis=1)
                for block in blocks
            ],
            axis=0,
        )
        for v in range(len(REFLECT))
    ]
    pick = marks((per * LANES, ghosts), 0, image)
    found = exact_dot(jnp.concatenate(values, axis=0), pick, ((1,), (0,)))
    devices = slabs * cross
    at = lax.broadcasted_iota(jnp.int32, (devices, ghosts), 0)
    mine = (at % slabs) * cross + (me + cross - at // slabs) % cross == owner
    return [
        reflect
        * jnp.sum(
            jnp.where(mine, found[v * devices : (v + 1) * devices], 0.0), axis=0, keepdims=True
        )
        for v, reflect in enumerate(REFLECT)
    ]


def prepare_kernel(
    slices,
    at,
    face_hbm,
    courant_hbm,
    tables_hbm,
    cell_hbm,
    owner_hbm,
    image_hbm,
    mask_hbm,
    state_hbm,
    message_ref,
    kept_ref,
    face_ref,
    courant_ref,
    table_ref,
    cell_ref,
    owner_ref,
    image_ref,
    mask_ref,
    state_ref,
    turned_ref,
    pair_ref,
    matrix_ref,
    adjoint_ref,
    weight_ref,
    cleared_ref,
    rest_ref,
    sems,
):
    var_count, rows, pencils = state_ref.shape
    cells = var_count * rows
    count = pencils // LANES
    ghosts = cell_ref.shape[0]
    padded = -(-count // 8) * 8
    p = lax.axis_index("pipe")
    slabs, height = slices.slabs, slices.height
    lines = slices.groups * slices.per
    _, reduce_at, adjoint_at, profile_at, weight_at = at
    copies = fetch(
        (face_hbm, courant_hbm, tables_hbm.at[p], cell_hbm, owner_hbm, image_hbm, mask_hbm, state_hbm),
        (face_ref, courant_ref, table_ref, cell_ref, owner_ref, image_ref, mask_ref, state_ref),
        sems,
    )

    def send(line, slab):
        for t in range(slices.full):
            start, end = slices.tiles_at(t)
            message_ref[pl.ds(line * slices.full + t, end - start, stride=height), :] = slab[start:end]
        for m in range(slices.rest):
            tail = slices.full * slabs + m
            rest_ref[m * lines + line : m * lines + line + 1, :] = slab[tail : tail + 1]

    def send_value(functional, v, slab):
        send(functional * var_count + v, slab)

    def send_coefficient(which, slab):
        send(6 * var_count + which, slab)

    copies[0].wait()
    turn(turned_ref, face_ref[...])

    def face(i):
        return slab_at(turned_ref, i, rows, count)

    link = face(0)
    margin = jnp.ones_like(link)
    first_margin = margin
    to_up, to_first = [None] * rows, [None] * rows
    for i in range(1, rows - 1):
        above = face(i)
        inverse = 1.0 / (link + margin + above)
        low, up = link * inverse, above * inverse
        to_up[i], to_first[i] = up, low
        for k, part in enumerate((up, low, inverse)):
            start = kept_at(k, i, rows, count)
            kept_ref[start : start + count, :] = part
        first_margin += low * margin
        link = link * up
        margin = 1.0 + margin * up
    send_coefficient(LINK_IN, link)
    send_coefficient(MARGIN_FIRST, first_margin)
    send_coefficient(MARGIN_LAST, margin)
    send_coefficient(LINK_UP, jnp.where(p == slabs - 1, 0.0, face(rows - 1)))

    zero, one = jnp.zeros_like(margin), jnp.ones_like(margin)
    first, last = [None] * rows, [None] * rows
    first[0], first[rows - 1], last[0], last[rows - 1] = one, zero, zero, one
    for i in range(rows - 2, 0, -1):
        first[i] = to_first[i] + to_up[i] * first[i + 1]
        last[i] = to_up[i] * last[i + 1]
    copies[1].wait()
    turn(turned_ref, courant_ref[...])
    for i in range(rows):
        speed = slab_at(turned_ref, i, rows, count)
        start = kept_at(3, i, rows, count)
        kept_ref[start : start + count, :] = speed
        put_slab(pair_ref, i, 2 * rows, count, first[i] * speed)
        put_slab(pair_ref, rows + i, 2 * rows, count, last[i] * speed)
    for t in range(count):
        matrix_ref[:, tile(t)] = pair_ref[t * 2 * rows : (t + 1) * 2 * rows, :]
    copies[2].wait()
    kept_ref[kept_ref.shape[0] - 40 :, :] = table_ref[profile_at : profile_at + 40, :]
    turn(
        adjoint_ref, full_dot(table_ref[adjoint_at : adjoint_at + 40, : 2 * rows], matrix_ref[...])
    )
    for k in range(6):
        send_coefficient(FIRST_LO + k, slab_at(adjoint_ref, 2 * rows + k, 40, count))
    weight_ref[:, padded - 8 :, :] = jnp.zeros((2 * rows, 8, LANES), jnp.float32)
    for i, share in enumerate(first + last):
        weight_ref[i, :count, :] = share - slab_at(adjoint_ref, i, 40, count)

    for copy in copies[3:6]:
        copy.wait()
    row, pencil = place_of(cell_ref[...].reshape(1, ghosts), rows, pencils)
    lane_tile = jnp.right_shift(pencil, 7)
    lane_marks = marks((LANES, ghosts), 0, pencil - lane_tile * LANES)
    picked = exact_dot(
        weight_ref[...].reshape(2 * rows * padded, LANES), lane_marks, ((1,), (0,))
    ).reshape(2, rows, padded, ghosts)
    at_cell = (lax.broadcasted_iota(jnp.int32, (rows, padded, ghosts), 0) == row[None]) & (
        lax.broadcasted_iota(jnp.int32, (rows, padded, ghosts), 1) == lane_tile[None]
    )
    row_marks = jnp.where(lax.broadcasted_iota(jnp.int32, (rows, ghosts), 0) == row, 1.0, 0.0)
    up_down = full_dot(table_ref[weight_at : weight_at + 8, :rows], row_marks)

    def at_ghosts(values):
        return jnp.sum(jnp.sum(jnp.where(at_cell, values, 0.0), axis=0), axis=0, keepdims=True)

    about = jnp.concatenate(
        [
            pencil.astype(jnp.float32),
            row.astype(jnp.float32),
            owner_ref[...].reshape(1, ghosts).astype(jnp.float32),
            image_ref[...].reshape(1, ghosts).astype(jnp.float32),
            up_down[0:2],
            at_ghosts(picked[0]),
            at_ghosts(picked[1]),
        ],
        axis=0,
    )
    for j in range(slabs):
        start = j * height + slices.meta_at
        message_ref[start : start + 8, :] = about

    copies[6].wait()
    copies[7].wait()
    solid = mask_ref[...] == 1
    for v in range(var_count):
        here = slice(v * rows, (v + 1) * rows)
        cleared_ref[here, :] = jnp.where(solid, 0.0, state_ref[v])
    turn(turned_ref, cleared_ref[...])
    turn(pair_ref, full_dot(table_ref[reduce_at : reduce_at + 16, :cells], cleared_ref[...]))
    for k in range(2 * var_count):
        send(k, slab_at(pair_ref, k, 16, count))
    for v in range(var_count):
        low = high = zero
        for i in range(rows):
            cell = slab_at(turned_ref, v * rows + i, cells, count)
            if i == 0:
                send_value(ROW_FIRST, v, cell)
            if i == rows - 1:
                send_value(ROW_LAST, v, cell)
            low += weight_ref[i, :count, :] * cell
            high += weight_ref[rows + i, :count, :] * cell
        send_value(RIGHT_FIRST, v, low)
        send_value(RIGHT_LAST, v, high)

    block = lane_block(max(slices.groups, 1), slices.width)
    for m in range(slices.rest):
        lined = [
            rest_ref[pl.ds(m * lines + k, slices.groups, stride=slices.per), :]
            for k in range(slices.per)
        ]
        for i in range(slices.per):
            packed = lined[0]
            for k in range(slices.per):
                moved = moved_lanes(lined[k], (k - i) * slices.width)
                packed = moved if k == 0 else jnp.where(block == k, moved, packed)
            start = (m * slices.per + i) * height + slices.packed_at
            message_ref[start : start + slices.groups, :] = packed


def solve_kernel(slices, carry_up, carry_down, message_ref, *refs):
    *blocks, back_ref, ghost_ref, rest_ref, back_rest_ref = refs
    slabs, var_count, chunk, full = slices.slabs, slices.var_count, slices.chunk, slices.full
    height, per, width = slices.height, slices.per, slices.width
    me = lax.axis_index("pipe")

    def meta(p, k):
        start = p * height + slices.meta_at + k
        return message_ref[start : start + 1, :]

    def meta_all(k):
        return jnp.concatenate([meta(p, k) for p in range(slabs)], axis=1).astype(jnp.int32)

    values = ghost_values(blocks, meta_all(OWNER), meta_all(IMAGE))
    ghost_lines = 6 * var_count + 2
    ghosts = LANES
    place = lax.broadcasted_iota(jnp.int32, (chunk * LANES, ghosts), 0)
    slot, lane = place // LANES, place % LANES
    pencil_at = jnp.where(
        slot < full,
        (me + slot * slabs) * LANES + lane,
        (full * slabs + me // per) * LANES + (me % per) * width + lane,
    )
    for p in range(slabs):
        row = meta(p, ROW)
        weights = (
            meta(p, WEIGHT_UP),
            meta(p, WEIGHT_DOWN),
            jnp.where(row == 0.0, 1.0, 0.0),
            jnp.where(row == 15.0, 1.0, 0.0),
            meta(p, WEIGHT_FIRST),
            meta(p, WEIGHT_LAST),
        )
        here = jnp.concatenate([value[:, tile(p)] for value in values], axis=0)
        shares = jnp.concatenate(
            [here * weight for weight in weights] + [jnp.zeros((2, ghosts), jnp.float32)], axis=0
        )
        spots = jnp.where(pencil_at == meta(p, PENCIL).astype(jnp.int32), 1.0, 0.0)
        share = exact_dot(shares, spots.astype(jnp.bfloat16), ((1,), (1,)))
        for t in range(chunk):
            start = (p * chunk + t) * ghost_lines
            ghost_ref[start : start + ghost_lines, :] = share[:, tile(t)]
        if slices.rest:
            start = p * height + slices.packed_at
            packed = message_ref[start : start + slices.groups, :]
            for k in range(per):
                rest_ref[pl.ds(p * slices.groups * per + k, slices.groups, stride=per), :] = (
                    moved_lanes(packed, -k * width)
                )

    def sent(p, line):
        start = p * height + line * full
        slab = message_ref[start : start + full, :]
        if slices.rest:
            start = p * slices.groups * per + line
            slab = jnp.concatenate([slab, rest_ref[start : start + 1, :]], axis=0)
        return slab

    def value(p, functional, v):
        line = functional * var_count + v
        start = p * chunk * ghost_lines + line
        return sent(p, line) + ghost_ref[pl.ds(start, chunk, stride=ghost_lines), :]

    def give(p, functional, v, slab):
        line = functional * var_count + v
        start = p * slices.back_height + line * full
        back_ref[start : start + full, :] = slab[:full]
        if slices.rest:
            start = p * slices.back_groups * per + line
            back_rest_ref[start : start + 1, :] = slab[full:]

    coefficients = [
        [sent(p, 6 * var_count + k) for k in range(COEFFICIENTS)] for p in range(slabs)
    ]
    nodes = 2 * slabs
    ratio, scale = [], []
    margin = coefficients[0][MARGIN_FIRST]
    for k in range(nodes):
        link = coefficients[k // 2][LINK_UP if k % 2 else LINK_IN]
        inverse = 1.0 / (margin + link)
        ratio.append(link * inverse)
        scale.append(inverse)
        if k < nodes - 1:
            following = coefficients[(k + 1) // 2][MARGIN_FIRST if k % 2 else MARGIN_LAST]
            margin = following + margin * ratio[k]

    zero = jnp.zeros((chunk, LANES), jnp.float32)
    for v in range(var_count):
        lo, hi = [zero] * slabs, [zero] * slabs
        below, above = [zero] * slabs, [zero] * slabs
        for p in range(1, slabs):
            lo[p] = value(p - 1, Z_UP, v) + float(carry_up[p]) * lo[p - 1]
            below[p] = value(p - 1, ROW_LAST, v)
        for p in range(slabs - 2, -1, -1):
            hi[p] = value(p + 1, Z_DOWN, v) + float(carry_down[p]) * hi[p + 1]
            above[p] = value(p + 1, ROW_FIRST, v)
        right = []
        for p in range(slabs):
            coefficient = coefficients[p]
            right.append(
                value(p, RIGHT_FIRST, v)
                - coefficient[FIRST_LO] * lo[p]
                - coefficient[FIRST_HI] * hi[p]
                - coefficient[FIRST_EDGE] * below[p]
            )
            right.append(
                value(p, RIGHT_LAST, v)
                - coefficient[LAST_LO] * lo[p]
                - coefficient[LAST_HI] * hi[p]
                - coefficient[LAST_EDGE] * above[p]
            )
            give(p, 2, v, lo[p])
            give(p, 3, v, hi[p])
        for k in range(1, nodes):
            right[k] = right[k] + ratio[k - 1] * right[k - 1]
        x = right[nodes - 1] * scale[nodes - 1]
        give(slabs - 1, 1, v, x)
        for k in range(nodes - 2, -1, -1):
            x = right[k] * scale[k] + ratio[k] * x
            give(k // 2, k % 2, v, x)
    if slices.rest:
        groups = slices.back_groups
        block = lane_block(groups, width)
        for p in range(slabs):
            for k in range(per):
                lined = back_rest_ref[pl.ds(p * groups * per + k, groups, stride=per), :]
                moved = moved_lanes(lined, k * width)
                packed = moved if k == 0 else jnp.where(block == k, moved, packed)
            start = p * slices.back_height + slices.back_packed_at
            back_ref[start : start + groups, :] = packed


def fill_kernel(at, owner_hbm, image_hbm, cell_hbm, courant_hbm, tables_hbm, mask_hbm, state_hbm, *refs):
    *blocks, turned_ref, up_ref, down_ref = refs[:-9]
    owner_ref, image_ref, cell_ref, courant_ref, table_ref, mask_ref, state_ref = refs[-9:-2]
    filled_ref, sems = refs[-2:]
    var_count, rows, pencils = state_ref.shape
    cells = var_count * rows
    count = pencils // LANES
    ghosts = cell_ref.shape[0]
    copies = fetch(
        (
            owner_hbm,
            image_hbm,
            cell_hbm,
            courant_hbm,
            tables_hbm.at[lax.axis_index("pipe")],
            mask_hbm,
            state_hbm,
        ),
        (owner_ref, image_ref, cell_ref, courant_ref, table_ref, mask_ref, state_ref),
        sems,
    )
    for copy in copies[:3]:
        copy.wait()
    owner, image = (ref[...].reshape(1, ghosts) for ref in (owner_ref, image_ref))
    values = ghost_values(blocks, owner, image)
    row, pencil = place_of(cell_ref[...].reshape(1, ghosts), rows, pencils)
    spots = marks((pencils, ghosts), 0, pencil)
    at_row = lax.broadcasted_iota(jnp.int32, (rows, ghosts), 0) == row
    spread = jnp.concatenate([jnp.where(at_row, value, 0.0) for value in values], axis=0)
    placed = exact_dot(spread, spots, ((1,), (1,)))
    for copy in copies[3:]:
        copy.wait()
    solid = mask_ref[...] == 1
    for v in range(var_count):
        here = slice(v * rows, (v + 1) * rows)
        filled_ref[here, :] = jnp.where(solid, 0.0, state_ref[v]) + placed[here]
    for v in range(var_count):
        for t in range(count):
            line = slice(v * count + t, v * count + t + 1)
            down_ref[line, :] = filled_ref[v * rows : v * rows + 1, tile(t)]
            up_ref[line, :] = filled_ref[(v + 1) * rows - 1 : (v + 1) * rows, tile(t)]
    own = full_dot(table_ref[at[0] : at[0] + cells, :cells], filled_ref[...])
    turn(turned_ref.at[: cells * count, :], own)
    courant = courant_ref[...]
    for v in range(var_count):
        here = slice(v * rows, (v + 1) * rows)
        right = filled_ref[here, :] - courant * own[here]
        for t in range(count):
            start = (count + t) * cells + v * rows
            turned_ref[start : start + rows, :] = right[:, tile(t)]


def finish_kernel(
    slices,
    back_ref,
    turned_ref,
    kept_ref,
    below_ref,
    above_ref,
    derivative_hbm,
    segment_hbm,
    derivative_ref,
    segment_ref,
    derivative_turned_ref,
    segment_turned_ref,
    tail_ref,
    sems,
):
    var_count, rows, pencils = segment_ref.shape
    count = pencils // LANES
    cells = var_count * rows
    variables = range(var_count)
    profile_at = kept_ref.shape[0] - 40
    back_height, groups, per = slices.back_height, slices.back_groups, slices.per
    block = lane_block(max(groups, 1), slices.width)
    for m in range(slices.rest):
        packed = []
        for i in range(per):
            start = (m * per + i) * back_height + slices.back_packed_at
            packed.append(back_ref[start : start + groups, :])
        for k in range(per):
            for i in range(per):
                moved = moved_lanes(packed[i], (i - k) * slices.width)
                joined = moved if i == 0 else jnp.where(block == i, moved, joined)
            tail_ref[pl.ds(m * groups * per + k, groups, stride=per), :] = joined

    def got(functional, v):
        line = functional * var_count + v
        parts = []
        for t in range(slices.full):
            start, end = slices.tiles_at(t)
            parts.append(
                back_ref[pl.ds(line * slices.full + t, end - start, stride=back_height), :]
            )
        for m in range(slices.rest):
            start = m * groups * per + line
            parts.append(tail_ref[start : start + 1, :])
        return jnp.concatenate(parts, axis=0)

    def profile(k):
        return kept_ref[profile_at + k : profile_at + k + 1, :]

    def kept(which, i):
        start = kept_at(which, i, rows, count)
        return kept_ref[start : start + count, :]

    def give(turned, straight, hbm, which):
        copies = []
        for v in variables:
            for t in range(count):
                start = t * cells + v * rows
                straight[v, :, tile(t)] = turned[start : start + rows, :]
            copies.append(
                pltpu.make_async_copy(straight.at[v], hbm.at[v], sems.at[which * var_count + v])
            )
            copies[-1].start()
        return copies

    lo, hi = [got(2, v) for v in variables], [got(3, v) for v in variables]
    swept = [[None] * rows for _ in variables]
    for i in range(rows):
        for v in variables:
            row = v * rows + i
            edge = slice(v * count, (v + 1) * count)
            far = profile(i) * lo[v] + profile(rows + i) * hi[v]
            if i == 0:
                far += profile(2 * rows) * below_ref[edge, :]
            if i == rows - 1:
                far += profile(2 * rows + 1) * above_ref[edge, :]
            value = slab_at(turned_ref, row, cells, count) + far
            put_slab(derivative_turned_ref, row, cells, count, value)
            if 0 < i < rows - 1:
                right = slab_at(turned_ref, cells * count + row, cells, count)
                right -= kept(3, i) * far
                if i > 1:
                    right += kept(0, i - 1) * swept[v][i - 1]
                swept[v][i] = right
    copies = give(derivative_turned_ref, derivative_ref, derivative_hbm, 0)
    first, last = [got(0, v) for v in variables], [got(1, v) for v in variables]
    x = list(last)
    for v in variables:
        put_slab(segment_turned_ref, v * rows, cells, count, first[v])
        put_slab(segment_turned_ref, (v + 1) * rows - 1, cells, count, last[v])
    for i in range(rows - 2, 0, -1):
        for v in variables:
            x[v] = kept(2, i) * swept[v][i] + kept(1, i) * first[v] + kept(0, i) * x[v]
            put_slab(segment_turned_ref, v * rows + i, cells, count, x[v])
    copies += give(segment_turned_ref, segment_ref, segment_hbm, 1)
    for copy in copies:
        copy.wait()


def call(kernel, outs, scratch, sems, args, near=(), far_out=False, limit=62):
    whole = pl.BlockSpec(memory_space=pltpu.VMEM)
    far = pl.BlockSpec(memory_space=pltpu.HBM)
    buffers = [
        pltpu.VMEM(s.shape, s.dtype) if hasattr(s, "dtype") else pltpu.VMEM(s, jnp.float32)
        for s in scratch
    ]
    buffers += [pltpu.SemaphoreType.DMA((size,)) for size in sems]
    return pl.pallas_call(
        kernel,
        out_shape=[jax.ShapeDtypeStruct(shape, jnp.float32) for shape in outs],
        in_specs=[whole if k in near else far for k in range(len(args))],
        out_specs=[far if far_out else whole] * len(outs),
        scratch_shapes=buffers,
        compiler_params=pltpu.CompilerParams(vmem_limit_bytes=limit * 2**20),
    )(*args)


def exchange(message, axes):
    return lax.all_to_all(message, axes, 0, 0, tiled=True)


def local(
    state,
    face_diffusion,
    courant,
    cell_mask,
    ghost_cell,
    ghost_owner,
    ghost_image,
    image_base,
    image_weight,
):
    var_count, rows, pencils = state.shape
    slabs, cross = lax.axis_size("pipe"), lax.axis_size("cross")
    count = pencils // LANES
    cells = var_count * rows
    images = image_base.shape[0]
    tables, at, carry_up, carry_down = derivative_tables(slabs, rows, var_count)
    slices = Slices(slabs, count, var_count)
    tables = jnp.asarray(tables)
    table = jax.ShapeDtypeStruct(tables.shape[1:], jnp.float32)
    turned = (cells * count, LANES)
    edge = (var_count * count, LANES)
    kept = (kept_at(4, 0, rows, count) + 40, LANES)

    (image_values,) = call(
        image_kernel,
        [(slabs, var_count * images // LANES, LANES)],
        [state, image_base, image_weight],
        [3],
        (state, image_base, image_weight),
    )
    image_values = exchange(image_values, "pipe")

    arguments = (
        face_diffusion,
        courant,
        tables,
        ghost_cell,
        ghost_owner,
        ghost_image,
        cell_mask,
        state,
    )
    message, kept_here = call(
        functools.partial(prepare_kernel, slices, at),
        [(slabs * slices.height, LANES), kept],
        [face_diffusion, courant, table, ghost_cell, ghost_owner, ghost_image, cell_mask, state]
        + [
            turned,
            (2 * rows * count, LANES),
            (2 * rows, pencils),
            (40 * count, LANES),
            (2 * rows, -(-count // 8) * 8, LANES),
            (cells, pencils),
            (max(slices.rest, 1) * max(slices.groups, 1) * slices.per, LANES),
        ],
        [len(arguments)],
        arguments,
    )
    image_values, message = lax.optimization_barrier((image_values, message))
    message = exchange(message, "pipe")
    blocks = [image_values] + [
        lax.ppermute(image_values, "cross", [(i, (i + s) % cross) for i in range(cross)])
        for s in range(1, cross)
    ]
    arguments = (ghost_owner, ghost_image, ghost_cell, courant, tables, cell_mask, state, *blocks)
    turned_here, up, down = call(
        functools.partial(fill_kernel, at),
        [(2 * cells * count, LANES), edge, edge],
        [ghost_owner, ghost_image, ghost_cell, courant, table, cell_mask, state, (cells, pencils)],
        [7],
        arguments,
        near=range(7, 7 + cross),
        limit=48,
    )
    forward = [(i, i + 1) for i in range(slabs - 1)]
    below = lax.ppermute(up, "pipe", forward)
    above = lax.ppermute(down, "pipe", [(j, i) for i, j in forward])

    spare = slabs * slices.per
    (back,) = call(
        functools.partial(solve_kernel, slices, carry_up, carry_down),
        [(slabs * slices.back_height, LANES)],
        [
            (slabs * slices.chunk * (6 * var_count + 2), LANES),
            (max(slices.groups, 1) * spare, LANES),
            (max(slices.back_groups, 1) * spare, LANES),
        ],
        [],
        (message, *blocks),
        near=range(1 + cross),
        limit=24,
    )
    back = exchange(back, "pipe")
    arguments = (back, turned_here, kept_here, below, above)
    return tuple(
        call(
            functools.partial(finish_kernel, slices),
            [state.shape, state.shape],
            [
                state.shape,
                state.shape,
                turned,
                turned,
                (max(slices.rest, 1) * max(slices.back_groups, 1) * slices.per, LANES),
            ],
            [2 * var_count],
            arguments,
            near=range(len(arguments)),
            far_out=True,
            limit=48,
        )
    )


def solution(mesh):
    in_specs = (
        P(None, "pipe", "cross"),
        P("pipe", "cross"),
        P("pipe", "cross"),
        P("pipe", "cross"),
        P(("pipe", "cross")),
        P(("pipe", "cross")),
        P(("pipe", "cross")),
        P(("pipe", "cross")),
        P(None, ("pipe", "cross")),
    )
    out_specs = (P(None, "pipe", "cross"), P(None, "pipe", "cross"))
    return jax.shard_map(local, mesh=mesh, in_specs=in_specs, out_specs=out_specs, check_vma=False)
```

time: 636 us -> 59.5 us (0.09)
  waiting for transfers between devices: 382 us -> 17.4 us
  starting transfers between devices: 107 us -> 21.4 us
  blocking collectives: 59.4 us -> 0 us
  other arithmetic: 47.2 us -> 0 us
  local copies, waits for them, and re-layouts: 36.9 us -> 5.65 us
  Pallas kernels: 0 us -> 13.6 us
    ppermute x30 -> x5, waiting for transfers between devices: 382 us -> 8.78 us  [the longest x1 4.25 us: local(): above = lax.ppermute(down, 'pipe', [(j, i) for i, j in forward])]
    ppermute x30 -> x5, starting transfers between devices: 107 us -> 6.99 us  [the longest x1 3.92 us: local(): below = lax.ppermute(up, 'pipe', forward)]
    all_gather x1 -> x0, blocking collectives: 59.4 us -> none  [local(): lax.all_gather(image_values, ('pipe', 'cross'), axis=1, tiled=True)]
    select_n x4 -> x0, other arithmetic: 21.1 us -> none  [the longest x1 21.1 us: local(): cleared = jnp.where(cell_mask.reshape(1, -1) == 1, 0.0, flat_state)]
    scatter x1 -> x0, other arithmetic: 14.8 us -> none  [local(): cleared.at[:, ghost_cell].set(reflection * picked)]
    all_to_all x0 -> x3, starting transfers between devices: none -> 14.4 us  [exchange(): return lax.all_to_all(message, axes, 0, 0, tiled=True)]
    pallas_call x0 -> x5, Pallas kernels: none -> 13.6 us  [call(): pl.pallas_call(kernel, out_shape=[jax.ShapeDtypeStruct(shape, jnp.float32...]
    gather x1 -> x0, local copies, waits for them, and re-layouts: 11.8 us -> none  [local(): image_values = jnp.sum(flat_state[:, corners] * image_weight[None], axis=1)]
  transfers between devices with their start and end apart: 30 -> 8, of which waited for: 23 -> 7; matrix products, arithmetic and copies ran while one was open for 1% -> 0% of each run, Pallas kernels for 0% -> 11%
where the time goes in v1:
time: 59.5 us; the launch traced here: 58.9 us
  starting transfers between devices  21.4 us (36%)
  waiting for transfers between devices  17.4 us (29%)
  Pallas kernels  13.6 us (23%)
  local copies, waits for them, and re-layouts  5.65 us (9%)
  between operations  0.77 us (1%)
    all_to_all x3, starting transfers between devices, exchange(): return lax.all_to_all(message, axes, 0, 0, tiled=True)  14.4 us
    pallas_call x5, Pallas kernels, call(): pl.pallas_call(kernel, out_shape=[jax.ShapeDtypeStruct(shape, jnp.float32...  13.6 us
    all_to_all x3, waiting for transfers between devices, exchange(): return lax.all_to_all(message, axes, 0, 0, tiled=True)  8.65 us
    unnamed x28, local copies, waits for them, and re-layouts  5.65 us
    ppermute x1, waiting for transfers between devices, local(): above = lax.ppermute(down, 'pipe', [(j, i) for i, j in forward])  4.25 us
    ppermute x3, waiting for transfers between devices, local(): lax.ppermute(image_values, 'cross', [(i, (i + s) % cross) for i in range(...  4.1 us
    ppermute x1, starting transfers between devices, local(): below = lax.ppermute(up, 'pipe', forward)  3.92 us
    ppermute x3, starting transfers between devices, local(): lax.ppermute(image_values, 'cross', [(i, (i + s) % cross) for i in range(...  1.78 us
  transfers between devices with their start and end apart: 8, of which 7 were waited for; matrix products, arithmetic and copies ran while one was open for 0% of the time, Pallas kernels for 11%

profile of v1, /device:TPU:0, one launch (start us, length us, event | category | flops | bytes accessed | tf_op | source)
XLA Modules:
  0.0 58.9 jit_solution(17388630715588490093)
XLA Ops:
  0.6 2.9 %shard_map.113 = f32[8,10,128]{2,1,0:T(8,128)} custom-call(f32[5,16,2304]{2,1,0:T(8,128)} %state_hbm.5, s32[256]{0:T(256)} %base_hbm.1, f32[8,256]{1,0:T(8,128)} %weight_hbm.1), custom_call_target="tpu_custom_call" | custom-call | tf_op jit(solution)/shard_map/pallas_call | solution.py:729
  3.6 7.3 %all-to-all-start = ((f32[8,10,128]{2,1,0:T(8,128)}), f32[8,10,128]{2,1,0:T(8,128)S(1)}, u32[]{:S(2)}, u32[]{:S(2)}) async-start(f32[8,10,128]{2,1,0:T(8,128)} %shard_map.113), calls=%async_computation | async-start | bytes 131072 | tf_op jit(solution)/shard_map/all_to_all | solution.py:740
  10.9 4.0 %shard_map.114 = (f32[832,128]{1,0:T(8,128)}, f32[1576,128]{1,0:T(8,128)}) custom-call(f32[16,2304]{1,0:T(8,128)} %face_hbm.1, f32[16,2304]{1,0:T(8,128)} %courant_hbm.3, f32[8,192,128]{2,1,0:T(8,128)} %constant.2.clone.tables_hbm, s32[128]{0:T(128)} %cell_hbm.3, s32[128]{0:T(128)} %owner_hbm.3, s32[128]{0:T(128)} %image_hbm.3, s32[16,2304]{1,0:T(8,128)} %mask_hbm.3, ...), custom_call_target="tpu_custom_call" | custom-call | tf_op jit(solution)/shard_map/pallas_call | solution.py:729
  14.9 0.0 copy-start
  14.9 0.0 copy-start.1
  14.9 0.0 copy-start.3
  15.0 0.0 copy-start.4
  15.0 2.8 %all-to-all-done.refs_0_ = f32[8,10,128]{2,1,0:T(8,128)S(1)} async-done(((f32[8,10,128]{2,1,0:T(8,128)}), f32[8,10,128]{2,1,0:T(8,128)S(1)}, u32[]{:S(2)}, u32[]{:S(2)}) %all-to-all-start) | async-done | bytes 40992 | tf_op jit(solution)/shard_map/all_to_all | solution.py:740
  17.8 3.5 %all-to-all-start.1 = ((f32[8,104,128]{2,1,0:T(8,128)}), f32[8,104,128]{2,1,0:T(8,128)S(1)}, u32[]{:S(2)}, u32[]{:S(2)}) async-start(f32[8,104,128]{2,1,0:T(8,128)} %bitcast.6), calls=%async_computation.1 | async-start | bytes 851968 | tf_op jit(solution)/shard_map/all_to_all | solution.py:740
  21.2 0.1 collective-permute-start.2
  21.3 1.6 %collective-permute-start.1 = (f32[8,10,128]{2,1,0:T(8,128)S(1)}, f32[8,10,128]{2,1,0:T(8,128)S(1)}, u32[]{:S(2)}, u32[]{:S(2)}) collective-permute-start(f32[8,10,128]{2,1,0:T(8,128)S(1)} %all-to-all-done.refs_0_), channel_id=1, source_target_pairs={{0,2},{1,3},{2,0},{3,1},{4,6},{5,7},{6,4},{7,5},{8,10},{9,11},{10,... | collective-permute-start | bytes 122888 | tf_op jit(solution)/shard_map/ppermute | solution.py:805
  22.9 0.2 collective-permute-start
  23.0 0.2 collective-permute-done.2.refs_3_
  23.2 3.7 %collective-permute-done.1.refs_2_ = f32[8,10,128]{2,1,0:T(8,128)S(1)} collective-permute-done((f32[8,10,128]{2,1,0:T(8,128)S(1)}, f32[8,10,128]{2,1,0:T(8,128)S(1)}, u32[]{:S(2)}, u32[]{:S(2)}) %collective-permute-start.1) | collective-permute-done | bytes 40992 | tf_op jit(solution)/shard_map/ppermute | solution.py:805
  26.9 0.2 collective-permute-done.refs_1_
  27.1 5.8 %all-to-all-done.1 = f32[8,104,128]{2,1,0:T(8,128)S(1)} async-done(((f32[8,104,128]{2,1,0:T(8,128)}), f32[8,104,128]{2,1,0:T(8,128)S(1)}, u32[]{:S(2)}, u32[]{:S(2)}) %all-to-all-start.1) | async-done | bytes 426016 | tf_op jit(solution)/shard_map/all_to_all | solution.py:740
  33.0 2.0 %shard_map.115 = f32[384,128]{1,0:T(8,128)} custom-call(f32[832,128]{1,0:T(8,128)S(1)} %bitcast.4, f32[8,10,128]{2,1,0:T(8,128)S(1)} %all-to-all-done.refs_0_, f32[8,10,128]{2,1,0:T(8,128)S(1)} %collective-permute-done.refs_1_, f32[8,10,128]{2,1,0:T(8,128)S(1)} %collective-permute-done.1.refs_2_, f32[8,10,128]{2,1,0:T(8,128)S(1)} %collective-permute-done.2.refs_3_), custom_call_target="tpu_custom_call" | custom-call | tf_op jit(solution)/shard_map/pallas_call | solution.py:729
  35.0 3.6 %all-to-all-start.2 = ((f32[8,48,128]{2,1,0:T(8,128)}), f32[8,48,128]{2,1,0:T(8,128)S(1)}, u32[]{:S(2)}, u32[]{:S(2)}) async-start(f32[8,48,128]{2,1,0:T(8,128)} %bitcast.2), calls=%async_computation.2 | async-start | bytes 393216 | tf_op jit(solution)/shard_map/all_to_all | solution.py:740
  38.7 0.8 %copy-done.6 = f32[8,10,128]{2,1,0:T(8,128)S(1)} copy-done((f32[8,10,128]{2,1,0:T(8,128)S(1)}, f32[8,10,128]{2,1,0:T(8,128)}, u32[]{:S(2)}) %copy-start.6) | copy-done | bytes 40984
  39.5 0.8 %copy-done.8 = f32[8,10,128]{2,1,0:T(8,128)S(1)} copy-done((f32[8,10,128]{2,1,0:T(8,128)S(1)}, f32[8,10,128]{2,1,0:T(8,128)}, u32[]{:S(2)}) %copy-start.8) | copy-done | bytes 40984
  40.4 0.8 %copy-done.10 = f32[8,10,128]{2,1,0:T(8,128)S(1)} copy-done((f32[8,10,128]{2,1,0:T(8,128)S(1)}, f32[8,10,128]{2,1,0:T(8,128)}, u32[]{:S(2)}) %copy-start.10) | copy-done | bytes 40984
  41.2 0.7 %copy-done.11 = s32[128]{0:T(128)S(1)} copy-done((s32[128]{0:T(128)S(1)}, s32[128]{0:T(128)}, u32[]{:S(2)}) %copy-start.11) | copy-done | bytes 536
  41.9 0.7 %copy-done.12 = s32[128]{0:T(128)S(1)} copy-done((s32[128]{0:T(128)S(1)}, s32[128]{0:T(128)}, u32[]{:S(2)}) %copy-start.12) | copy-done | bytes 536
  42.5 0.7 %copy-done.13 = s32[128]{0:T(128)S(1)} copy-done((s32[128]{0:T(128)S(1)}, s32[128]{0:T(128)}, u32[]{:S(2)}) %copy-start.13) | copy-done | bytes 536
  43.2 2.5 %shard_map.116 = (f32[2880,128]{1,0:T(8,128)S(1)}, f32[90,128]{1,0:T(8,128)S(1)}, f32[90,128]{1,0:T(8,128)S(1)}) custom-call(s32[128]{0:T(128)S(1)} %copy-done.12, s32[128]{0:T(128)S(1)} %copy-done.13, s32[128]{0:T(128)S(1)} %copy-done.11, f32[16,2304]{1,0:T(8,128)S(1)} %copy-done.3, f32[8,192,128]{2,1,0:T(8,128)S(1)} %copy-done.1, ...), custom_call_target="tpu_custom_call" | custom-call | tf_op jit(solution)/shard_map/pallas_call | solution.py:729
  45.6 3.9 %collective-permute-start.3 = (f32[90,128]{1,0:T(8,128)S(1)}, f32[90,128]{1,0:T(8,128)S(1)}, u32[]{:S(2)}, u32[]{:S(2)}) collective-permute-start(f32[90,128]{1,0:T(8,128)S(1)} %get-tuple-element.14), channel_id=1, source_target_pairs={{0,4},{4,8},{8,12},{12,16},{16,20},{20,24},{24,28},{1,5},{5,9},{9,... | collective-permute-start | bytes 138248 | tf_op jit(solution)/shard_map/ppermute | solution.py:819
  49.6 1.3 %collective-permute-start.4 = (f32[90,128]{1,0:T(8,128)S(1)}, f32[90,128]{1,0:T(8,128)S(1)}, u32[]{:S(2)}, u32[]{:S(2)}) collective-permute-start(f32[90,128]{1,0:T(8,128)S(1)} %get-tuple-element.15), channel_id=1, source_target_pairs={{4,0},{8,4},{12,8},{16,12},{20,16},{24,20},{28,24},{5,1},{9,5},{13... | collective-permute-start | bytes 138248 | tf_op jit(solution)/shard_map/ppermute | solution.py:820
  50.9 0.4 collective-permute-done.3.below_ref
  51.3 4.3 %collective-permute-done.4.above_ref = f32[90,128]{1,0:T(8,128)S(1)} collective-permute-done((f32[90,128]{1,0:T(8,128)S(1)}, f32[90,128]{1,0:T(8,128)S(1)}, u32[]{:S(2)}, u32[]{:S(2)}) %collective-permute-start.4) | collective-permute-done | bytes 46112 | tf_op jit(solution)/shard_map/ppermute | solution.py:820
  55.5 0.0 all-to-all-done.2
  55.6 1.1 %copy-done.2 = f32[1576,128]{1,0:T(8,128)S(1)} copy-done((f32[1576,128]{1,0:T(8,128)S(1)}, f32[1576,128]{1,0:T(8,128)}, u32[]{:S(2)}) %copy-start.2) | copy-done | bytes 806936
  56.7 2.2 %shard_map.117 = (f32[5,16,2304]{2,1,0:T(8,128)}, f32[5,16,2304]{2,1,0:T(8,128)}) custom-call(f32[384,128]{1,0:T(8,128)S(1)} %bitcast.5, f32[2880,128]{1,0:T(8,128)S(1)} %get-tuple-element.12.turned_ref, f32[1576,128]{1,0:T(8,128)S(1)} %copy-done.2, f32[90,128]{1,0:T(8,128)S(1)} %collective-permute-done.3.below_ref, ...), custom_call_target="tpu_custom_call" | custom-call | tf_op jit(solution)/shard_map/pallas_call | solution.py:729
  (17 shorter events, 0.0 us)
Async XLA Ops:
  3.6 14.2 %all-to-all-start = ((f32[8,10,128]{2,1,0:T(8,128)}), f32[8,10,128]{2,1,0:T(8,128)S(1)}, u32[]{:S(2)}, u32[]{:S(2)}) async-start(f32[8,10,128]{2,1,0:T(8,128)} %shard_map.113), calls=%async_computation | async-start | bytes 131072 | tf_op jit(solution)/shard_map/all_to_all | solution.py:740
  14.9 23.7 %copy-start = (f32[5,16,2304]{2,1,0:T(8,128)S(1)}, f32[5,16,2304]{2,1,0:T(8,128)}, u32[]{:S(2)}) copy-start(f32[5,16,2304]{2,1,0:T(8,128)} %state_hbm.5) | copy-start | bytes 2211844
  14.9 23.7 %copy-start.1 = (f32[8,192,128]{2,1,0:T(8,128)S(1)}, f32[8,192,128]{2,1,0:T(8,128)}, u32[]{:S(2)}) copy-start(f32[8,192,128]{2,1,0:T(8,128)} %constant.2.clone.tables_hbm) | copy-start | bytes 2359300
  14.9 23.7 %copy-start.3 = (f32[16,2304]{1,0:T(8,128)S(1)}, f32[16,2304]{1,0:T(8,128)}, u32[]{:S(2)}) copy-start(f32[16,2304]{1,0:T(8,128)} %courant_hbm.3) | copy-start | bytes 442372
  15.0 23.7 %copy-start.4 = (s32[16,2304]{1,0:T(8,128)S(1)}, s32[16,2304]{1,0:T(8,128)}, u32[]{:S(2)}) copy-start(s32[16,2304]{1,0:T(8,128)} %mask_hbm.3) | copy-start | bytes 442372
  17.8 15.2 %all-to-all-start.1 = ((f32[8,104,128]{2,1,0:T(8,128)}), f32[8,104,128]{2,1,0:T(8,128)S(1)}, u32[]{:S(2)}, u32[]{:S(2)}) async-start(f32[8,104,128]{2,1,0:T(8,128)} %bitcast.6), calls=%async_computation.1 | async-start | bytes 851968 | tf_op jit(solution)/shard_map/all_to_all | solution.py:740
  21.2 2.0 %collective-permute-start.2 = (f32[8,10,128]{2,1,0:T(8,128)S(1)}, f32[8,10,128]{2,1,0:T(8,128)S(1)}, u32[]{:S(2)}, u32[]{:S(2)}) collective-permute-start(f32[8,10,128]{2,1,0:T(8,128)S(1)} %all-to-all-done.refs_0_), channel_id=1, source_target_pairs={{0,3},{1,0},{2,1},{3,2},{4,7},{5,4},{6,5},{7,6},{8,11},{9,8},{10,9... | collective-permute-start | bytes 122888 | tf_op jit(solution)/shard_map/ppermute | solution.py:805
  21.3 5.6 %collective-permute-start.1 = (f32[8,10,128]{2,1,0:T(8,128)S(1)}, f32[8,10,128]{2,1,0:T(8,128)S(1)}, u32[]{:S(2)}, u32[]{:S(2)}) collective-permute-start(f32[8,10,128]{2,1,0:T(8,128)S(1)} %all-to-all-done.refs_0_), channel_id=1, source_target_pairs={{0,2},{1,3},{2,0},{3,1},{4,6},{5,7},{6,4},{7,5},{8,10},{9,11},{10,... | collective-permute-start | bytes 122888 | tf_op jit(solution)/shard_map/ppermute | solution.py:805
  22.9 4.3 %collective-permute-start = (f32[8,10,128]{2,1,0:T(8,128)S(1)}, f32[8,10,128]{2,1,0:T(8,128)S(1)}, u32[]{:S(2)}, u32[]{:S(2)}) collective-permute-start(f32[8,10,128]{2,1,0:T(8,128)S(1)} %all-to-all-done.refs_0_), channel_id=1, source_target_pairs={{0,1},{1,2},{2,3},{3,0},{4,5},{5,6},{6,7},{7,4},{8,9},{9,10},{10,1... | collective-permute-start | bytes 122888 | tf_op jit(solution)/shard_map/ppermute | solution.py:805
  23.2 11.8 %copy-start.5 = (f32[8,10,128]{2,1,0:T(8,128)}, f32[8,10,128]{2,1,0:T(8,128)S(1)}, u32[]{:S(2)}) copy-start(f32[8,10,128]{2,1,0:T(8,128)S(1)} %collective-permute-done.2.refs_3_) | copy-start | bytes 122884
  26.9 8.0 %copy-start.7 = (f32[8,10,128]{2,1,0:T(8,128)}, f32[8,10,128]{2,1,0:T(8,128)S(1)}, u32[]{:S(2)}) copy-start(f32[8,10,128]{2,1,0:T(8,128)S(1)} %collective-permute-done.1.refs_2_) | copy-start | bytes 122884
  27.1 7.9 %copy-start.9 = (f32[8,10,128]{2,1,0:T(8,128)}, f32[8,10,128]{2,1,0:T(8,128)S(1)}, u32[]{:S(2)}) copy-start(f32[8,10,128]{2,1,0:T(8,128)S(1)} %collective-permute-done.refs_1_) | copy-start | bytes 122884
  35.0 20.6 %all-to-all-start.2 = ((f32[8,48,128]{2,1,0:T(8,128)}), f32[8,48,128]{2,1,0:T(8,128)S(1)}, u32[]{:S(2)}, u32[]{:S(2)}) async-start(f32[8,48,128]{2,1,0:T(8,128)} %bitcast.2), calls=%async_computation.2 | async-start | bytes 393216 | tf_op jit(solution)/shard_map/all_to_all | solution.py:740
  38.7 0.8 %copy-start.6 = (f32[8,10,128]{2,1,0:T(8,128)S(1)}, f32[8,10,128]{2,1,0:T(8,128)}, u32[]{:S(2)}) copy-start(f32[8,10,128]{2,1,0:T(8,128)} %copy-done.5) | copy-start | bytes 122884
  39.5 0.8 %copy-start.8 = (f32[8,10,128]{2,1,0:T(8,128)S(1)}, f32[8,10,128]{2,1,0:T(8,128)}, u32[]{:S(2)}) copy-start(f32[8,10,128]{2,1,0:T(8,128)} %copy-done.7) | copy-start | bytes 122884
  40.4 0.8 %copy-start.10 = (f32[8,10,128]{2,1,0:T(8,128)S(1)}, f32[8,10,128]{2,1,0:T(8,128)}, u32[]{:S(2)}) copy-start(f32[8,10,128]{2,1,0:T(8,128)} %copy-done.9) | copy-start | bytes 122884
  41.2 0.7 %copy-start.11 = (s32[128]{0:T(128)S(1)}, s32[128]{0:T(128)}, u32[]{:S(2)}) copy-start(s32[128]{0:T(128)} %cell_hbm.3) | copy-start | bytes 1540
  41.8 0.7 %copy-start.12 = (s32[128]{0:T(128)S(1)}, s32[128]{0:T(128)}, u32[]{:S(2)}) copy-start(s32[128]{0:T(128)} %owner_hbm.3) | copy-start | bytes 1540
  42.5 0.7 %copy-start.13 = (s32[128]{0:T(128)S(1)}, s32[128]{0:T(128)}, u32[]{:S(2)}) copy-start(s32[128]{0:T(128)} %image_hbm.3) | copy-start | bytes 1540
  45.6 5.7 %collective-permute-start.3 = (f32[90,128]{1,0:T(8,128)S(1)}, f32[90,128]{1,0:T(8,128)S(1)}, u32[]{:S(2)}, u32[]{:S(2)}) collective-permute-start(f32[90,128]{1,0:T(8,128)S(1)} %get-tuple-element.14), channel_id=1, source_target_pairs={{0,4},{4,8},{8,12},{12,16},{16,20},{20,24},{24,28},{1,5},{5,9},{9,... | collective-permute-start | bytes 138248 | tf_op jit(solution)/shard_map/ppermute | solution.py:819
  49.6 6.0 %collective-permute-start.4 = (f32[90,128]{1,0:T(8,128)S(1)}, f32[90,128]{1,0:T(8,128)S(1)}, u32[]{:S(2)}, u32[]{:S(2)}) collective-permute-start(f32[90,128]{1,0:T(8,128)S(1)} %get-tuple-element.15), channel_id=1, source_target_pairs={{4,0},{8,4},{12,8},{16,12},{20,16},{24,20},{28,24},{5,1},{9,5},{13... | collective-permute-start | bytes 138248 | tf_op jit(solution)/shard_map/ppermute | solution.py:820
  55.6 1.1 %copy-start.2 = (f32[1576,128]{1,0:T(8,128)S(1)}, f32[1576,128]{1,0:T(8,128)}, u32[]{:S(2)}) copy-start(f32[1576,128]{1,0:T(8,128)} %get-tuple-element.13.kept_ref) | copy-start | bytes 2420740

commit v2 on v1

--- a/solution.py
+++ b/solution.py
@@ -143,6 +143,16 @@
     return (which * rows + i) * (-(-count // 8) * 8)
 
 
+def stay_at(rows, count, cells):
+    kept = kept_at(4, 0, rows, count) + 40
+    return kept, kept, kept + cells, kept + cells + 8
+
+
+def ready_at(rows, count, cells):
+    kept = 2 * cells * count
+    return cells * count, kept, kept + stay_at(rows, count, cells)[3]
+
+
 def fetch(sources, targets, sems):
     copies = [
         pltpu.make_async_copy(source, target, sems.at[k])
@@ -154,20 +164,22 @@
 
 
 class Slices:
-    def __init__(self, slabs, count, var_count):
+    def __init__(self, slabs, count, cross, var_count, images):
         rest = count % slabs
-        self.slabs, self.count, self.var_count = slabs, count, var_count
+        self.slabs, self.count, self.cross, self.var_count = slabs, count, cross, var_count
+        self.image_rows = var_count * images // LANES
         shared = rest > 0 and slabs % rest == 0 and LANES % (slabs // rest) == 0
         self.full = count // slabs if shared else -(-count // slabs)
         self.rest = rest if shared else 0
         self.per = slabs // rest if shared else 1
         self.width = LANES // self.per
         self.chunk = self.full + (1 if shared else 0)
-        self.lines, self.back_lines = 6 * var_count + COEFFICIENTS, 4 * var_count
+        self.lines, self.back_lines = 6 * var_count + COEFFICIENTS, 6 * var_count
         self.groups, self.back_groups = (self.group_count(n) for n in (self.lines, self.back_lines))
         self.meta_at = self.lines * self.full
         self.packed_at = self.meta_at + 8
-        self.height = -(-(self.packed_at + self.groups) // 8) * 8
+        self.images_at = self.packed_at + self.groups
+        self.height = -(-(self.images_at + self.image_rows) // 8) * 8
         self.back_packed_at = self.back_lines * self.full
         self.back_height = -(-(self.back_packed_at + self.back_groups) // 8) * 8
 
@@ -187,21 +199,14 @@
     return x if by == 0 else pltpu.roll(x, by, 1)
 
 
-def image_kernel(state_hbm, base_hbm, weight_hbm, out_ref, state_ref, base_ref, weight_ref, sems):
-    var_count, rows, pencils = state_ref.shape
-    images = base_ref.shape[0]
-    copies = fetch(
-        (state_hbm, base_hbm, weight_hbm), (state_ref, base_ref, weight_ref), sems
-    )
-    for copy in copies[1:]:
-        copy.wait()
-    row, pencil = place_of(base_ref[...].reshape(1, images), rows, pencils)
+def image_lines(x, base, weight_ref, rows, var_count):
+    pencils = x.shape[1]
+    images = base.shape[1]
+    row, pencil = place_of(base, rows, pencils)
     pick = marks((pencils, images), 0, pencil)
     row_at = lax.broadcasted_iota(jnp.int32, (rows, images), 0)
     lower, upper = row_at == row, row_at == row + 1
     total = [jnp.zeros((rows, images), jnp.float32) for _ in range(var_count)]
-    copies[0].wait()
-    x = state_ref[...].reshape(var_count * rows, pencils)
     for corner, shift in enumerate((0, 1, LINE, LINE + 1)):
         moved = x if shift == 0 else pltpu.roll(x, pencils - shift, 1)
         pieces = jnp.concatenate(split(moved, 2), axis=0)
@@ -216,32 +221,35 @@
     for v in range(var_count):
         value = jnp.sum(total[v], axis=0, keepdims=True)
         lines += [value[:, tile(t)] for t in range(images // LANES)]
-    lines = jnp.concatenate(lines, axis=0)
-    for k in range(out_ref.shape[0]):
-        out_ref[k] = lines
-
-
-def ghost_values(blocks, owner, image):
-    cross = len(blocks)
-    slabs, lines, _ = blocks[0].shape
-    per = lines // len(REFLECT)
+    return jnp.concatenate(lines, axis=0)
+
+
+def ghost_values(slices, blocks, owner, image):
+    per = slices.image_rows // slices.var_count
+    slabs, cross = slices.slabs, slices.cross
     ghosts = owner.shape[1]
-    me = lax.axis_index("cross")
+    across = lax.axis_index("cross")
     values = [
         jnp.concatenate(
             [
-                jnp.concatenate([block[:, v * per + t, :] for t in range(per)], axis=1)
+                jnp.concatenate(
+                    [
+                        block[pl.ds(v * per + t, slabs, stride=slices.image_rows), :]
+                        for t in range(per)
+                    ],
+                    axis=1,
+                )
                 for block in blocks
             ],
             axis=0,
         )
-        for v in range(len(REFLECT))
+        for v in range(slices.var_count)
     ]
     pick = marks((per * LANES, ghosts), 0, image)
     found = exact_dot(jnp.concatenate(values, axis=0), pick, ((1,), (0,)))
     devices = slabs * cross
     at = lax.broadcasted_iota(jnp.int32, (devices, ghosts), 0)
-    mine = (at % slabs) * cross + (me + cross - at // slabs) % cross == owner
+    mine = (at % slabs) * cross + (across + cross - at // slabs) % cross == owner
     return [
         reflect
         * jnp.sum(
@@ -261,9 +269,11 @@
     owner_hbm,
     image_hbm,
     mask_hbm,
+    base_hbm,
+    corner_hbm,
     state_hbm,
     message_ref,
-    kept_ref,
+    stay_ref,
     face_ref,
     courant_ref,
     table_ref,
@@ -271,6 +281,8 @@
     owner_ref,
     image_ref,
     mask_ref,
+    base_ref,
+    corner_ref,
     state_ref,
     turned_ref,
     pair_ref,
@@ -289,12 +301,35 @@
     p = lax.axis_index("pipe")
     slabs, height = slices.slabs, slices.height
     lines = slices.groups * slices.per
-    _, reduce_at, adjoint_at, profile_at, weight_at = at
+    own_at, reduce_at, adjoint_at, profile_at, weight_at = at
     copies = fetch(
-        (face_hbm, courant_hbm, tables_hbm.at[p], cell_hbm, owner_hbm, image_hbm, mask_hbm, state_hbm),
-        (face_ref, courant_ref, table_ref, cell_ref, owner_ref, image_ref, mask_ref, state_ref),
+        (
+            face_hbm,
+            courant_hbm,
+            tables_hbm.at[p],
+            cell_hbm,
+            owner_hbm,
+            image_hbm,
+            mask_hbm,
+            base_hbm,
+            corner_hbm,
+            state_hbm,
+        ),
+        (
+            face_ref,
+            courant_ref,
+            table_ref,
+            cell_ref,
+            owner_ref,
+            image_ref,
+            mask_ref,
+            base_ref,
+            corner_ref,
+            state_ref,
+        ),
         sems,
     )
+    kept, own, about_at, cleared_at = stay_at(rows, count, cells)
 
     def send(line, slab):
         for t in range(slices.full):
@@ -327,7 +362,7 @@
         to_up[i], to_first[i] = up, low
         for k, part in enumerate((up, low, inverse)):
             start = kept_at(k, i, rows, count)
-            kept_ref[start : start + count, :] = part
+            stay_ref[start : start + count, :] = part
         first_margin += low * margin
         link = link * up
         margin = 1.0 + margin * up
@@ -347,13 +382,14 @@
     for i in range(rows):
         speed = slab_at(turned_ref, i, rows, count)
         start = kept_at(3, i, rows, count)
-        kept_ref[start : start + count, :] = speed
+        stay_ref[start : start + count, :] = speed
         put_slab(pair_ref, i, 2 * rows, count, first[i] * speed)
         put_slab(pair_ref, rows + i, 2 * rows, count, last[i] * speed)
     for t in range(count):
         matrix_ref[:, tile(t)] = pair_ref[t * 2 * rows : (t + 1) * 2 * rows, :]
     copies[2].wait()
-    kept_ref[kept_ref.shape[0] - 40 :, :] = table_ref[profile_at : profile_at + 40, :]
+    stay_ref[kept - 40 : kept, :] = table_ref[profile_at : profile_at + 40, :]
+    stay_ref[own : own + cells, :] = table_ref[own_at : own_at + cells, :]
     turn(
         adjoint_ref, full_dot(table_ref[adjoint_at : adjoint_at + 40, : 2 * rows], matrix_ref[...])
     )
@@ -395,21 +431,32 @@
     for j in range(slabs):
         start = j * height + slices.meta_at
         message_ref[start : start + 8, :] = about
-
-    copies[6].wait()
-    copies[7].wait()
+    stay_ref[about_at : about_at + 8, :] = about
+    for copy in copies[6:]:
+        copy.wait()
+    values = image_lines(
+        state_ref[...].reshape(cells, pencils),
+        base_ref[...].reshape(1, base_ref.shape[0]),
+        corner_ref,
+        rows,
+        var_count,
+    )
+    for j in range(slabs):
+        start = j * height + slices.images_at
+        message_ref[start : start + slices.image_rows, :] = values
     solid = mask_ref[...] == 1
     for v in range(var_count):
         here = slice(v * rows, (v + 1) * rows)
         cleared_ref[here, :] = jnp.where(solid, 0.0, state_ref[v])
-    turn(turned_ref, cleared_ref[...])
+    turned = stay_ref.at[cleared_at : cleared_at + cells * count, :]
+    turn(turned, cleared_ref[...])
     turn(pair_ref, full_dot(table_ref[reduce_at : reduce_at + 16, :cells], cleared_ref[...]))
     for k in range(2 * var_count):
         send(k, slab_at(pair_ref, k, 16, count))
     for v in range(var_count):
         low = high = zero
         for i in range(rows):
-            cell = slab_at(turned_ref, v * rows + i, cells, count)
+            cell = slab_at(stay_ref, cleared_at + v * rows + i, cells, count)
             if i == 0:
                 send_value(ROW_FIRST, v, cell)
             if i == rows - 1:
@@ -447,7 +494,7 @@
     def meta_all(k):
         return jnp.concatenate([meta(p, k) for p in range(slabs)], axis=1).astype(jnp.int32)
 
-    values = ghost_values(blocks, meta_all(OWNER), meta_all(IMAGE))
+    values = ghost_values(slices, blocks, meta_all(OWNER), meta_all(IMAGE))
     ghost_lines = 6 * var_count + 2
     ghosts = LANES
     place = lax.broadcasted_iota(jnp.int32, (chunk * LANES, ghosts), 0)
@@ -547,6 +594,8 @@
             )
             give(p, 2, v, lo[p])
             give(p, 3, v, hi[p])
+            give(p, 4, v, below[p])
+            give(p, 5, v, above[p])
         for k in range(1, nodes):
             right[k] = right[k] + ratio[k - 1] * right[k - 1]
         x = right[nodes - 1] * scale[nodes - 1]
@@ -566,65 +615,62 @@
             back_ref[start : start + groups, :] = packed
 
 
-def fill_kernel(at, owner_hbm, image_hbm, cell_hbm, courant_hbm, tables_hbm, mask_hbm, state_hbm, *refs):
-    *blocks, turned_ref, up_ref, down_ref = refs[:-9]
-    owner_ref, image_ref, cell_ref, courant_ref, table_ref, mask_ref, state_ref = refs[-9:-2]
-    filled_ref, sems = refs[-2:]
-    var_count, rows, pencils = state_ref.shape
+def pick_kernel(slices, message_ref, values_ref):
+    size = slices.image_rows
+    for p in range(slices.slabs):
+        start = p * slices.height + slices.images_at
+        values_ref[p * size : (p + 1) * size, :] = message_ref[start : start + size, :]
+
+
+def own_kernel(shape, stay_ref, ready_ref):
+    var_count, rows, pencils = shape
     cells = var_count * rows
     count = pencils // LANES
-    ghosts = cell_ref.shape[0]
-    copies = fetch(
-        (
-            owner_hbm,
-            image_hbm,
-            cell_hbm,
-            courant_hbm,
-            tables_hbm.at[lax.axis_index("pipe")],
-            mask_hbm,
-            state_hbm,
-        ),
-        (owner_ref, image_ref, cell_ref, courant_ref, table_ref, mask_ref, state_ref),
-        sems,
-    )
-    for copy in copies[:3]:
-        copy.wait()
-    owner, image = (ref[...].reshape(1, ghosts) for ref in (owner_ref, image_ref))
-    values = ghost_values(blocks, owner, image)
-    row, pencil = place_of(cell_ref[...].reshape(1, ghosts), rows, pencils)
-    spots = marks((pencils, ghosts), 0, pencil)
-    at_row = lax.broadcasted_iota(jnp.int32, (rows, ghosts), 0) == row
+    _, own_at, _, cleared_at = stay_at(rows, count, cells)
+    cells_at, kept_start, end = ready_at(rows, count, cells)
+    cleared = [
+        stay_ref[cleared_at + t * cells : cleared_at + (t + 1) * cells, :] for t in range(count)
+    ]
+    for t in range(count):
+        ready_ref[cells_at + t * cells : cells_at + (t + 1) * cells, :] = cleared[t]
+    turn(
+        ready_ref.at[: cells * count, :],
+        full_dot(stay_ref[own_at : own_at + cells, :cells], jnp.concatenate(cleared, axis=1)),
+    )
+    ready_ref[kept_start:end, :] = stay_ref[:cleared_at, :]
+
+
+def fill_kernel(slices, shape, ready_ref, *refs):
+    *blocks, filled_ref = refs
+    var_count, rows, pencils = shape
+    cells = var_count * rows
+    count = pencils // LANES
+    _, own_at, about_at, _ = stay_at(rows, count, cells)
+    _, kept_start, end = ready_at(rows, count, cells)
+
+    def known(k):
+        start = kept_start + about_at + k
+        return ready_ref[start : start + 1, :].astype(jnp.int32)
+
+    values = ghost_values(slices, blocks, known(OWNER), known(IMAGE))
+    ghosts = LANES
+    at_row = lax.broadcasted_iota(jnp.int32, (rows, ghosts), 0) == known(ROW)
     spread = jnp.concatenate([jnp.where(at_row, value, 0.0) for value in values], axis=0)
-    placed = exact_dot(spread, spots, ((1,), (1,)))
-    for copy in copies[3:]:
-        copy.wait()
-    solid = mask_ref[...] == 1
-    for v in range(var_count):
-        here = slice(v * rows, (v + 1) * rows)
-        filled_ref[here, :] = jnp.where(solid, 0.0, state_ref[v]) + placed[here]
-    for v in range(var_count):
-        for t in range(count):
-            line = slice(v * count + t, v * count + t + 1)
-            down_ref[line, :] = filled_ref[v * rows : v * rows + 1, tile(t)]
-            up_ref[line, :] = filled_ref[(v + 1) * rows - 1 : (v + 1) * rows, tile(t)]
-    own = full_dot(table_ref[at[0] : at[0] + cells, :cells], filled_ref[...])
-    turn(turned_ref.at[: cells * count, :], own)
-    courant = courant_ref[...]
-    for v in range(var_count):
-        here = slice(v * rows, (v + 1) * rows)
-        right = filled_ref[here, :] - courant * own[here]
-        for t in range(count):
-            start = (count + t) * cells + v * rows
-            turned_ref[start : start + rows, :] = right[:, tile(t)]
+    own = ready_ref[kept_start + own_at : kept_start + own_at + cells, :cells]
+    both = jnp.concatenate([full_dot(own, spread), spread], axis=0)
+    spots = marks((pencils, ghosts), 0, known(PENCIL))
+    added = exact_dot(both, spots, ((1,), (1,)))
+    for t in range(count):
+        for k in range(2):
+            here = slice((k * count + t) * cells, (k * count + t + 1) * cells)
+            filled_ref[here, :] = ready_ref[here, :] + added[k * cells : (k + 1) * cells, tile(t)]
+    filled_ref[kept_start:end, :] = ready_ref[kept_start:end, :]
 
 
 def finish_kernel(
     slices,
     back_ref,
-    turned_ref,
-    kept_ref,
-    below_ref,
-    above_ref,
+    ready_ref,
     derivative_hbm,
     segment_hbm,
     derivative_ref,
@@ -638,7 +684,8 @@
     count = pencils // LANES
     cells = var_count * rows
     variables = range(var_count)
-    profile_at = kept_ref.shape[0] - 40
+    filled_start, kept_start, _ = ready_at(rows, count, cells)
+    profile_at = kept_start + stay_at(rows, count, cells)[0] - 40
     back_height, groups, per = slices.back_height, slices.back_groups, slices.per
     block = lane_block(max(groups, 1), slices.width)
     for m in range(slices.rest):
@@ -666,11 +713,11 @@
         return jnp.concatenate(parts, axis=0)
 
     def profile(k):
-        return kept_ref[profile_at + k : profile_at + k + 1, :]
+        return ready_ref[profile_at + k : profile_at + k + 1, :]
 
     def kept(which, i):
-        start = kept_at(which, i, rows, count)
-        return kept_ref[start : start + count, :]
+        start = kept_start + kept_at(which, i, rows, count)
+        return ready_ref[start : start + count, :]
 
     def give(turned, straight, hbm, which):
         copies = []
@@ -689,17 +736,15 @@
     for i in range(rows):
         for v in variables:
             row = v * rows + i
-            edge = slice(v * count, (v + 1) * count)
             far = profile(i) * lo[v] + profile(rows + i) * hi[v]
             if i == 0:
-                far += profile(2 * rows) * below_ref[edge, :]
+                far += profile(2 * rows) * got(4, v)
             if i == rows - 1:
-                far += profile(2 * rows + 1) * above_ref[edge, :]
-            value = slab_at(turned_ref, row, cells, count) + far
+                far += profile(2 * rows + 1) * got(5, v)
+            value = slab_at(ready_ref, row, cells, count) + far
             put_slab(derivative_turned_ref, row, cells, count, value)
             if 0 < i < rows - 1:
-                right = slab_at(turned_ref, cells * count + row, cells, count)
-                right -= kept(3, i) * far
+                right = slab_at(ready_ref, filled_start + row, cells, count) - kept(3, i) * value
                 if i > 1:
                     right += kept(0, i - 1) * swept[v][i - 1]
                 swept[v][i] = right
@@ -757,21 +802,11 @@
     cells = var_count * rows
     images = image_base.shape[0]
     tables, at, carry_up, carry_down = derivative_tables(slabs, rows, var_count)
-    slices = Slices(slabs, count, var_count)
+    slices = Slices(slabs, count, cross, var_count, images)
     tables = jnp.asarray(tables)
-    table = jax.ShapeDtypeStruct(tables.shape[1:], jnp.float32)
     turned = (cells * count, LANES)
-    edge = (var_count * count, LANES)
-    kept = (kept_at(4, 0, rows, count) + 40, LANES)
-
-    (image_values,) = call(
-        image_kernel,
-        [(slabs, var_count * images // LANES, LANES)],
-        [state, image_base, image_weight],
-        [3],
-        (state, image_base, image_weight),
-    )
-    image_values = exchange(image_values, "pipe")
+    stay = stay_at(rows, count, cells)[3] + cells * count
+    ready = (ready_at(rows, count, cells)[2], LANES)
 
     arguments = (
         face_diffusion,
@@ -781,14 +816,18 @@
         ghost_owner,
         ghost_image,
         cell_mask,
+        image_base,
+        image_weight,
         state,
     )
-    message, kept_here = call(
+    buffers = list(arguments)
+    buffers[2] = jax.ShapeDtypeStruct(tables.shape[1:], jnp.float32)
+    message, stay = call(
         functools.partial(prepare_kernel, slices, at),
-        [(slabs * slices.height, LANES), kept],
-        [face_diffusion, courant, table, ghost_cell, ghost_owner, ghost_image, cell_mask, state]
+        [(slabs * slices.height, LANES), (stay, LANES)],
+        buffers
         + [
-            turned,
+            (rows * count, LANES),
             (2 * rows * count, LANES),
             (2 * rows, pencils),
             (40 * count, LANES),
@@ -799,25 +838,23 @@
         [len(arguments)],
         arguments,
     )
-    image_values, message = lax.optimization_barrier((image_values, message))
     message = exchange(message, "pipe")
+    (ready,) = call(
+        functools.partial(own_kernel, state.shape), [ready], [], [], (stay,), near=(0,), limit=48
+    )
+    (image_values,) = call(
+        functools.partial(pick_kernel, slices),
+        [(slabs * slices.image_rows, LANES)],
+        [],
+        [],
+        (message,),
+        near=(0,),
+        limit=24,
+    )
     blocks = [image_values] + [
-        lax.ppermute(image_values, "cross", [(i, (i + s) % cross) for i in range(cross)])
-        for s in range(1, cross)
+        lax.ppermute(image_values, "cross", [(i, (i + u) % cross) for i in range(cross)])
+        for u in range(1, cross)
     ]
-    arguments = (ghost_owner, ghost_image, ghost_cell, courant, tables, cell_mask, state, *blocks)
-    turned_here, up, down = call(
-        functools.partial(fill_kernel, at),
-        [(2 * cells * count, LANES), edge, edge],
-        [ghost_owner, ghost_image, ghost_cell, courant, table, cell_mask, state, (cells, pencils)],
-        [7],
-        arguments,
-        near=range(7, 7 + cross),
-        limit=48,
-    )
-    forward = [(i, i + 1) for i in range(slabs - 1)]
-    below = lax.ppermute(up, "pipe", forward)
-    above = lax.ppermute(down, "pipe", [(j, i) for i, j in forward])
 
     spare = slabs * slices.per
     (back,) = call(
@@ -834,7 +871,15 @@
         limit=24,
     )
     back = exchange(back, "pipe")
-    arguments = (back, turned_here, kept_here, below, above)
+    (ready,) = call(
+        functools.partial(fill_kernel, slices, state.shape),
+        [ready.shape],
+        [],
+        [],
+        (ready, *blocks),
+        near=range(1 + cross),
+        limit=48,
+    )
     return tuple(
         call(
             functools.partial(finish_kernel, slices),
@@ -847,8 +892,8 @@
                 (max(slices.rest, 1) * max(slices.back_groups, 1) * slices.per, LANES),
             ],
             [2 * var_count],
-            arguments,
-            near=range(len(arguments)),
+            (back, ready),
+            near=range(2),
             far_out=True,
             limit=48,
         )

time: 59.5 us -> 48.6 us (0.82)
  blocking collectives: 0 us -> 20.7 us
  starting transfers between devices: 21.4 us -> 5.31 us
  waiting for transfers between devices: 17.4 us -> 10.3 us
  local copies, waits for them, and re-layouts: 5.65 us -> 0.01 us
  Pallas kernels: 13.6 us -> 11.3 us
    all_to_all x0 -> x1, blocking collectives: none -> 20.7 us  [exchange(): return lax.all_to_all(message, axes, 0, 0, tiled=True)]
    all_to_all x3 -> x1, starting transfers between devices: 14.4 us -> 3.59 us  [exchange(): return lax.all_to_all(message, axes, 0, 0, tiled=True)]
    unnamed x28 -> x2, local copies, waits for them, and re-layouts: 5.65 us -> 0.01 us
    ppermute x5 -> x3, waiting for transfers between devices: 8.78 us -> 3.27 us  [local(): lax.ppermute(image_values, 'cross', [(i, (i + u) % cross) for i in range(...]
    ppermute x5 -> x3, starting transfers between devices: 6.99 us -> 1.71 us  [local(): lax.ppermute(image_values, 'cross', [(i, (i + u) % cross) for i in range(...]
    pallas_call x5 -> x6, Pallas kernels: 13.6 us -> 11.3 us  [call(): pl.pallas_call(kernel, out_shape=[jax.ShapeDtypeStruct(shape, jnp.float32...]
    all_to_all x3 -> x1, waiting for transfers between devices: 8.65 us -> 7.04 us  [exchange(): return lax.all_to_all(message, axes, 0, 0, tiled=True)]
  transfers between devices with their start and end apart: 8 -> 4, of which waited for: 7 -> 3; matrix products, arithmetic and copies ran while one was open for 0% -> 0% of each run, Pallas kernels for 11% -> 4%
where the time goes in v2:
time: 48.6 us; the launch traced here: 48.3 us
  blocking collectives  20.7 us (43%)
  Pallas kernels  11.3 us (23%)
  waiting for transfers between devices  10.3 us (21%)
  starting transfers between devices  5.31 us (11%)
  between operations  0.68 us (1%)
    all_to_all x1, blocking collectives, exchange(): return lax.all_to_all(message, axes, 0, 0, tiled=True)  20.7 us
    pallas_call x6, Pallas kernels, call(): pl.pallas_call(kernel, out_shape=[jax.ShapeDtypeStruct(shape, jnp.float32...  11.3 us
    all_to_all x1, waiting for transfers between devices, exchange(): return lax.all_to_all(message, axes, 0, 0, tiled=True)  7.04 us
    all_to_all x1, starting transfers between devices, exchange(): return lax.all_to_all(message, axes, 0, 0, tiled=True)  3.59 us
    ppermute x3, waiting for transfers between devices, local(): lax.ppermute(image_values, 'cross', [(i, (i + u) % cross) for i in range(...  3.27 us
    ppermute x3, starting transfers between devices, local(): lax.ppermute(image_values, 'cross', [(i, (i + u) % cross) for i in range(...  1.71 us
  transfers between devices with their start and end apart: 4, of which 3 were waited for; matrix products, arithmetic and copies ran while one was open for 0% of the time, Pallas kernels for 4%

profile of v2, /device:TPU:0, one launch (start us, length us, event | category | flops | bytes accessed | tf_op | source)
XLA Modules:
  0.0 48.3 jit_solution(7036787289342848813)
XLA Ops:
  0.6 5.2 %shard_map.113 = (f32[896,128]{1,0:T(8,128)}, f32[3104,128]{1,0:T(8,128)}) custom-call(f32[16,2304]{1,0:T(8,128)} %face_hbm.1, f32[16,2304]{1,0:T(8,128)} %courant_hbm.1, f32[8,192,128]{2,1,0:T(8,128)} %constant.2.clone.tables_hbm, s32[128]{0:T(128)} %cell_hbm.1, s32[128]{0:T(128)} %owner_hbm.1, s32[128]{0:T(128)} %image_hbm.1, s32[16,2304]{1,0:T(8,128)} %mask_hbm.1, ...), custom_call_target="tpu_custom_call" | custom-call | tf_op jit(solution)/shard_map/pallas_call | solution.py:774
  5.9 0.0 copy-start
  5.9 20.7 %all_to_all.22 = f32[8,112,128]{2,1,0:T(8,128)S(1)} all-to-all(f32[8,112,128]{2,1,0:T(8,128)} %bitcast.7), channel_id=1, replica_groups=mesh['pipe'=8,'cross'=4] {'pipe'}, dimensions={0} | all-to-all | bytes 917504 | tf_op jit(solution)/shard_map/all_to_all | solution.py:785
  26.6 0.0 collective-permute-start.2
  26.6 1.6 %collective-permute-start.1 = (f32[80,128]{1,0:T(8,128)S(1)}, f32[80,128]{1,0:T(8,128)S(1)}, u32[]{:S(2)}, u32[]{:S(2)}) collective-permute-start(f32[80,128]{1,0:T(8,128)S(1)} %shard_map.114.refs_0_), channel_id=1, source_target_pairs={{0,2},{1,3},{2,0},{3,1},{4,6},{5,7},{6,4},{7,5},{8,10},{9,11},{10,... | collective-permute-start | bytes 122888 | tf_op jit(solution)/shard_map/ppermute | solution.py:855
  28.1 0.2 collective-permute-start
  28.3 0.0 collective-permute-done.2.refs_3_
  28.3 2.6 %collective-permute-done.1.refs_2_ = f32[80,128]{1,0:T(8,128)S(1)} collective-permute-done((f32[80,128]{1,0:T(8,128)S(1)}, f32[80,128]{1,0:T(8,128)S(1)}, u32[]{:S(2)}, u32[]{:S(2)}) %collective-permute-start.1) | collective-permute-done | bytes 40992 | tf_op jit(solution)/shard_map/ppermute | solution.py:855
  30.9 0.6 %collective-permute-done.refs_1_ = f32[80,128]{1,0:T(8,128)S(1)} collective-permute-done((f32[80,128]{1,0:T(8,128)S(1)}, f32[80,128]{1,0:T(8,128)S(1)}, u32[]{:S(2)}, u32[]{:S(2)}) %collective-permute-start) | collective-permute-done | bytes 40992 | tf_op jit(solution)/shard_map/ppermute | solution.py:855
  31.6 2.0 %shard_map.115 = f32[576,128]{1,0:T(8,128)} custom-call(f32[896,128]{1,0:T(8,128)S(1)} %bitcast.5, f32[80,128]{1,0:T(8,128)S(1)} %shard_map.114.refs_0_, f32[80,128]{1,0:T(8,128)S(1)} %collective-permute-done.refs_1_, f32[80,128]{1,0:T(8,128)S(1)} %collective-permute-done.1.refs_2_, f32[80,128]{1,0:T(8,128)S(1)} %collective-permute-done.2.refs_3_), custom_call_target="tpu_custom_call" | custom-call | tf_op jit(solution)/shard_map/pallas_call | solution.py:774
  33.5 3.6 %all-to-all-start.1 = ((f32[8,72,128]{2,1,0:T(8,128)}), f32[8,72,128]{2,1,0:T(8,128)S(1)}, u32[]{:S(2)}, u32[]{:S(2)}) async-start(f32[8,72,128]{2,1,0:T(8,128)} %bitcast.2), calls=%async_computation.1 | async-start | bytes 589824 | tf_op jit(solution)/shard_map/all_to_all | solution.py:785
  37.1 0.0 copy-done
  37.1 0.7 %shard_map.116.ready_ref = f32[4544,128]{1,0:T(8,128)S(1)} custom-call(f32[3104,128]{1,0:T(8,128)S(1)} %copy-done), custom_call_target="tpu_custom_call" | custom-call | tf_op jit(solution)/shard_map/pallas_call | solution.py:774
  37.9 1.2 %shard_map.117.ready_ref = f32[4544,128]{1,0:T(8,128)S(1)} custom-call(f32[4544,128]{1,0:T(8,128)S(1)} %shard_map.116.ready_ref, f32[80,128]{1,0:T(8,128)S(1)} %shard_map.114.refs_0_, f32[80,128]{1,0:T(8,128)S(1)} %collective-permute-done.refs_1_, f32[80,128]{1,0:T(8,128)S(1)} %collective-permute-done.1.refs_2_, f32[80,128]{1,0:T(8,128)S(1)} %collective-permute-done.2.refs_3_), custom_call_target="tpu_custom_call" | custom-call | tf_op jit(solution)/shard_map/pallas_call | solution.py:774
  39.1 7.0 %all-to-all-done.1 = f32[8,72,128]{2,1,0:T(8,128)S(1)} async-done(((f32[8,72,128]{2,1,0:T(8,128)}), f32[8,72,128]{2,1,0:T(8,128)S(1)}, u32[]{:S(2)}, u32[]{:S(2)}) %all-to-all-start.1) | async-done | bytes 294944 | tf_op jit(solution)/shard_map/all_to_all | solution.py:785
  46.1 2.2 %shard_map.118 = (f32[5,16,2304]{2,1,0:T(8,128)}, f32[5,16,2304]{2,1,0:T(8,128)}) custom-call(f32[576,128]{1,0:T(8,128)S(1)} %bitcast.6, f32[4544,128]{1,0:T(8,128)S(1)} %shard_map.117.ready_ref), custom_call_target="tpu_custom_call" | custom-call | tf_op jit(solution)/shard_map/pallas_call | solution.py:774
  (1 shorter events, 0.0 us)
Async XLA Ops:
  5.9 31.2 %copy-start = (f32[3104,128]{1,0:T(8,128)S(1)}, f32[3104,128]{1,0:T(8,128)}, u32[]{:S(2)}) copy-start(f32[3104,128]{1,0:T(8,128)} %get-tuple-element.5.stay_ref) | copy-start | bytes 4767748
  26.6 1.7 %collective-permute-start.2 = (f32[80,128]{1,0:T(8,128)S(1)}, f32[80,128]{1,0:T(8,128)S(1)}, u32[]{:S(2)}, u32[]{:S(2)}) collective-permute-start(f32[80,128]{1,0:T(8,128)S(1)} %shard_map.114.refs_0_), channel_id=1, source_target_pairs={{0,3},{1,0},{2,1},{3,2},{4,7},{5,4},{6,5},{7,6},{8,11},{9,8},{10,9... | collective-permute-start | bytes 122888 | tf_op jit(solution)/shard_map/ppermute | solution.py:855
  26.6 4.3 %collective-permute-start.1 = (f32[80,128]{1,0:T(8,128)S(1)}, f32[80,128]{1,0:T(8,128)S(1)}, u32[]{:S(2)}, u32[]{:S(2)}) collective-permute-start(f32[80,128]{1,0:T(8,128)S(1)} %shard_map.114.refs_0_), channel_id=1, source_target_pairs={{0,2},{1,3},{2,0},{3,1},{4,6},{5,7},{6,4},{7,5},{8,10},{9,11},{10,... | collective-permute-start | bytes 122888 | tf_op jit(solution)/shard_map/ppermute | solution.py:855
  28.1 3.4 %collective-permute-start = (f32[80,128]{1,0:T(8,128)S(1)}, f32[80,128]{1,0:T(8,128)S(1)}, u32[]{:S(2)}, u32[]{:S(2)}) collective-permute-start(f32[80,128]{1,0:T(8,128)S(1)} %shard_map.114.refs_0_), channel_id=1, source_target_pairs={{0,1},{1,2},{2,3},{3,0},{4,5},{5,6},{6,7},{7,4},{8,9},{9,10},{10,1... | collective-permute-start | bytes 122888 | tf_op jit(solution)/shard_map/ppermute | solution.py:855
  33.5 12.6 %all-to-all-start.1 = ((f32[8,72,128]{2,1,0:T(8,128)}), f32[8,72,128]{2,1,0:T(8,128)S(1)}, u32[]{:S(2)}, u32[]{:S(2)}) async-start(f32[8,72,128]{2,1,0:T(8,128)} %bitcast.2), calls=%async_computation.1 | async-start | bytes 589824 | tf_op jit(solution)/shard_map/all_to_all | solution.py:785

commit v3 on v2

--- a/solution.py
+++ b/solution.py
@@ -153,6 +153,13 @@
     return cells * count, kept, kept + stay_at(rows, count, cells)[3]
 
 
+def done_at(rows, count, cells):
+    x = cells * count
+    response = 2 * x
+    profile = response + 4 * rows * count
+    return x, response, profile, profile + 40
+
+
 def fetch(sources, targets, sems):
     copies = [
         pltpu.make_async_copy(source, target, sems.at[k])
@@ -185,6 +192,12 @@
 
     def group_count(self, lines):
         return -(-lines // self.per) if self.rest else 0
+
+    def row(self, functional, t):
+        return (functional * self.full + t) * self.var_count
+
+    def coefficient_row(self, which, t):
+        return 6 * self.full * self.var_count + which * self.full + t
 
     def tiles_at(self, t):
         return t * self.slabs, min(self.count, (t + 1) * self.slabs)
@@ -273,7 +286,7 @@
     corner_hbm,
     state_hbm,
     message_ref,
-    stay_ref,
+    stay_hbm,
     face_ref,
     courant_ref,
     table_ref,
@@ -284,14 +297,18 @@
     base_ref,
     corner_ref,
     state_ref,
-    turned_ref,
+    stay_ref,
+    face_turned_ref,
+    courant_turned_ref,
     pair_ref,
+    z_ref,
     matrix_ref,
     adjoint_ref,
     weight_ref,
     cleared_ref,
     rest_ref,
     sems,
+    stay_sem,
 ):
     var_count, rows, pencils = state_ref.shape
     cells = var_count * rows
@@ -331,25 +348,27 @@
     )
     kept, own, about_at, cleared_at = stay_at(rows, count, cells)
 
-    def send(line, slab):
-        for t in range(slices.full):
+    def send(line, rows_at, slab):
+        for t, row_at in enumerate(rows_at):
             start, end = slices.tiles_at(t)
-            message_ref[pl.ds(line * slices.full + t, end - start, stride=height), :] = slab[start:end]
+            message_ref[pl.ds(row_at, end - start, stride=height), :] = slab[start:end]
         for m in range(slices.rest):
             tail = slices.full * slabs + m
             rest_ref[m * lines + line : m * lines + line + 1, :] = slab[tail : tail + 1]
 
     def send_value(functional, v, slab):
-        send(functional * var_count + v, slab)
+        rows_at = [slices.row(functional, t) + v for t in range(slices.full)]
+        send(functional * var_count + v, rows_at, slab)
 
     def send_coefficient(which, slab):
-        send(6 * var_count + which, slab)
+        rows_at = [slices.coefficient_row(which, t) for t in range(slices.full)]
+        send(6 * var_count + which, rows_at, slab)
 
     copies[0].wait()
-    turn(turned_ref, face_ref[...])
+    turn(face_turned_ref, face_ref[...])
 
     def face(i):
-        return slab_at(turned_ref, i, rows, count)
+        return slab_at(face_turned_ref, i, rows, count)
 
     link = face(0)
     margin = jnp.ones_like(link)
@@ -378,9 +397,9 @@
         first[i] = to_first[i] + to_up[i] * first[i + 1]
         last[i] = to_up[i] * last[i + 1]
     copies[1].wait()
-    turn(turned_ref, courant_ref[...])
+    turn(courant_turned_ref, courant_ref[...])
     for i in range(rows):
-        speed = slab_at(turned_ref, i, rows, count)
+        speed = slab_at(courant_turned_ref, i, rows, count)
         start = kept_at(3, i, rows, count)
         stay_ref[start : start + count, :] = speed
         put_slab(pair_ref, i, 2 * rows, count, first[i] * speed)
@@ -448,23 +467,27 @@
     for v in range(var_count):
         here = slice(v * rows, (v + 1) * rows)
         cleared_ref[here, :] = jnp.where(solid, 0.0, state_ref[v])
-    turned = stay_ref.at[cleared_at : cleared_at + cells * count, :]
-    turn(turned, cleared_ref[...])
-    turn(pair_ref, full_dot(table_ref[reduce_at : reduce_at + 16, :cells], cleared_ref[...]))
-    for k in range(2 * var_count):
-        send(k, slab_at(pair_ref, k, 16, count))
+    turn(stay_ref.at[cleared_at : cleared_at + cells * count, :], cleared_ref[...])
+    turn(z_ref, full_dot(table_ref[reduce_at : reduce_at + 16, :cells], cleared_ref[...]))
     for v in range(var_count):
-        low = high = zero
-        for i in range(rows):
+        send_value(Z_UP, v, slab_at(z_ref, v, 16, count))
+        send_value(Z_DOWN, v, slab_at(z_ref, var_count + v, 16, count))
+    staying = pltpu.make_async_copy(stay_ref, stay_hbm, stay_sem.at[0])
+    staying.start()
+    low, high = ([jnp.zeros((count, LANES), jnp.float32)] * var_count for _ in range(2))
+    for i in range(rows):
+        to_low, to_high = weight_ref[i, :count, :], weight_ref[rows + i, :count, :]
+        for v in range(var_count):
             cell = slab_at(stay_ref, cleared_at + v * rows + i, cells, count)
             if i == 0:
                 send_value(ROW_FIRST, v, cell)
             if i == rows - 1:
                 send_value(ROW_LAST, v, cell)
-            low += weight_ref[i, :count, :] * cell
-            high += weight_ref[rows + i, :count, :] * cell
-        send_value(RIGHT_FIRST, v, low)
-        send_value(RIGHT_LAST, v, high)
+            low[v] = low[v] + to_low * cell
+            high[v] = high[v] + to_high * cell
+    for v in range(var_count):
+        send_value(RIGHT_FIRST, v, low[v])
+        send_value(RIGHT_LAST, v, high[v])
 
     block = lane_block(max(slices.groups, 1), slices.width)
     for m in range(slices.rest):
@@ -479,10 +502,46 @@
                 packed = moved if k == 0 else jnp.where(block == k, moved, packed)
             start = (m * slices.per + i) * height + slices.packed_at
             message_ref[start : start + slices.groups, :] = packed
-
-
-def solve_kernel(slices, carry_up, carry_down, message_ref, *refs):
-    *blocks, back_ref, ghost_ref, rest_ref, back_rest_ref = refs
+    staying.wait()
+
+
+def chain_kernel(slices, message_ref, rest_ref, chain_ref):
+    slabs, chunk, full = slices.slabs, slices.chunk, slices.full
+    height, per, width = slices.height, slices.per, slices.width
+    if slices.rest:
+        for p in range(slabs):
+            start = p * height + slices.packed_at
+            packed = message_ref[start : start + slices.groups, :]
+            for k in range(per):
+                rest_ref[pl.ds(p * slices.groups * per + k, slices.groups, stride=per), :] = (
+                    moved_lanes(packed, -k * width)
+                )
+    else:
+        rest_ref[...] = jnp.zeros_like(rest_ref)
+
+    def sent(p, which):
+        start = p * height + slices.coefficient_row(which, 0)
+        slab = message_ref[start : start + full, :]
+        if slices.rest:
+            start = p * slices.groups * per + 6 * slices.var_count + which
+            slab = jnp.concatenate([slab, rest_ref[start : start + 1, :]], axis=0)
+        return slab
+
+    nodes = 2 * slabs
+    margin = sent(0, MARGIN_FIRST)
+    for k in range(nodes):
+        link = sent(k // 2, LINK_UP if k % 2 else LINK_IN)
+        inverse = 1.0 / (margin + link)
+        ratio = link * inverse
+        chain_ref[16 * k : 16 * k + chunk, :] = ratio
+        chain_ref[16 * k + 8 : 16 * k + 8 + chunk, :] = inverse
+        if k < nodes - 1:
+            following = sent((k + 1) // 2, MARGIN_FIRST if k % 2 else MARGIN_LAST)
+            margin = following + margin * ratio
+
+
+def solve_kernel(slices, carry_up, carry_down, message_ref, rest_ref, chain_ref, *refs):
+    *blocks, back_ref, ghost_ref, back_rest_ref = refs
     slabs, var_count, chunk, full = slices.slabs, slices.var_count, slices.chunk, slices.full
     height, per, width = slices.height, slices.per, slices.width
     me = lax.axis_index("pipe")
@@ -495,7 +554,6 @@
         return jnp.concatenate([meta(p, k) for p in range(slabs)], axis=1).astype(jnp.int32)
 
     values = ghost_values(slices, blocks, meta_all(OWNER), meta_all(IMAGE))
-    ghost_lines = 6 * var_count + 2
     ghosts = LANES
     place = lax.broadcasted_iota(jnp.int32, (chunk * LANES, ghosts), 0)
     slot, lane = place // LANES, place % LANES
@@ -504,6 +562,7 @@
         (me + slot * slabs) * LANES + lane,
         (full * slabs + me // per) * LANES + (me % per) * width + lane,
     )
+    none = jnp.zeros((8 - var_count, ghosts), jnp.float32)
     for p in range(slabs):
         row = meta(p, ROW)
         weights = (
@@ -514,95 +573,79 @@
             meta(p, WEIGHT_FIRST),
             meta(p, WEIGHT_LAST),
         )
-        here = jnp.concatenate([value[:, tile(p)] for value in values], axis=0)
-        shares = jnp.concatenate(
-            [here * weight for weight in weights] + [jnp.zeros((2, ghosts), jnp.float32)], axis=0
-        )
+        here = jnp.concatenate([value[:, tile(p)] for value in values] + [none], axis=0)
+        shares = jnp.concatenate([here * weight for weight in weights], axis=0)
         spots = jnp.where(pencil_at == meta(p, PENCIL).astype(jnp.int32), 1.0, 0.0)
         share = exact_dot(shares, spots.astype(jnp.bfloat16), ((1,), (1,)))
         for t in range(chunk):
-            start = (p * chunk + t) * ghost_lines
-            ghost_ref[start : start + ghost_lines, :] = share[:, tile(t)]
-        if slices.rest:
-            start = p * height + slices.packed_at
-            packed = message_ref[start : start + slices.groups, :]
-            for k in range(per):
-                rest_ref[pl.ds(p * slices.groups * per + k, slices.groups, stride=per), :] = (
-                    moved_lanes(packed, -k * width)
-                )
-
-    def sent(p, line):
-        start = p * height + line * full
-        slab = message_ref[start : start + full, :]
-        if slices.rest:
-            start = p * slices.groups * per + line
-            slab = jnp.concatenate([slab, rest_ref[start : start + 1, :]], axis=0)
-        return slab
-
-    def value(p, functional, v):
-        line = functional * var_count + v
-        start = p * chunk * ghost_lines + line
-        return sent(p, line) + ghost_ref[pl.ds(start, chunk, stride=ghost_lines), :]
-
-    def give(p, functional, v, slab):
-        line = functional * var_count + v
-        start = p * slices.back_height + line * full
-        back_ref[start : start + full, :] = slab[:full]
-        if slices.rest:
-            start = p * slices.back_groups * per + line
-            back_rest_ref[start : start + 1, :] = slab[full:]
-
-    coefficients = [
-        [sent(p, 6 * var_count + k) for k in range(COEFFICIENTS)] for p in range(slabs)
-    ]
+            start = (p * chunk + t) * 48
+            ghost_ref[start : start + 48, :] = share[:, tile(t)]
+
     nodes = 2 * slabs
-    ratio, scale = [], []
-    margin = coefficients[0][MARGIN_FIRST]
-    for k in range(nodes):
-        link = coefficients[k // 2][LINK_UP if k % 2 else LINK_IN]
-        inverse = 1.0 / (margin + link)
-        ratio.append(link * inverse)
-        scale.append(inverse)
-        if k < nodes - 1:
-            following = coefficients[(k + 1) // 2][MARGIN_FIRST if k % 2 else MARGIN_LAST]
-            margin = following + margin * ratio[k]
-
-    zero = jnp.zeros((chunk, LANES), jnp.float32)
-    for v in range(var_count):
-        lo, hi = [zero] * slabs, [zero] * slabs
-        below, above = [zero] * slabs, [zero] * slabs
+    zero = jnp.zeros((var_count, LANES), jnp.float32)
+    for t in range(chunk):
+
+        def value(p, functional):
+            if t < full:
+                start = p * height + slices.row(functional, t)
+                sent = message_ref[start : start + var_count, :]
+            else:
+                start = p * slices.groups * per + functional * var_count
+                sent = rest_ref[start : start + var_count, :]
+            start = (p * chunk + t) * 48 + functional * 8
+            return sent + ghost_ref[start : start + var_count, :]
+
+        def coefficient(p, which):
+            if t < full:
+                start = p * height + slices.coefficient_row(which, t)
+                return message_ref[start : start + 1, :]
+            start = p * slices.groups * per + 6 * var_count + which
+            return rest_ref[start : start + 1, :]
+
+        def give(p, functional, block):
+            if t < full:
+                start = p * slices.back_height + slices.row(functional, t)
+                back_ref[start : start + var_count, :] = block
+            else:
+                start = p * slices.back_groups * per + functional * var_count
+                back_rest_ref[start : start + var_count, :] = block
+
+        def ratio(k):
+            return chain_ref[16 * k + t : 16 * k + t + 1, :]
+
+        def scale(k):
+            return chain_ref[16 * k + 8 + t : 16 * k + 9 + t, :]
+
+        lo, hi, below, above = ([zero] * slabs for _ in range(4))
         for p in range(1, slabs):
-            lo[p] = value(p - 1, Z_UP, v) + float(carry_up[p]) * lo[p - 1]
-            below[p] = value(p - 1, ROW_LAST, v)
+            lo[p] = value(p - 1, Z_UP) + float(carry_up[p]) * lo[p - 1]
+            below[p] = value(p - 1, ROW_LAST)
         for p in range(slabs - 2, -1, -1):
-            hi[p] = value(p + 1, Z_DOWN, v) + float(carry_down[p]) * hi[p + 1]
-            above[p] = value(p + 1, ROW_FIRST, v)
+            hi[p] = value(p + 1, Z_DOWN) + float(carry_down[p]) * hi[p + 1]
+            above[p] = value(p + 1, ROW_FIRST)
         right = []
         for p in range(slabs):
-            coefficient = coefficients[p]
             right.append(
-                value(p, RIGHT_FIRST, v)
-                - coefficient[FIRST_LO] * lo[p]
-                - coefficient[FIRST_HI] * hi[p]
-                - coefficient[FIRST_EDGE] * below[p]
+                value(p, RIGHT_FIRST)
+                - coefficient(p, FIRST_LO) * lo[p]
+                - coefficient(p, FIRST_HI) * hi[p]
+                - coefficient(p, FIRST_EDGE) * below[p]
             )
             right.append(
-                value(p, RIGHT_LAST, v)
-                - coefficient[LAST_LO] * lo[p]
-                - coefficient[LAST_HI] * hi[p]
-                - coefficient[LAST_EDGE] * above[p]
+                value(p, RIGHT_LAST)
+                - coefficient(p, LAST_LO) * lo[p]
+                - coefficient(p, LAST_HI) * hi[p]
+                - coefficient(p, LAST_EDGE) * above[p]
             )
-            give(p, 2, v, lo[p])
-            give(p, 3, v, hi[p])
-            give(p, 4, v, below[p])
-            give(p, 5, v, above[p])
+            for functional, block in enumerate((lo[p], hi[p], below[p], above[p])):
+                give(p, 2 + functional, block)
         for k in range(1, nodes):
-            right[k] = right[k] + ratio[k - 1] * right[k - 1]
-        x = right[nodes - 1] * scale[nodes - 1]
-        give(slabs - 1, 1, v, x)
+            right[k] = right[k] + ratio(k - 1) * right[k - 1]
+        x = right[nodes - 1] * scale(nodes - 1)
+        give(slabs - 1, 1, x)
         for k in range(nodes - 2, -1, -1):
-            x = right[k] * scale[k] + ratio[k] * x
-            give(k // 2, k % 2, v, x)
+            x = right[k] * scale(k) + ratio(k) * x
+            give(k // 2, k % 2, x)
     if slices.rest:
         groups = slices.back_groups
         block = lane_block(groups, width)
@@ -641,12 +684,12 @@
 
 
 def fill_kernel(slices, shape, ready_ref, *refs):
-    *blocks, filled_ref = refs
+    *blocks, done_ref, filled_ref = refs
     var_count, rows, pencils = shape
     cells = var_count * rows
     count = pencils // LANES
     _, own_at, about_at, _ = stay_at(rows, count, cells)
-    _, kept_start, end = ready_at(rows, count, cells)
+    cells_at, kept_start, _ = ready_at(rows, count, cells)
 
     def known(k):
         start = kept_start + about_at + k
@@ -661,31 +704,62 @@
     spots = marks((pencils, ghosts), 0, known(PENCIL))
     added = exact_dot(both, spots, ((1,), (1,)))
     for t in range(count):
-        for k in range(2):
-            here = slice((k * count + t) * cells, (k * count + t + 1) * cells)
-            filled_ref[here, :] = ready_ref[here, :] + added[k * cells : (k + 1) * cells, tile(t)]
-    filled_ref[kept_start:end, :] = ready_ref[kept_start:end, :]
+        here = slice(t * cells, (t + 1) * cells)
+        there = slice(cells_at + t * cells, cells_at + (t + 1) * cells)
+        done_ref[here, :] = ready_ref[here, :] + added[:cells, tile(t)]
+        filled_ref[here, :] = ready_ref[there, :] + added[cells:, tile(t)]
+    x_at, response_at, profile_at, _ = done_at(rows, count, cells)
+
+    def kept(which, i):
+        start = kept_start + kept_at(which, i, rows, count)
+        return ready_ref[start : start + count, :]
+
+    def profile(k):
+        start = kept_start + own_at - 40 + k
+        return ready_ref[start : start + 1, :]
+
+    def put(at, i, height, value):
+        done_ref[pl.ds(at + i, count, stride=height), :] = value
+
+    swept = []
+    for i in range(1, rows - 1):
+        speed = kept(3, i)
+        here = [-speed * profile(i), -speed * profile(rows + i)]
+        for v in range(var_count):
+            row = v * rows + i
+            own_slab = slab_at(done_ref, row, cells, count)
+            here.append(slab_at(filled_ref, row, cells, count) - speed * own_slab)
+        if swept:
+            ratio = kept(0, i - 1)
+            here = [x + ratio * y for x, y in zip(here, swept[-1])]
+        swept.append(here)
+    zero = jnp.zeros((count, LANES), jnp.float32)
+    one = jnp.ones((count, LANES), jnp.float32)
+    x = [zero] * (2 + var_count)
+    first, last = zero, one
+    for i in range(rows - 1, -1, -1):
+        if 0 < i < rows - 1:
+            ratio, inverse = kept(0, i), kept(2, i)
+            first, last = kept(1, i) + ratio * first, ratio * last
+            x = [inverse * y + ratio * z for y, z in zip(swept[i - 1], x)]
+        if i == 0:
+            first, last, x = one, zero, [zero] * (2 + var_count)
+        for k, value in enumerate([first, last] + x[:2]):
+            put(response_at + k * rows * count, i, rows, value)
+        for v in range(var_count):
+            put(x_at, v * rows + i, cells, x[2 + v])
+    done_ref[profile_at : profile_at + 40, :] = ready_ref[
+        kept_start + own_at - 40 : kept_start + own_at, :
+    ]
 
 
 def finish_kernel(
-    slices,
-    back_ref,
-    ready_ref,
-    derivative_hbm,
-    segment_hbm,
-    derivative_ref,
-    segment_ref,
-    derivative_turned_ref,
-    segment_turned_ref,
-    tail_ref,
-    sems,
+    slices, back_ref, done_ref, derivative_hbm, segment_hbm, derivative_ref, segment_ref, tail_ref, sems
 ):
     var_count, rows, pencils = segment_ref.shape
     count = pencils // LANES
     cells = var_count * rows
-    variables = range(var_count)
-    filled_start, kept_start, _ = ready_at(rows, count, cells)
-    profile_at = kept_start + stay_at(rows, count, cells)[0] - 40
+    x_at, response_at, profile_at, _ = done_at(rows, count, cells)
     back_height, groups, per = slices.back_height, slices.back_groups, slices.per
     block = lane_block(max(groups, 1), slices.width)
     for m in range(slices.rest):
@@ -699,71 +773,52 @@
                 joined = moved if i == 0 else jnp.where(block == i, moved, joined)
             tail_ref[pl.ds(m * groups * per + k, groups, stride=per), :] = joined
 
-    def got(functional, v):
-        line = functional * var_count + v
-        parts = []
-        for t in range(slices.full):
-            start, end = slices.tiles_at(t)
-            parts.append(
-                back_ref[pl.ds(line * slices.full + t, end - start, stride=back_height), :]
+    def got(functional, v, t):
+        step, j = t // slices.slabs, t % slices.slabs
+        if step < slices.full:
+            start = j * back_height + slices.row(functional, step) + v
+            return back_ref[start : start + 1, :]
+        start = j * groups * per + functional * var_count + v
+        return tail_ref[start : start + 1, :]
+
+    lo_profile = done_ref[profile_at : profile_at + rows, :]
+    hi_profile = done_ref[profile_at + rows : profile_at + 2 * rows, :]
+    row_at = lax.broadcasted_iota(jnp.int32, (rows, LANES), 0)
+    edges = profile_at + 2 * rows
+    lo_edge = jnp.where(row_at == 0, done_ref[edges : edges + 1, :], 0.0)
+    hi_edge = jnp.where(row_at == rows - 1, done_ref[edges + 1 : edges + 2, :], 0.0)
+
+    def response(k, t):
+        start = response_at + (k * count + t) * rows
+        return done_ref[start : start + rows, :]
+
+    copies = []
+    for v in range(var_count):
+        for t in range(count):
+            start = t * cells + v * rows
+            lo, hi = got(2, v, t), got(3, v, t)
+            derivative_ref[v, :, tile(t)] = (
+                done_ref[start : start + rows, :]
+                + (lo_profile * lo + hi_profile * hi)
+                + (lo_edge * got(4, v, t) + hi_edge * got(5, v, t))
             )
-        for m in range(slices.rest):
-            start = m * groups * per + line
-            parts.append(tail_ref[start : start + 1, :])
-        return jnp.concatenate(parts, axis=0)
-
-    def profile(k):
-        return ready_ref[profile_at + k : profile_at + k + 1, :]
-
-    def kept(which, i):
-        start = kept_start + kept_at(which, i, rows, count)
-        return ready_ref[start : start + count, :]
-
-    def give(turned, straight, hbm, which):
-        copies = []
-        for v in variables:
-            for t in range(count):
-                start = t * cells + v * rows
-                straight[v, :, tile(t)] = turned[start : start + rows, :]
+            segment_ref[v, :, tile(t)] = (
+                done_ref[x_at + start : x_at + start + rows, :]
+                + (response(0, t) * got(0, v, t) + response(1, t) * got(1, v, t))
+                + (response(2, t) * lo + response(3, t) * hi)
+            )
+        for which, (ref, hbm) in enumerate(
+            ((derivative_ref, derivative_hbm), (segment_ref, segment_hbm))
+        ):
             copies.append(
-                pltpu.make_async_copy(straight.at[v], hbm.at[v], sems.at[which * var_count + v])
+                pltpu.make_async_copy(ref.at[v], hbm.at[v], sems.at[which * var_count + v])
             )
             copies[-1].start()
-        return copies
-
-    lo, hi = [got(2, v) for v in variables], [got(3, v) for v in variables]
-    swept = [[None] * rows for _ in variables]
-    for i in range(rows):
-        for v in variables:
-            row = v * rows + i
-            far = profile(i) * lo[v] + profile(rows + i) * hi[v]
-            if i == 0:
-                far += profile(2 * rows) * got(4, v)
-            if i == rows - 1:
-                far += profile(2 * rows + 1) * got(5, v)
-            value = slab_at(ready_ref, row, cells, count) + far
-            put_slab(derivative_turned_ref, row, cells, count, value)
-            if 0 < i < rows - 1:
-                right = slab_at(ready_ref, filled_start + row, cells, count) - kept(3, i) * value
-                if i > 1:
-                    right += kept(0, i - 1) * swept[v][i - 1]
-                swept[v][i] = right
-    copies = give(derivative_turned_ref, derivative_ref, derivative_hbm, 0)
-    first, last = [got(0, v) for v in variables], [got(1, v) for v in variables]
-    x = list(last)
-    for v in variables:
-        put_slab(segment_turned_ref, v * rows, cells, count, first[v])
-        put_slab(segment_turned_ref, (v + 1) * rows - 1, cells, count, last[v])
-    for i in range(rows - 2, 0, -1):
-        for v in variables:
-            x[v] = kept(2, i) * swept[v][i] + kept(1, i) * first[v] + kept(0, i) * x[v]
-            put_slab(segment_turned_ref, v * rows + i, cells, count, x[v])
-    copies += give(segment_turned_ref, segment_ref, segment_hbm, 1)
     for copy in copies:
         copy.wait()
 
 
-def call(kernel, outs, scratch, sems, args, near=(), far_out=False, limit=62):
+def call(kernel, outs, scratch, sems, args, near=(), far_out=(), limit=62):
     whole = pl.BlockSpec(memory_space=pltpu.VMEM)
     far = pl.BlockSpec(memory_space=pltpu.HBM)
     buffers = [
@@ -775,7 +830,7 @@
         kernel,
         out_shape=[jax.ShapeDtypeStruct(shape, jnp.float32) for shape in outs],
         in_specs=[whole if k in near else far for k in range(len(args))],
-        out_specs=[far if far_out else whole] * len(outs),
+        out_specs=[far if k in far_out else whole for k in range(len(outs))],
         scratch_shapes=buffers,
         compiler_params=pltpu.CompilerParams(vmem_limit_bytes=limit * 2**20),
     )(*args)
@@ -827,16 +882,20 @@
         [(slabs * slices.height, LANES), (stay, LANES)],
         buffers
         + [
+            (stay, LANES),
+            (rows * count, LANES),
             (rows * count, LANES),
             (2 * rows * count, LANES),
+            (16 * count, LANES),
             (2 * rows, pencils),
             (40 * count, LANES),
             (2 * rows, -(-count // 8) * 8, LANES),
             (cells, pencils),
             (max(slices.rest, 1) * max(slices.groups, 1) * slices.per, LANES),
         ],
-        [len(arguments)],
+        [len(arguments), 1],
         arguments,
+        far_out=(1,),
     )
     message = exchange(message, "pipe")
     (ready,) = call(
@@ -856,25 +915,32 @@
         for u in range(1, cross)
     ]
 
-    spare = slabs * slices.per
+    rest, chain = call(
+        functools.partial(chain_kernel, slices),
+        [(slabs * max(slices.groups, 1) * slices.per, LANES), (2 * slabs * 16, LANES)],
+        [],
+        [],
+        (message,),
+        near=(0,),
+        limit=24,
+    )
     (back,) = call(
         functools.partial(solve_kernel, slices, carry_up, carry_down),
         [(slabs * slices.back_height, LANES)],
         [
-            (slabs * slices.chunk * (6 * var_count + 2), LANES),
-            (max(slices.groups, 1) * spare, LANES),
-            (max(slices.back_groups, 1) * spare, LANES),
+            (slabs * slices.chunk * 48, LANES),
+            (slabs * max(slices.back_groups, 1) * slices.per, LANES),
         ],
         [],
-        (message, *blocks),
-        near=range(1 + cross),
+        (message, rest, chain, *blocks),
+        near=range(3 + cross),
         limit=24,
     )
     back = exchange(back, "pipe")
-    (ready,) = call(
+    (done,) = call(
         functools.partial(fill_kernel, slices, state.shape),
-        [ready.shape],
-        [],
+        [(done_at(rows, count, cells)[3], LANES)],
+        [turned],
         [],
         (ready, *blocks),
         near=range(1 + cross),
@@ -887,14 +953,12 @@
             [
                 state.shape,
                 state.shape,
-                turned,
-                turned,
                 (max(slices.rest, 1) * max(slices.back_groups, 1) * slices.per, LANES),
             ],
             [2 * var_count],
-            (back, ready),
+            (back, done),
             near=range(2),
-            far_out=True,
+            far_out=(0, 1),
             limit=48,
         )
     )

time: 48.6 us -> 48.1 us (0.990)
  waiting for transfers between devices: 10.3 us -> 9.15 us
  Pallas kernels: 11.3 us -> 11.9 us
    all_to_all x1, waiting for transfers between devices: 7.04 us -> 6.12 us  [exchange(): return lax.all_to_all(message, axes, 0, 0, tiled=True)]
    pallas_call x6 -> x7, Pallas kernels: 11.3 us -> 11.9 us  [call(): pl.pallas_call(kernel, out_shape=[jax.ShapeDtypeStruct(shape, jnp.float32...]
  transfers between devices with their start and end apart: 4 -> 4, of which waited for: 3 -> 3; matrix products, arithmetic and copies ran while one was open for 0% -> 0% of each run, Pallas kernels for 4% -> 6%
where the time goes in v3:
time: 48.1 us; the launch traced here: 47.8 us
  blocking collectives  20.7 us (43%)
  Pallas kernels  11.9 us (25%)
  waiting for transfers between devices  9.15 us (19%)
  starting transfers between devices  5.31 us (11%)
  between operations  0.69 us (1%)
    all_to_all x1, blocking collectives, exchange(): return lax.all_to_all(message, axes, 0, 0, tiled=True)  20.7 us
    pallas_call x7, Pallas kernels, call(): pl.pallas_call(kernel, out_shape=[jax.ShapeDtypeStruct(shape, jnp.float32...  11.9 us
    all_to_all x1, waiting for transfers between devices, exchange(): return lax.all_to_all(message, axes, 0, 0, tiled=True)  6.12 us
    all_to_all x1, starting transfers between devices, exchange(): return lax.all_to_all(message, axes, 0, 0, tiled=True)  3.6 us
    ppermute x3, waiting for transfers between devices, local(): lax.ppermute(image_values, 'cross', [(i, (i + u) % cross) for i in range(...  3.04 us
    ppermute x3, starting transfers between devices, local(): lax.ppermute(image_values, 'cross', [(i, (i + u) % cross) for i in range(...  1.71 us
  transfers between devices with their start and end apart: 4, of which 3 were waited for; matrix products, arithmetic and copies ran while one was open for 0% of the time, Pallas kernels for 6%

profile of v3, /device:TPU:0, one launch (start us, length us, event | category | flops | bytes accessed | tf_op | source)
XLA Modules:
  0.0 47.8 jit_solution(14285971119542246049)
XLA Ops:
  0.6 5.8 %shard_map.113 = (f32[896,128]{1,0:T(8,128)}, f32[3104,128]{1,0:T(8,128)}) custom-call(f32[16,2304]{1,0:T(8,128)} %face_hbm.1, f32[16,2304]{1,0:T(8,128)} %courant_hbm.1, f32[8,192,128]{2,1,0:T(8,128)} %constant.2.clone.tables_hbm, s32[128]{0:T(128)} %cell_hbm.1, s32[128]{0:T(128)} %owner_hbm.1, s32[128]{0:T(128)} %image_hbm.1, s32[16,2304]{1,0:T(8,128)} %mask_hbm.1, ...), custom_call_target="tpu_custom_call" | custom-call | tf_op jit(solution)/shard_map/pallas_call | solution.py:829
  6.5 0.0 copy-start
  6.5 20.7 %all_to_all.22 = f32[8,112,128]{2,1,0:T(8,128)S(1)} all-to-all(f32[8,112,128]{2,1,0:T(8,128)} %bitcast.8), channel_id=1, replica_groups=mesh['pipe'=8,'cross'=4] {'pipe'}, dimensions={0} | all-to-all | bytes 917504 | tf_op jit(solution)/shard_map/all_to_all | solution.py:840
  27.2 0.0 collective-permute-start.2
  27.2 1.6 %collective-permute-start.1 = (f32[80,128]{1,0:T(8,128)S(1)}, f32[80,128]{1,0:T(8,128)S(1)}, u32[]{:S(2)}, u32[]{:S(2)}) collective-permute-start(f32[80,128]{1,0:T(8,128)S(1)} %shard_map.115.refs_0_), channel_id=1, source_target_pairs={{0,2},{1,3},{2,0},{3,1},{4,6},{5,7},{6,4},{7,5},{8,10},{9,11},{10,... | collective-permute-start | bytes 122888 | tf_op jit(solution)/shard_map/ppermute | solution.py:914
  28.7 0.2 collective-permute-start
  28.9 0.2 shard_map.114
  29.1 0.0 collective-permute-done.2.refs_3_
  29.1 2.4 %collective-permute-done.1.refs_2_ = f32[80,128]{1,0:T(8,128)S(1)} collective-permute-done((f32[80,128]{1,0:T(8,128)S(1)}, f32[80,128]{1,0:T(8,128)S(1)}, u32[]{:S(2)}, u32[]{:S(2)}) %collective-permute-start.1) | collective-permute-done | bytes 40992 | tf_op jit(solution)/shard_map/ppermute | solution.py:914
  31.5 0.6 %collective-permute-done.refs_1_ = f32[80,128]{1,0:T(8,128)S(1)} collective-permute-done((f32[80,128]{1,0:T(8,128)S(1)}, f32[80,128]{1,0:T(8,128)S(1)}, u32[]{:S(2)}, u32[]{:S(2)}) %collective-permute-start) | collective-permute-done | bytes 40992 | tf_op jit(solution)/shard_map/ppermute | solution.py:914
  32.2 1.7 %shard_map.116 = f32[576,128]{1,0:T(8,128)} custom-call(f32[896,128]{1,0:T(8,128)S(1)} %bitcast.6, f32[320,128]{1,0:T(8,128)S(1)} %get-tuple-element.7.rest_ref, f32[256,128]{1,0:T(8,128)S(1)} %get-tuple-element.8.chain_ref, f32[80,128]{1,0:T(8,128)S(1)} %shard_map.115.refs_0_, f32[80,128]{1,0:T(8,128)S(1)} %collective-permute-done.refs_1_, ...), custom_call_target="tpu_custom_call" | custom-call | tf_op jit(solution)/shard_map/pallas_call | solution.py:829
  33.8 3.6 %all-to-all-start.1 = ((f32[8,72,128]{2,1,0:T(8,128)}), f32[8,72,128]{2,1,0:T(8,128)S(1)}, u32[]{:S(2)}, u32[]{:S(2)}) async-start(f32[8,72,128]{2,1,0:T(8,128)} %bitcast.2), calls=%async_computation.1 | async-start | bytes 589824 | tf_op jit(solution)/shard_map/all_to_all | solution.py:840
  37.4 0.0 copy-done
  37.4 0.7 %shard_map.117.ready_ref = f32[4544,128]{1,0:T(8,128)S(1)} custom-call(f32[3104,128]{1,0:T(8,128)S(1)} %copy-done), custom_call_target="tpu_custom_call" | custom-call | tf_op jit(solution)/shard_map/pallas_call | solution.py:829
  38.2 2.1 %shard_map.118.done_ref = f32[4072,128]{1,0:T(8,128)S(1)} custom-call(f32[4544,128]{1,0:T(8,128)S(1)} %shard_map.117.ready_ref, f32[80,128]{1,0:T(8,128)S(1)} %shard_map.115.refs_0_, f32[80,128]{1,0:T(8,128)S(1)} %collective-permute-done.refs_1_, f32[80,128]{1,0:T(8,128)S(1)} %collective-permute-done.1.refs_2_, f32[80,128]{1,0:T(8,128)S(1)} %collective-permute-done.2.refs_3_), custom_call_target="tpu_custom_call" | custom-call | tf_op jit(solution)/shard_map/pallas_call | solution.py:829
  40.3 6.1 %all-to-all-done.1 = f32[8,72,128]{2,1,0:T(8,128)S(1)} async-done(((f32[8,72,128]{2,1,0:T(8,128)}), f32[8,72,128]{2,1,0:T(8,128)S(1)}, u32[]{:S(2)}, u32[]{:S(2)}) %all-to-all-start.1) | async-done | bytes 294944 | tf_op jit(solution)/shard_map/all_to_all | solution.py:840
  46.4 1.3 %shard_map.119 = (f32[5,16,2304]{2,1,0:T(8,128)}, f32[5,16,2304]{2,1,0:T(8,128)}) custom-call(f32[576,128]{1,0:T(8,128)S(1)} %bitcast.7, f32[4072,128]{1,0:T(8,128)S(1)} %shard_map.118.done_ref), custom_call_target="tpu_custom_call" | custom-call | tf_op jit(solution)/shard_map/pallas_call | solution.py:829
  (1 shorter events, 0.0 us)
Async XLA Ops:
  6.5 31.0 %copy-start = (f32[3104,128]{1,0:T(8,128)S(1)}, f32[3104,128]{1,0:T(8,128)}, u32[]{:S(2)}) copy-start(f32[3104,128]{1,0:T(8,128)} %get-tuple-element.9.stay_ref) | copy-start | bytes 4767748
  27.2 1.9 %collective-permute-start.2 = (f32[80,128]{1,0:T(8,128)S(1)}, f32[80,128]{1,0:T(8,128)S(1)}, u32[]{:S(2)}, u32[]{:S(2)}) collective-permute-start(f32[80,128]{1,0:T(8,128)S(1)} %shard_map.115.refs_0_), channel_id=1, source_target_pairs={{0,3},{1,0},{2,1},{3,2},{4,7},{5,4},{6,5},{7,6},{8,11},{9,8},{10,9... | collective-permute-start | bytes 122888 | tf_op jit(solution)/shard_map/ppermute | solution.py:914
  27.2 4.3 %collective-permute-start.1 = (f32[80,128]{1,0:T(8,128)S(1)}, f32[80,128]{1,0:T(8,128)S(1)}, u32[]{:S(2)}, u32[]{:S(2)}) collective-permute-start(f32[80,128]{1,0:T(8,128)S(1)} %shard_map.115.refs_0_), channel_id=1, source_target_pairs={{0,2},{1,3},{2,0},{3,1},{4,6},{5,7},{6,4},{7,5},{8,10},{9,11},{10,... | collective-permute-start | bytes 122888 | tf_op jit(solution)/shard_map/ppermute | solution.py:914
  28.7 3.4 %collective-permute-start = (f32[80,128]{1,0:T(8,128)S(1)}, f32[80,128]{1,0:T(8,128)S(1)}, u32[]{:S(2)}, u32[]{:S(2)}) collective-permute-start(f32[80,128]{1,0:T(8,128)S(1)} %shard_map.115.refs_0_), channel_id=1, source_target_pairs={{0,1},{1,2},{2,3},{3,0},{4,5},{5,6},{6,7},{7,4},{8,9},{9,10},{10,1... | collective-permute-start | bytes 122888 | tf_op jit(solution)/shard_map/ppermute | solution.py:914
  33.8 12.6 %all-to-all-start.1 = ((f32[8,72,128]{2,1,0:T(8,128)}), f32[8,72,128]{2,1,0:T(8,128)S(1)}, u32[]{:S(2)}, u32[]{:S(2)}) async-start(f32[8,72,128]{2,1,0:T(8,128)} %bitcast.2), calls=%async_computation.1 | async-start | bytes 589824 | tf_op jit(solution)/shard_map/all_to_all | solution.py:840

commit v4 on v3

--- a/solution.py
+++ b/solution.py
@@ -153,11 +153,11 @@
     return cells * count, kept, kept + stay_at(rows, count, cells)[3]
 
 
-def done_at(rows, count, cells):
+def done_at(rows, count, cells, var_count):
     x = cells * count
     response = 2 * x
     profile = response + 4 * rows * count
-    return x, response, profile, profile + 40
+    return x, response, profile, profile + 40, profile + 40 + 2 * var_count * count
 
 
 def fetch(sources, targets, sems):
@@ -181,7 +181,7 @@
         self.per = slabs // rest if shared else 1
         self.width = LANES // self.per
         self.chunk = self.full + (1 if shared else 0)
-        self.lines, self.back_lines = 6 * var_count + COEFFICIENTS, 6 * var_count
+        self.lines, self.back_lines = 6 * var_count + COEFFICIENTS, 4 * var_count
         self.groups, self.back_groups = (self.group_count(n) for n in (self.lines, self.back_lines))
         self.meta_at = self.lines * self.full
         self.packed_at = self.meta_at + 8
@@ -220,10 +220,10 @@
     row_at = lax.broadcasted_iota(jnp.int32, (rows, images), 0)
     lower, upper = row_at == row, row_at == row + 1
     total = [jnp.zeros((rows, images), jnp.float32) for _ in range(var_count)]
+    pieces = jnp.concatenate(split(x, 2), axis=0)
     for corner, shift in enumerate((0, 1, LINE, LINE + 1)):
-        moved = x if shift == 0 else pltpu.roll(x, pencils - shift, 1)
-        pieces = jnp.concatenate(split(moved, 2), axis=0)
-        found = jnp.dot(pieces, pick, preferred_element_type=jnp.float32)
+        moved = pieces if shift == 0 else pltpu.roll(pieces, pencils - shift, 1)
+        found = jnp.dot(moved, pick, preferred_element_type=jnp.float32)
         found = found[: var_count * rows] + found[var_count * rows :]
         weight = jnp.where(lower, weight_ref[corner : corner + 1], 0.0) + jnp.where(
             upper, weight_ref[corner + 4 : corner + 5], 0.0
@@ -287,6 +287,8 @@
     state_hbm,
     message_ref,
     stay_hbm,
+    up_ref,
+    down_ref,
     face_ref,
     courant_ref,
     table_ref,
@@ -298,6 +300,7 @@
     corner_ref,
     state_ref,
     stay_ref,
+    turned_ref,
     face_turned_ref,
     courant_turned_ref,
     pair_ref,
@@ -346,7 +349,7 @@
         ),
         sems,
     )
-    kept, own, about_at, cleared_at = stay_at(rows, count, cells)
+    kept, own, about_at, _ = stay_at(rows, count, cells)
 
     def send(line, rows_at, slab):
         for t, row_at in enumerate(rows_at):
@@ -451,6 +454,12 @@
         start = j * height + slices.meta_at
         message_ref[start : start + 8, :] = about
     stay_ref[about_at : about_at + 8, :] = about
+    edge = var_count * count
+    for ref in (up_ref, down_ref):
+        ref[edge : ref.shape[0] - 8, :] = jnp.zeros((ref.shape[0] - 8 - edge, LANES), jnp.float32)
+        ref[ref.shape[0] - 8 :, :] = about
+    staying = pltpu.make_async_copy(stay_ref, stay_hbm, stay_sem.at[0])
+    staying.start()
     for copy in copies[6:]:
         copy.wait()
     values = image_lines(
@@ -467,22 +476,22 @@
     for v in range(var_count):
         here = slice(v * rows, (v + 1) * rows)
         cleared_ref[here, :] = jnp.where(solid, 0.0, state_ref[v])
-    turn(stay_ref.at[cleared_at : cleared_at + cells * count, :], cleared_ref[...])
+    turn(turned_ref, cleared_ref[...])
     turn(z_ref, full_dot(table_ref[reduce_at : reduce_at + 16, :cells], cleared_ref[...]))
     for v in range(var_count):
         send_value(Z_UP, v, slab_at(z_ref, v, 16, count))
         send_value(Z_DOWN, v, slab_at(z_ref, var_count + v, 16, count))
-    staying = pltpu.make_async_copy(stay_ref, stay_hbm, stay_sem.at[0])
-    staying.start()
     low, high = ([jnp.zeros((count, LANES), jnp.float32)] * var_count for _ in range(2))
     for i in range(rows):
         to_low, to_high = weight_ref[i, :count, :], weight_ref[rows + i, :count, :]
         for v in range(var_count):
-            cell = slab_at(stay_ref, cleared_at + v * rows + i, cells, count)
+            cell = slab_at(turned_ref, v * rows + i, cells, count)
             if i == 0:
                 send_value(ROW_FIRST, v, cell)
+                down_ref[v * count : (v + 1) * count, :] = cell
             if i == rows - 1:
                 send_value(ROW_LAST, v, cell)
+                up_ref[v * count : (v + 1) * count, :] = cell
             low[v] = low[v] + to_low * cell
             high[v] = high[v] + to_high * cell
     for v in range(var_count):
@@ -637,8 +646,8 @@
                 - coefficient(p, LAST_HI) * hi[p]
                 - coefficient(p, LAST_EDGE) * above[p]
             )
-            for functional, block in enumerate((lo[p], hi[p], below[p], above[p])):
-                give(p, 2 + functional, block)
+            give(p, 2, lo[p])
+            give(p, 3, hi[p])
         for k in range(1, nodes):
             right[k] = right[k] + ratio(k - 1) * right[k - 1]
         x = right[nodes - 1] * scale(nodes - 1)
@@ -665,50 +674,64 @@
         values_ref[p * size : (p + 1) * size, :] = message_ref[start : start + size, :]
 
 
-def own_kernel(shape, stay_ref, ready_ref):
-    var_count, rows, pencils = shape
+def own_kernel(stay_ref, mask_ref, state_ref, ready_ref, cleared_ref):
+    var_count, rows, pencils = state_ref.shape
     cells = var_count * rows
     count = pencils // LANES
-    _, own_at, _, cleared_at = stay_at(rows, count, cells)
+    own_at = stay_at(rows, count, cells)[1]
     cells_at, kept_start, end = ready_at(rows, count, cells)
-    cleared = [
-        stay_ref[cleared_at + t * cells : cleared_at + (t + 1) * cells, :] for t in range(count)
-    ]
-    for t in range(count):
-        ready_ref[cells_at + t * cells : cells_at + (t + 1) * cells, :] = cleared[t]
+    solid = mask_ref[...] == 1
+    for v in range(var_count):
+        cleared_ref[v * rows : (v + 1) * rows, :] = jnp.where(solid, 0.0, state_ref[v])
+    turn(ready_ref.at[cells_at:kept_start, :], cleared_ref[...])
     turn(
-        ready_ref.at[: cells * count, :],
-        full_dot(stay_ref[own_at : own_at + cells, :cells], jnp.concatenate(cleared, axis=1)),
-    )
-    ready_ref[kept_start:end, :] = stay_ref[:cleared_at, :]
-
-
-def fill_kernel(slices, shape, ready_ref, *refs):
-    *blocks, done_ref, filled_ref = refs
+        ready_ref.at[:cells_at, :],
+        full_dot(stay_ref[own_at : own_at + cells, :cells], cleared_ref[...]),
+    )
+    ready_ref[kept_start:end, :] = stay_ref[...]
+
+
+def fill_kernel(slices, shape, ready_ref, below_ref, above_ref, *refs):
+    *blocks, done_ref, filled_ref, edge_ref = refs
     var_count, rows, pencils = shape
     cells = var_count * rows
     count = pencils // LANES
     _, own_at, about_at, _ = stay_at(rows, count, cells)
     cells_at, kept_start, _ = ready_at(rows, count, cells)
 
+    ghosts = LANES
+    about = [ready_ref[kept_start + about_at : kept_start + about_at + 8, :]]
+    about += [ref[ref.shape[0] - 8 :, :] for ref in (below_ref, above_ref)]
+
     def known(k):
-        start = kept_start + about_at + k
-        return ready_ref[start : start + 1, :].astype(jnp.int32)
+        return jnp.concatenate([x[k : k + 1] for x in about], axis=1).astype(jnp.int32)
 
     values = ghost_values(slices, blocks, known(OWNER), known(IMAGE))
-    ghosts = LANES
-    at_row = lax.broadcasted_iota(jnp.int32, (rows, ghosts), 0) == known(ROW)
-    spread = jnp.concatenate([jnp.where(at_row, value, 0.0) for value in values], axis=0)
+    row, pencil = known(ROW), known(PENCIL)
+    at_row = lax.broadcasted_iota(jnp.int32, (rows, ghosts), 0) == row[:, :ghosts]
+    spread = jnp.concatenate([jnp.where(at_row, value[:, :ghosts], 0.0) for value in values], axis=0)
     own = ready_ref[kept_start + own_at : kept_start + own_at + cells, :cells]
     both = jnp.concatenate([full_dot(own, spread), spread], axis=0)
-    spots = marks((pencils, ghosts), 0, known(PENCIL))
+    spots = marks((pencils, ghosts), 0, pencil[:, :ghosts])
     added = exact_dot(both, spots, ((1,), (1,)))
     for t in range(count):
         here = slice(t * cells, (t + 1) * cells)
         there = slice(cells_at + t * cells, cells_at + (t + 1) * cells)
         done_ref[here, :] = ready_ref[here, :] + added[:cells, tile(t)]
         filled_ref[here, :] = ready_ref[there, :] + added[cells:, tile(t)]
-    x_at, response_at, profile_at, _ = done_at(rows, count, cells)
+    x_at, response_at, profile_at, edge_at, _ = done_at(rows, count, cells, var_count)
+    none = jnp.zeros((8 - var_count, ghosts), jnp.float32)
+    for k, (ref, wanted) in enumerate(((below_ref, rows - 1), (above_ref, 0))):
+        here = slice((k + 1) * ghosts, (k + 2) * ghosts)
+        at_edge = row[:, here] == wanted
+        spread = [jnp.where(at_edge, value[:, here], 0.0) for value in values] + [none]
+        spots = marks((pencils, ghosts), 0, pencil[:, here])
+        turn(edge_ref, exact_dot(jnp.concatenate(spread, axis=0), spots, ((1,), (1,))))
+        for v in range(var_count):
+            start = edge_at + (k * var_count + v) * count
+            done_ref[start : start + count, :] = ref[v * count : (v + 1) * count, :] + slab_at(
+                edge_ref, v, 8, count
+            )
 
     def kept(which, i):
         start = kept_start + kept_at(which, i, rows, count)
@@ -759,7 +782,7 @@
     var_count, rows, pencils = segment_ref.shape
     count = pencils // LANES
     cells = var_count * rows
-    x_at, response_at, profile_at, _ = done_at(rows, count, cells)
+    x_at, response_at, profile_at, edge_at, _ = done_at(rows, count, cells, var_count)
     back_height, groups, per = slices.back_height, slices.back_groups, slices.per
     block = lane_block(max(groups, 1), slices.width)
     for m in range(slices.rest):
@@ -788,6 +811,10 @@
     lo_edge = jnp.where(row_at == 0, done_ref[edges : edges + 1, :], 0.0)
     hi_edge = jnp.where(row_at == rows - 1, done_ref[edges + 1 : edges + 2, :], 0.0)
 
+    def edge(k, v, t):
+        start = edge_at + (k * var_count + v) * count + t
+        return done_ref[start : start + 1, :]
+
     def response(k, t):
         start = response_at + (k * count + t) * rows
         return done_ref[start : start + rows, :]
@@ -800,7 +827,7 @@
             derivative_ref[v, :, tile(t)] = (
                 done_ref[start : start + rows, :]
                 + (lo_profile * lo + hi_profile * hi)
-                + (lo_edge * got(4, v, t) + hi_edge * got(5, v, t))
+                + (lo_edge * edge(0, v, t) + hi_edge * edge(1, v, t))
             )
             segment_ref[v, :, tile(t)] = (
                 done_ref[x_at + start : x_at + start + rows, :]
@@ -860,7 +887,7 @@
     slices = Slices(slabs, count, cross, var_count, images)
     tables = jnp.asarray(tables)
     turned = (cells * count, LANES)
-    stay = stay_at(rows, count, cells)[3] + cells * count
+    stay = stay_at(rows, count, cells)[3]
     ready = (ready_at(rows, count, cells)[2], LANES)
 
     arguments = (
@@ -877,12 +904,14 @@
     )
     buffers = list(arguments)
     buffers[2] = jax.ShapeDtypeStruct(tables.shape[1:], jnp.float32)
-    message, stay = call(
+    edge = (-(-var_count * count // 8) * 8 + 8, LANES)
+    message, stay, up, down = call(
         functools.partial(prepare_kernel, slices, at),
-        [(slabs * slices.height, LANES), (stay, LANES)],
+        [(slabs * slices.height, LANES), (stay, LANES), edge, edge],
         buffers
         + [
             (stay, LANES),
+            turned,
             (rows * count, LANES),
             (rows * count, LANES),
             (2 * rows * count, LANES),
@@ -898,8 +927,18 @@
         far_out=(1,),
     )
     message = exchange(message, "pipe")
+    forward = [(i, i + 1) for i in range(slabs - 1)]
+    below = lax.ppermute(up, "pipe", forward)
+    above = lax.ppermute(down, "pipe", [(j, i) for i, j in forward])
+    message, below, above = lax.optimization_barrier((message, below, above))
     (ready,) = call(
-        functools.partial(own_kernel, state.shape), [ready], [], [], (stay,), near=(0,), limit=48
+        own_kernel,
+        [ready],
+        [(cells, pencils)],
+        [],
+        (stay, cell_mask, state),
+        near=range(3),
+        limit=48,
     )
     (image_values,) = call(
         functools.partial(pick_kernel, slices),
@@ -939,11 +978,11 @@
     back = exchange(back, "pipe")
     (done,) = call(
         functools.partial(fill_kernel, slices, state.shape),
-        [(done_at(rows, count, cells)[3], LANES)],
-        [turned],
+        [(done_at(rows, count, cells, var_count)[4], LANES)],
+        [turned, (8 * count, LANES)],
         [],
-        (ready, *blocks),
-        near=range(1 + cross),
+        (ready, below, above, *blocks),
+        near=range(3 + cross),
         limit=48,
     )
     return tuple(

time: 48.1 us -> 46.7 us (0.971)
  blocking collectives: 20.7 us -> 0 us
  starting transfers between devices: 5.31 us -> 18.2 us
  waiting for transfers between devices: 9.15 us -> 16.2 us
  Pallas kernels: 11.9 us -> 11.2 us
    all_to_all x1 -> x0, blocking collectives: 20.7 us -> none  [exchange(): return lax.all_to_all(message, axes, 0, 0, tiled=True)]
    all_to_all x1 -> x2, starting transfers between devices: 3.6 us -> 11.2 us  [exchange(): return lax.all_to_all(message, axes, 0, 0, tiled=True)]
    ppermute x0 -> x2, starting transfers between devices: none -> 5.21 us  [the longest x1 3.92 us: local(): below = lax.ppermute(up, 'pipe', forward)]
    ppermute x0 -> x2, waiting for transfers between devices: none -> 5.08 us  [the longest x1 4.15 us: local(): above = lax.ppermute(down, 'pipe', [(j, i) for i, j in forward])]
    all_to_all x1 -> x2, waiting for transfers between devices: 6.12 us -> 8.04 us  [exchange(): return lax.all_to_all(message, axes, 0, 0, tiled=True)]
    pallas_call x7, Pallas kernels: 11.9 us -> 11.2 us  [call(): pl.pallas_call(kernel, out_shape=[jax.ShapeDtypeStruct(shape, jnp.float32...]
  transfers between devices with their start and end apart: 4 -> 7, of which waited for: 3 -> 6; matrix products, arithmetic and copies ran while one was open for 0% -> 0% of each run, Pallas kernels for 6% -> 7%
where the time goes in v4:
time: 46.7 us; the launch traced here: 46.3 us
  starting transfers between devices  18.2 us (39%)
  waiting for transfers between devices  16.2 us (35%)
  Pallas kernels  11.2 us (24%)
  between operations  0.74 us (2%)
    all_to_all x2, starting transfers between devices, exchange(): return lax.all_to_all(message, axes, 0, 0, tiled=True)  11.2 us
    pallas_call x7, Pallas kernels, call(): pl.pallas_call(kernel, out_shape=[jax.ShapeDtypeStruct(shape, jnp.float32...  11.2 us
    all_to_all x2, waiting for transfers between devices, exchange(): return lax.all_to_all(message, axes, 0, 0, tiled=True)  8.04 us
    ppermute x1, waiting for transfers between devices, local(): above = lax.ppermute(down, 'pipe', [(j, i) for i, j in forward])  4.15 us
    ppermute x1, starting transfers between devices, local(): below = lax.ppermute(up, 'pipe', forward)  3.92 us
    ppermute x3, waiting for transfers between devices, local(): lax.ppermute(image_values, 'cross', [(i, (i + u) % cross) for i in range(...  3.04 us
    ppermute x3, starting transfers between devices, local(): lax.ppermute(image_values, 'cross', [(i, (i + u) % cross) for i in range(...  1.71 us
    ppermute x1, starting transfers between devices, local(): above = lax.ppermute(down, 'pipe', [(j, i) for i, j in forward])  1.29 us
  transfers between devices with their start and end apart: 7, of which 6 were waited for; matrix products, arithmetic and copies ran while one was open for 0% of the time, Pallas kernels for 7%

profile of v4, /device:TPU:0, one launch (start us, length us, event | category | flops | bytes accessed | tf_op | source)
XLA Modules:
  0.0 46.3 jit_solution(7615783538133071742)
XLA Ops:
  0.6 0.0 copy-start.2
  0.6 0.0 copy-start
  0.7 5.0 %shard_map.113 = (f32[896,128]{1,0:T(8,128)}, f32[1664,128]{1,0:T(8,128)}, f32[104,128]{1,0:T(8,128)}, f32[104,128]{1,0:T(8,128)}) custom-call(f32[16,2304]{1,0:T(8,128)} %face_hbm.1, f32[16,2304]{1,0:T(8,128)} %courant_hbm.1, f32[8,192,128]{2,1,0:T(8,128)} %constant.2.clone.tables_hbm, s32[128]{0:T(128)} %cell_hbm.1, s32[128]{0:T(128)} %owner_hbm.1, ...), custom_call_target="tpu_custom_call" | custom-call | tf_op jit(solution)/shard_map/pallas_call | solution.py:856
  5.7 0.0 copy-start.1
  5.7 7.4 %all-to-all-start = ((f32[8,112,128]{2,1,0:T(8,128)}), f32[8,112,128]{2,1,0:T(8,128)S(1)}, u32[]{:S(2)}, u32[]{:S(2)}) async-start(f32[8,112,128]{2,1,0:T(8,128)} %bitcast.8), calls=%async_computation | async-start | bytes 917504 | tf_op jit(solution)/shard_map/all_to_all | solution.py:867
  13.1 3.9 %collective-permute-start = (f32[104,128]{1,0:T(8,128)}, f32[104,128]{1,0:T(8,128)S(1)}, u32[]{:S(2)}, u32[]{:S(2)}) collective-permute-start(f32[104,128]{1,0:T(8,128)} %get-tuple-element.12), channel_id=1, source_target_pairs={{0,4},{4,8},{8,12},{12,16},{16,20},{20,24},{24,28},{1,5},{5,9},{9,... | collective-permute-start | bytes 159752 | tf_op jit(solution)/shard_map/ppermute | solution.py:931
  17.0 1.3 %collective-permute-start.1 = (f32[104,128]{1,0:T(8,128)}, f32[104,128]{1,0:T(8,128)S(1)}, u32[]{:S(2)}, u32[]{:S(2)}) collective-permute-start(f32[104,128]{1,0:T(8,128)} %get-tuple-element.13), channel_id=1, source_target_pairs={{4,0},{8,4},{12,8},{16,12},{20,16},{24,20},{28,24},{5,1},{9,5},{13... | collective-permute-start | bytes 159752 | tf_op jit(solution)/shard_map/ppermute | solution.py:932
  18.3 0.9 %collective-permute-done.below_ref = f32[104,128]{1,0:T(8,128)S(1)} collective-permute-done((f32[104,128]{1,0:T(8,128)}, f32[104,128]{1,0:T(8,128)S(1)}, u32[]{:S(2)}, u32[]{:S(2)}) %collective-permute-start) | collective-permute-done | bytes 53280 | tf_op jit(solution)/shard_map/ppermute | solution.py:931
  19.3 4.2 %collective-permute-done.1.above_ref = f32[104,128]{1,0:T(8,128)S(1)} collective-permute-done((f32[104,128]{1,0:T(8,128)}, f32[104,128]{1,0:T(8,128)S(1)}, u32[]{:S(2)}, u32[]{:S(2)}) %collective-permute-start.1) | collective-permute-done | bytes 53280 | tf_op jit(solution)/shard_map/ppermute | solution.py:932
  23.4 3.3 %all-to-all-done = f32[8,112,128]{2,1,0:T(8,128)S(1)} async-done(((f32[8,112,128]{2,1,0:T(8,128)}), f32[8,112,128]{2,1,0:T(8,128)S(1)}, u32[]{:S(2)}, u32[]{:S(2)}) %all-to-all-start) | async-done | bytes 458784 | tf_op jit(solution)/shard_map/all_to_all | solution.py:867
  26.8 0.0 collective-permute-start.4
  26.8 1.6 %collective-permute-start.3 = (f32[80,128]{1,0:T(8,128)S(1)}, f32[80,128]{1,0:T(8,128)S(1)}, u32[]{:S(2)}, u32[]{:S(2)}) collective-permute-start(f32[80,128]{1,0:T(8,128)S(1)} %shard_map.115.refs_0_), channel_id=1, source_target_pairs={{0,2},{1,3},{2,0},{3,1},{4,6},{5,7},{6,4},{7,5},{8,10},{9,11},{10,... | collective-permute-start | bytes 122888 | tf_op jit(solution)/shard_map/ppermute | solution.py:953
  28.3 0.2 collective-permute-start.2
  28.5 0.2 shard_map.114
  28.7 0.0 collective-permute-done.4.refs_3_
  28.7 2.4 %collective-permute-done.3.refs_2_ = f32[80,128]{1,0:T(8,128)S(1)} collective-permute-done((f32[80,128]{1,0:T(8,128)S(1)}, f32[80,128]{1,0:T(8,128)S(1)}, u32[]{:S(2)}, u32[]{:S(2)}) %collective-permute-start.3) | collective-permute-done | bytes 40992 | tf_op jit(solution)/shard_map/ppermute | solution.py:953
  31.1 0.6 %collective-permute-done.2.refs_1_ = f32[80,128]{1,0:T(8,128)S(1)} collective-permute-done((f32[80,128]{1,0:T(8,128)S(1)}, f32[80,128]{1,0:T(8,128)S(1)}, u32[]{:S(2)}, u32[]{:S(2)}) %collective-permute-start.2) | collective-permute-done | bytes 40992 | tf_op jit(solution)/shard_map/ppermute | solution.py:953
  31.8 1.6 %shard_map.116 = f32[384,128]{1,0:T(8,128)} custom-call(f32[896,128]{1,0:T(8,128)S(1)} %bitcast.6, f32[320,128]{1,0:T(8,128)S(1)} %get-tuple-element.15.rest_ref, f32[256,128]{1,0:T(8,128)S(1)} %get-tuple-element.16.chain_ref, f32[80,128]{1,0:T(8,128)S(1)} %shard_map.115.refs_0_, f32[80,128]{1,0:T(8,128)S(1)} %collective-permute-done.2.refs_1_, ...), custom_call_target="tpu_custom_call" | custom-call | tf_op jit(solution)/shard_map/pallas_call | solution.py:856
  33.4 3.8 %all-to-all-start.1 = ((f32[8,48,128]{2,1,0:T(8,128)}), f32[8,48,128]{2,1,0:T(8,128)S(1)}, u32[]{:S(2)}, u32[]{:S(2)}) async-start(f32[8,48,128]{2,1,0:T(8,128)} %bitcast.2), calls=%async_computation.1 | async-start | bytes 393216 | tf_op jit(solution)/shard_map/all_to_all | solution.py:867
  37.2 0.0 copy-done.2
  37.2 0.0 copy-done
  37.2 0.0 copy-done.1
  37.2 0.8 %shard_map.117.ready_ref = f32[4544,128]{1,0:T(8,128)S(1)} custom-call(f32[1664,128]{1,0:T(8,128)S(1)} %copy-done.1, s32[16,2304]{1,0:T(8,128)S(1)} %copy-done.2, f32[5,16,2304]{2,1,0:T(8,128)S(1)} %copy-done), custom_call_target="tpu_custom_call" | custom-call | tf_op jit(solution)/shard_map/pallas_call | solution.py:856
  38.0 2.3 %shard_map.118.done_ref = f32[4252,128]{1,0:T(8,128)S(1)} custom-call(f32[4544,128]{1,0:T(8,128)S(1)} %shard_map.117.ready_ref, f32[104,128]{1,0:T(8,128)S(1)} %collective-permute-done.below_ref, f32[104,128]{1,0:T(8,128)S(1)} %collective-permute-done.1.above_ref, f32[80,128]{1,0:T(8,128)S(1)} %shard_map.115.refs_0_, ...), custom_call_target="tpu_custom_call" | custom-call | tf_op jit(solution)/shard_map/pallas_call | solution.py:856
  40.3 4.7 %all-to-all-done.1 = f32[8,48,128]{2,1,0:T(8,128)S(1)} async-done(((f32[8,48,128]{2,1,0:T(8,128)}), f32[8,48,128]{2,1,0:T(8,128)S(1)}, u32[]{:S(2)}, u32[]{:S(2)}) %all-to-all-start.1) | async-done | bytes 196640 | tf_op jit(solution)/shard_map/all_to_all | solution.py:867
  45.0 1.3 %shard_map.119 = (f32[5,16,2304]{2,1,0:T(8,128)}, f32[5,16,2304]{2,1,0:T(8,128)}) custom-call(f32[384,128]{1,0:T(8,128)S(1)} %bitcast.7, f32[4252,128]{1,0:T(8,128)S(1)} %shard_map.118.done_ref), custom_call_target="tpu_custom_call" | custom-call | tf_op jit(solution)/shard_map/pallas_call | solution.py:856
  (1 shorter events, 0.0 us)
Async XLA Ops:
  0.6 36.6 %copy-start.2 = (s32[16,2304]{1,0:T(8,128)S(1)}, s32[16,2304]{1,0:T(8,128)}, u32[]{:S(2)}) copy-start(s32[16,2304]{1,0:T(8,128)} %mask_ref.1) | copy-start | bytes 442372
  0.6 36.6 %copy-start = (f32[5,16,2304]{2,1,0:T(8,128)S(1)}, f32[5,16,2304]{2,1,0:T(8,128)}, u32[]{:S(2)}) copy-start(f32[5,16,2304]{2,1,0:T(8,128)} %state_ref.1) | copy-start | bytes 2211844
  5.7 31.6 %copy-start.1 = (f32[1664,128]{1,0:T(8,128)S(1)}, f32[1664,128]{1,0:T(8,128)}, u32[]{:S(2)}) copy-start(f32[1664,128]{1,0:T(8,128)} %get-tuple-element.17.stay_ref) | copy-start | bytes 2555908
  5.7 21.1 %all-to-all-start = ((f32[8,112,128]{2,1,0:T(8,128)}), f32[8,112,128]{2,1,0:T(8,128)S(1)}, u32[]{:S(2)}, u32[]{:S(2)}) async-start(f32[8,112,128]{2,1,0:T(8,128)} %bitcast.8), calls=%async_computation | async-start | bytes 917504 | tf_op jit(solution)/shard_map/all_to_all | solution.py:867
  13.1 6.2 %collective-permute-start = (f32[104,128]{1,0:T(8,128)}, f32[104,128]{1,0:T(8,128)S(1)}, u32[]{:S(2)}, u32[]{:S(2)}) collective-permute-start(f32[104,128]{1,0:T(8,128)} %get-tuple-element.12), channel_id=1, source_target_pairs={{0,4},{4,8},{8,12},{12,16},{16,20},{20,24},{24,28},{1,5},{5,9},{9,... | collective-permute-start | bytes 159752 | tf_op jit(solution)/shard_map/ppermute | solution.py:931
  17.0 6.4 %collective-permute-start.1 = (f32[104,128]{1,0:T(8,128)}, f32[104,128]{1,0:T(8,128)S(1)}, u32[]{:S(2)}, u32[]{:S(2)}) collective-permute-start(f32[104,128]{1,0:T(8,128)} %get-tuple-element.13), channel_id=1, source_target_pairs={{4,0},{8,4},{12,8},{16,12},{20,16},{24,20},{28,24},{5,1},{9,5},{13... | collective-permute-start | bytes 159752 | tf_op jit(solution)/shard_map/ppermute | solution.py:932
  26.8 1.9 %collective-permute-start.4 = (f32[80,128]{1,0:T(8,128)S(1)}, f32[80,128]{1,0:T(8,128)S(1)}, u32[]{:S(2)}, u32[]{:S(2)}) collective-permute-start(f32[80,128]{1,0:T(8,128)S(1)} %shard_map.115.refs_0_), channel_id=1, source_target_pairs={{0,3},{1,0},{2,1},{3,2},{4,7},{5,4},{6,5},{7,6},{8,11},{9,8},{10,9... | collective-permute-start | bytes 122888 | tf_op jit(solution)/shard_map/ppermute | solution.py:953
  26.8 4.3 %collective-permute-start.3 = (f32[80,128]{1,0:T(8,128)S(1)}, f32[80,128]{1,0:T(8,128)S(1)}, u32[]{:S(2)}, u32[]{:S(2)}) collective-permute-start(f32[80,128]{1,0:T(8,128)S(1)} %shard_map.115.refs_0_), channel_id=1, source_target_pairs={{0,2},{1,3},{2,0},{3,1},{4,6},{5,7},{6,4},{7,5},{8,10},{9,11},{10,... | collective-permute-start | bytes 122888 | tf_op jit(solution)/shard_map/ppermute | solution.py:953
  28.3 3.4 %collective-permute-start.2 = (f32[80,128]{1,0:T(8,128)S(1)}, f32[80,128]{1,0:T(8,128)S(1)}, u32[]{:S(2)}, u32[]{:S(2)}) collective-permute-start(f32[80,128]{1,0:T(8,128)S(1)} %shard_map.115.refs_0_), channel_id=1, source_target_pairs={{0,1},{1,2},{2,3},{3,0},{4,5},{5,6},{6,7},{7,4},{8,9},{9,10},{10,1... | collective-permute-start | bytes 122888 | tf_op jit(solution)/shard_map/ppermute | solution.py:953
  33.4 11.6 %all-to-all-start.1 = ((f32[8,48,128]{2,1,0:T(8,128)}), f32[8,48,128]{2,1,0:T(8,128)S(1)}, u32[]{:S(2)}, u32[]{:S(2)}) async-start(f32[8,48,128]{2,1,0:T(8,128)} %bitcast.2), calls=%async_computation.1 | async-start | bytes 393216 | tf_op jit(solution)/shard_map/all_to_all | solution.py:867

commit v5 on v4

--- a/solution.py
+++ b/solution.py
@@ -15,7 +15,8 @@
 Z_UP, Z_DOWN, ROW_FIRST, ROW_LAST, RIGHT_FIRST, RIGHT_LAST = range(6)
 LINK_IN, MARGIN_FIRST, MARGIN_LAST, LINK_UP, FIRST_LO, FIRST_HI, LAST_LO, LAST_HI, FIRST_EDGE, LAST_EDGE = range(10)
 COEFFICIENTS = 10
-PENCIL, ROW, OWNER, IMAGE, WEIGHT_UP, WEIGHT_DOWN, WEIGHT_FIRST, WEIGHT_LAST = range(8)
+CELL, COLUMN, WEIGHT_FIRST, WEIGHT_LAST = range(4)
+ABOUT = 4
 
 
 def derivative_tables(slabs, rows, var_count):
@@ -35,9 +36,10 @@
     M = inverse @ B
 
     cells = var_count * rows
-    own_at, reduce_at, adjoint_at, profile_at, weight_at = 0, cells, cells + 16, cells + 56, cells + 96
+    own_at, reduce_at, adjoint_at, profile_at = 0, cells, cells + 32, cells + 72
     tables = np.zeros((slabs, cells + 112, LANES))
     carry_up, carry_down = np.zeros(slabs), np.zeros(slabs)
+    ups, downs = np.zeros((slabs, rows)), np.zeros((slabs, rows))
     for p in range(slabs):
         table = tables[p]
         base = p * rows
@@ -63,8 +65,8 @@
         for v in range(var_count):
             at = slice(v * rows, (v + 1) * rows)
             table[own_at + v * rows : own_at + (v + 1) * rows, at] = own
-            table[reduce_at + v, at] = weight_up
-            table[reduce_at + var_count + v, at] = weight_down
+        table[reduce_at : reduce_at + rows] = weight_up[:, None]
+        table[reduce_at + rows : reduce_at + 2 * rows] = weight_down[:, None]
         table[adjoint_at : adjoint_at + rows, :rows] = own.T
         table[adjoint_at + rows : adjoint_at + 2 * rows, rows : 2 * rows] = own.T
         more = adjoint_at + 2 * rows
@@ -78,10 +80,9 @@
         table[profile_at + rows : profile_at + 2 * rows] = hi[:, None]
         table[profile_at + 2 * rows] = lo_edge[0]
         table[profile_at + 2 * rows + 1] = hi_edge[-1]
-        table[weight_at, :rows] = weight_up
-        table[weight_at + 1, :rows] = weight_down
-    at = (own_at, reduce_at, adjoint_at, profile_at, weight_at)
-    return tables.astype(np.float32), at, carry_up, carry_down
+        ups[p], downs[p] = weight_up, weight_down
+    at = (own_at, reduce_at, adjoint_at, profile_at)
+    return tables.astype(np.float32), at, (carry_up, carry_down, ups, downs)
 
 
 def split(x, parts):
@@ -184,7 +185,7 @@
         self.lines, self.back_lines = 6 * var_count + COEFFICIENTS, 4 * var_count
         self.groups, self.back_groups = (self.group_count(n) for n in (self.lines, self.back_lines))
         self.meta_at = self.lines * self.full
-        self.packed_at = self.meta_at + 8
+        self.packed_at = self.meta_at + ABOUT
         self.images_at = self.packed_at + self.groups
         self.height = -(-(self.images_at + self.image_rows) // 8) * 8
         self.back_packed_at = self.back_lines * self.full
@@ -212,18 +213,15 @@
     return x if by == 0 else pltpu.roll(x, by, 1)
 
 
-def image_lines(x, base, weight_ref, rows, var_count):
-    pencils = x.shape[1]
-    images = base.shape[1]
-    row, pencil = place_of(base, rows, pencils)
-    pick = marks((pencils, images), 0, pencil)
+def image_lines(x, row, pick_ref, weight_ref, rows, var_count):
+    pencils, images = pick_ref.shape
     row_at = lax.broadcasted_iota(jnp.int32, (rows, images), 0)
     lower, upper = row_at == row, row_at == row + 1
     total = [jnp.zeros((rows, images), jnp.float32) for _ in range(var_count)]
     pieces = jnp.concatenate(split(x, 2), axis=0)
     for corner, shift in enumerate((0, 1, LINE, LINE + 1)):
         moved = pieces if shift == 0 else pltpu.roll(pieces, pencils - shift, 1)
-        found = jnp.dot(moved, pick, preferred_element_type=jnp.float32)
+        found = jnp.dot(moved, pick_ref[...], preferred_element_type=jnp.float32)
         found = found[: var_count * rows] + found[var_count * rows :]
         weight = jnp.where(lower, weight_ref[corner : corner + 1], 0.0) + jnp.where(
             upper, weight_ref[corner + 4 : corner + 5], 0.0
@@ -237,10 +235,13 @@
     return jnp.concatenate(lines, axis=0)
 
 
-def ghost_values(slices, blocks, owner, image):
+def ghost_values(slices, blocks, column):
     per = slices.image_rows // slices.var_count
     slabs, cross = slices.slabs, slices.cross
-    ghosts = owner.shape[1]
+    ghosts = column.shape[1]
+    images = per * LANES
+    owner = ((column + 0.5) * (1.0 / images)).astype(jnp.int32)
+    image = column.astype(jnp.int32) - owner * images
     across = lax.axis_index("cross")
     values = [
         jnp.concatenate(
@@ -262,7 +263,7 @@
     found = exact_dot(jnp.concatenate(values, axis=0), pick, ((1,), (0,)))
     devices = slabs * cross
     at = lax.broadcasted_iota(jnp.int32, (devices, ghosts), 0)
-    mine = (at % slabs) * cross + (across + cross - at // slabs) % cross == owner
+    mine = (at % slabs) * cross + (across ^ (at // slabs)) == owner
     return [
         reflect
         * jnp.sum(
@@ -304,7 +305,7 @@
     face_turned_ref,
     courant_turned_ref,
     pair_ref,
-    z_ref,
+    pick_ref,
     matrix_ref,
     adjoint_ref,
     weight_ref,
@@ -321,7 +322,7 @@
     p = lax.axis_index("pipe")
     slabs, height = slices.slabs, slices.height
     lines = slices.groups * slices.per
-    own_at, reduce_at, adjoint_at, profile_at, weight_at = at
+    own_at, reduce_at, adjoint_at, profile_at = at
     copies = fetch(
         (
             face_hbm,
@@ -330,9 +331,9 @@
             cell_hbm,
             owner_hbm,
             image_hbm,
-            mask_hbm,
             base_hbm,
             corner_hbm,
+            mask_hbm,
             state_hbm,
         ),
         (
@@ -342,9 +343,9 @@
             cell_ref,
             owner_ref,
             image_ref,
-            mask_ref,
             base_ref,
             corner_ref,
+            mask_ref,
             state_ref,
         ),
         sems,
@@ -367,7 +368,10 @@
         rows_at = [slices.coefficient_row(which, t) for t in range(slices.full)]
         send(6 * var_count + which, rows_at, slab)
 
-    copies[0].wait()
+    for copy in copies[:8]:
+        copy.wait()
+    image_row, image_pencil = place_of(base_ref[...].reshape(1, -1), rows, pencils)
+    pick_ref[...] = marks(pick_ref.shape, 0, image_pencil)
     turn(face_turned_ref, face_ref[...])
 
     def face(i):
@@ -399,7 +403,6 @@
     for i in range(rows - 2, 0, -1):
         first[i] = to_first[i] + to_up[i] * first[i + 1]
         last[i] = to_up[i] * last[i + 1]
-    copies[1].wait()
     turn(courant_turned_ref, courant_ref[...])
     for i in range(rows):
         speed = slab_at(courant_turned_ref, i, rows, count)
@@ -409,7 +412,6 @@
         put_slab(pair_ref, rows + i, 2 * rows, count, last[i] * speed)
     for t in range(count):
         matrix_ref[:, tile(t)] = pair_ref[t * 2 * rows : (t + 1) * 2 * rows, :]
-    copies[2].wait()
     stay_ref[kept - 40 : kept, :] = table_ref[profile_at : profile_at + 40, :]
     stay_ref[own : own + cells, :] = table_ref[own_at : own_at + cells, :]
     turn(
@@ -421,8 +423,6 @@
     for i, share in enumerate(first + last):
         weight_ref[i, :count, :] = share - slab_at(adjoint_ref, i, 40, count)
 
-    for copy in copies[3:6]:
-        copy.wait()
     row, pencil = place_of(cell_ref[...].reshape(1, ghosts), rows, pencils)
     lane_tile = jnp.right_shift(pencil, 7)
     lane_marks = marks((LANES, ghosts), 0, pencil - lane_tile * LANES)
@@ -432,19 +432,16 @@
     at_cell = (lax.broadcasted_iota(jnp.int32, (rows, padded, ghosts), 0) == row[None]) & (
         lax.broadcasted_iota(jnp.int32, (rows, padded, ghosts), 1) == lane_tile[None]
     )
-    row_marks = jnp.where(lax.broadcasted_iota(jnp.int32, (rows, ghosts), 0) == row, 1.0, 0.0)
-    up_down = full_dot(table_ref[weight_at : weight_at + 8, :rows], row_marks)
 
     def at_ghosts(values):
         return jnp.sum(jnp.sum(jnp.where(at_cell, values, 0.0), axis=0), axis=0, keepdims=True)
 
     about = jnp.concatenate(
         [
-            pencil.astype(jnp.float32),
-            row.astype(jnp.float32),
-            owner_ref[...].reshape(1, ghosts).astype(jnp.float32),
-            image_ref[...].reshape(1, ghosts).astype(jnp.float32),
-            up_down[0:2],
+            cell_ref[...].reshape(1, ghosts).astype(jnp.float32),
+            (owner_ref[...] * base_ref.shape[0] + image_ref[...])
+            .reshape(1, ghosts)
+            .astype(jnp.float32),
             at_ghosts(picked[0]),
             at_ghosts(picked[1]),
         ],
@@ -452,19 +449,19 @@
     )
     for j in range(slabs):
         start = j * height + slices.meta_at
-        message_ref[start : start + 8, :] = about
-    stay_ref[about_at : about_at + 8, :] = about
+        message_ref[start : start + ABOUT, :] = about
+    stay_ref[about_at : about_at + ABOUT, :] = about
     edge = var_count * count
     for ref in (up_ref, down_ref):
-        ref[edge : ref.shape[0] - 8, :] = jnp.zeros((ref.shape[0] - 8 - edge, LANES), jnp.float32)
-        ref[ref.shape[0] - 8 :, :] = about
+        ref[edge : edge + ABOUT, :] = about
     staying = pltpu.make_async_copy(stay_ref, stay_hbm, stay_sem.at[0])
     staying.start()
-    for copy in copies[6:]:
+    for copy in copies[8:]:
         copy.wait()
     values = image_lines(
         state_ref[...].reshape(cells, pencils),
-        base_ref[...].reshape(1, base_ref.shape[0]),
+        image_row,
+        pick_ref,
         corner_ref,
         rows,
         var_count,
@@ -477,26 +474,28 @@
         here = slice(v * rows, (v + 1) * rows)
         cleared_ref[here, :] = jnp.where(solid, 0.0, state_ref[v])
     turn(turned_ref, cleared_ref[...])
-    turn(z_ref, full_dot(table_ref[reduce_at : reduce_at + 16, :cells], cleared_ref[...]))
-    for v in range(var_count):
-        send_value(Z_UP, v, slab_at(z_ref, v, 16, count))
-        send_value(Z_DOWN, v, slab_at(z_ref, var_count + v, 16, count))
-    low, high = ([jnp.zeros((count, LANES), jnp.float32)] * var_count for _ in range(2))
-    for i in range(rows):
-        to_low, to_high = weight_ref[i, :count, :], weight_ref[rows + i, :count, :]
-        for v in range(var_count):
-            cell = slab_at(turned_ref, v * rows + i, cells, count)
-            if i == 0:
-                send_value(ROW_FIRST, v, cell)
-                down_ref[v * count : (v + 1) * count, :] = cell
-            if i == rows - 1:
-                send_value(ROW_LAST, v, cell)
-                up_ref[v * count : (v + 1) * count, :] = cell
-            low[v] = low[v] + to_low * cell
-            high[v] = high[v] + to_high * cell
-    for v in range(var_count):
-        send_value(RIGHT_FIRST, v, low[v])
-        send_value(RIGHT_LAST, v, high[v])
+    for group in (range(0, 3), range(3, var_count)):
+        sums = {v: [zero] * 4 for v in group}
+        for i in range(rows):
+            up, down = reduce_at + i, reduce_at + rows + i
+            weights = (
+                table_ref[up : up + 1, :],
+                table_ref[down : down + 1, :],
+                weight_ref[i, :count, :],
+                weight_ref[rows + i, :count, :],
+            )
+            for v in group:
+                cell = slab_at(turned_ref, v * rows + i, cells, count)
+                if i == 0:
+                    send_value(ROW_FIRST, v, cell)
+                    down_ref[v * count : (v + 1) * count, :] = cell
+                if i == rows - 1:
+                    send_value(ROW_LAST, v, cell)
+                    up_ref[v * count : (v + 1) * count, :] = cell
+                sums[v] = [x + weight * cell for x, weight in zip(sums[v], weights)]
+        for v in group:
+            for functional, total in zip((Z_UP, Z_DOWN, RIGHT_FIRST, RIGHT_LAST), sums[v]):
+                send_value(functional, v, total)
 
     block = lane_block(max(slices.groups, 1), slices.width)
     for m in range(slices.rest):
@@ -549,7 +548,7 @@
             margin = following + margin * ratio
 
 
-def solve_kernel(slices, carry_up, carry_down, message_ref, rest_ref, chain_ref, *refs):
+def solve_kernel(slices, pencils, constants, message_ref, rest_ref, chain_ref, *refs):
     *blocks, back_ref, ghost_ref, back_rest_ref = refs
     slabs, var_count, chunk, full = slices.slabs, slices.var_count, slices.chunk, slices.full
     height, per, width = slices.height, slices.per, slices.width
@@ -560,9 +559,12 @@
         return message_ref[start : start + 1, :]
 
     def meta_all(k):
-        return jnp.concatenate([meta(p, k) for p in range(slabs)], axis=1).astype(jnp.int32)
-
-    values = ghost_values(slices, blocks, meta_all(OWNER), meta_all(IMAGE))
+        return jnp.concatenate([meta(p, k) for p in range(slabs)], axis=1)
+
+    carry_up, carry_down, ups, downs = constants
+    values = ghost_values(slices, blocks, meta_all(COLUMN))
+    rows = ups.shape[1]
+    row_of, pencil_of = place_of(meta_all(CELL).astype(jnp.int32), rows, pencils)
     ghosts = LANES
     place = lax.broadcasted_iota(jnp.int32, (chunk * LANES, ghosts), 0)
     slot, lane = place // LANES, place % LANES
@@ -573,18 +575,22 @@
     )
     none = jnp.zeros((8 - var_count, ghosts), jnp.float32)
     for p in range(slabs):
-        row = meta(p, ROW)
+        row = row_of[:, tile(p)]
+        up = down = jnp.zeros((1, ghosts), jnp.float32)
+        for i in range(rows):
+            up = jnp.where(row == i, float(ups[p, i]), up)
+            down = jnp.where(row == i, float(downs[p, i]), down)
         weights = (
-            meta(p, WEIGHT_UP),
-            meta(p, WEIGHT_DOWN),
-            jnp.where(row == 0.0, 1.0, 0.0),
-            jnp.where(row == 15.0, 1.0, 0.0),
+            up,
+            down,
+            jnp.where(row == 0, 1.0, 0.0),
+            jnp.where(row == rows - 1, 1.0, 0.0),
             meta(p, WEIGHT_FIRST),
             meta(p, WEIGHT_LAST),
         )
         here = jnp.concatenate([value[:, tile(p)] for value in values] + [none], axis=0)
         shares = jnp.concatenate([here * weight for weight in weights], axis=0)
-        spots = jnp.where(pencil_at == meta(p, PENCIL).astype(jnp.int32), 1.0, 0.0)
+        spots = jnp.where(pencil_at == pencil_of[:, tile(p)], 1.0, 0.0)
         share = exact_dot(shares, spots.astype(jnp.bfloat16), ((1,), (1,)))
         for t in range(chunk):
             start = (p * chunk + t) * 48
@@ -700,14 +706,15 @@
     cells_at, kept_start, _ = ready_at(rows, count, cells)
 
     ghosts = LANES
-    about = [ready_ref[kept_start + about_at : kept_start + about_at + 8, :]]
-    about += [ref[ref.shape[0] - 8 :, :] for ref in (below_ref, above_ref)]
+    about = [ready_ref[kept_start + about_at : kept_start + about_at + ABOUT, :]]
+    edge = var_count * count
+    about += [ref[edge : edge + ABOUT, :] for ref in (below_ref, above_ref)]
 
     def known(k):
-        return jnp.concatenate([x[k : k + 1] for x in about], axis=1).astype(jnp.int32)
-
-    values = ghost_values(slices, blocks, known(OWNER), known(IMAGE))
-    row, pencil = known(ROW), known(PENCIL)
+        return jnp.concatenate([x[k : k + 1] for x in about], axis=1)
+
+    values = ghost_values(slices, blocks, known(COLUMN))
+    row, pencil = place_of(known(CELL).astype(jnp.int32), rows, pencils)
     at_row = lax.broadcasted_iota(jnp.int32, (rows, ghosts), 0) == row[:, :ghosts]
     spread = jnp.concatenate([jnp.where(at_row, value[:, :ghosts], 0.0) for value in values], axis=0)
     own = ready_ref[kept_start + own_at : kept_start + own_at + cells, :cells]
@@ -883,7 +890,7 @@
     count = pencils // LANES
     cells = var_count * rows
     images = image_base.shape[0]
-    tables, at, carry_up, carry_down = derivative_tables(slabs, rows, var_count)
+    tables, at, constants = derivative_tables(slabs, rows, var_count)
     slices = Slices(slabs, count, cross, var_count, images)
     tables = jnp.asarray(tables)
     turned = (cells * count, LANES)
@@ -904,7 +911,7 @@
     )
     buffers = list(arguments)
     buffers[2] = jax.ShapeDtypeStruct(tables.shape[1:], jnp.float32)
-    edge = (-(-var_count * count // 8) * 8 + 8, LANES)
+    edge = (-(-(var_count * count + ABOUT) // 8) * 8, LANES)
     message, stay, up, down = call(
         functools.partial(prepare_kernel, slices, at),
         [(slabs * slices.height, LANES), (stay, LANES), edge, edge],
@@ -915,7 +922,7 @@
             (rows * count, LANES),
             (rows * count, LANES),
             (2 * rows * count, LANES),
-            (16 * count, LANES),
+            jax.ShapeDtypeStruct((pencils, images), jnp.bfloat16),
             (2 * rows, pencils),
             (40 * count, LANES),
             (2 * rows, -(-count // 8) * 8, LANES),
@@ -950,7 +957,7 @@
         limit=24,
     )
     blocks = [image_values] + [
-        lax.ppermute(image_values, "cross", [(i, (i + u) % cross) for i in range(cross)])
+        lax.ppermute(image_values, "cross", [(i, i ^ u) for i in range(cross)])
         for u in range(1, cross)
     ]
 
@@ -964,7 +971,7 @@
         limit=24,
     )
     (back,) = call(
-        functools.partial(solve_kernel, slices, carry_up, carry_down),
+        functools.partial(solve_kernel, slices, pencils, constants),
         [(slabs * slices.back_height, LANES)],
         [
             (slabs * slices.chunk * 48, LANES),

time: 46.7 us -> 45.8 us (0.981)
  waiting for transfers between devices: 16.2 us -> 15.1 us
    ppermute x3, waiting for transfers between devices: 3.04 us -> 2.3 us  [local(): lax.ppermute(image_values, 'cross', [(i, i ^ u) for i in range(cross)])]
where the time goes in v5:
time: 45.8 us; the launch traced here: 45.5 us
  starting transfers between devices  18.6 us (41%)
  waiting for transfers between devices  15.1 us (33%)
  Pallas kernels  11 us (24%)
  between operations  0.74 us (2%)
    all_to_all x2, starting transfers between devices, exchange(): return lax.all_to_all(message, axes, 0, 0, tiled=True)  11.5 us
    pallas_call x7, Pallas kernels, call(): pl.pallas_call(kernel, out_shape=[jax.ShapeDtypeStruct(shape, jnp.float32...  11 us
    all_to_all x2, waiting for transfers between devices, exchange(): return lax.all_to_all(message, axes, 0, 0, tiled=True)  7.96 us
    ppermute x1, waiting for transfers between devices, local(): above = lax.ppermute(down, 'pipe', [(j, i) for i, j in forward])  4.15 us
    ppermute x1, starting transfers between devices, local(): below = lax.ppermute(up, 'pipe', forward)  3.91 us
    ppermute x3, waiting for transfers between devices, local(): lax.ppermute(image_values, 'cross', [(i, i ^ u) for i in range(cross)])  2.3 us
    ppermute x3, starting transfers between devices, local(): lax.ppermute(image_values, 'cross', [(i, i ^ u) for i in range(cross)])  1.85 us
    ppermute x1, starting transfers between devices, local(): above = lax.ppermute(down, 'pipe', [(j, i) for i, j in forward])  1.29 us
  transfers between devices with their start and end apart: 7, of which 6 were waited for; matrix products, arithmetic and copies ran while one was open for 0% of the time, Pallas kernels for 7%

profile of v5, /device:TPU:0, one launch (start us, length us, event | category | flops | bytes accessed | tf_op | source)
XLA Modules:
  0.0 45.5 jit_solution(15415595426544230641)
XLA Ops:
  0.6 0.0 copy-start.2
  0.6 0.0 copy-start
  0.7 4.8 %shard_map.113 = (f32[832,128]{1,0:T(8,128)}, f32[1664,128]{1,0:T(8,128)}, f32[96,128]{1,0:T(8,128)}, f32[96,128]{1,0:T(8,128)}) custom-call(f32[16,2304]{1,0:T(8,128)} %face_hbm.1, f32[16,2304]{1,0:T(8,128)} %courant_hbm.1, f32[8,192,128]{2,1,0:T(8,128)} %constant.2.clone.tables_hbm, s32[128]{0:T(128)} %cell_hbm.1, s32[128]{0:T(128)} %owner_hbm.1, ...), custom_call_target="tpu_custom_call" | custom-call | tf_op jit(solution)/shard_map/pallas_call | solution.py:863
  5.5 0.0 copy-start.1
  5.5 7.4 %all-to-all-start = ((f32[8,104,128]{2,1,0:T(8,128)}), f32[8,104,128]{2,1,0:T(8,128)S(1)}, u32[]{:S(2)}, u32[]{:S(2)}) async-start(f32[8,104,128]{2,1,0:T(8,128)} %bitcast.8), calls=%async_computation | async-start | bytes 851968 | tf_op jit(solution)/shard_map/all_to_all | solution.py:874
  12.9 3.9 %collective-permute-start = (f32[96,128]{1,0:T(8,128)}, f32[96,128]{1,0:T(8,128)S(1)}, u32[]{:S(2)}, u32[]{:S(2)}) collective-permute-start(f32[96,128]{1,0:T(8,128)} %get-tuple-element.12), channel_id=1, source_target_pairs={{0,4},{4,8},{8,12},{12,16},{16,20},{20,24},{24,28},{1,5},{5,9},{9,... | collective-permute-start | bytes 147464 | tf_op jit(solution)/shard_map/ppermute | solution.py:938
  16.9 1.3 %collective-permute-start.1 = (f32[96,128]{1,0:T(8,128)}, f32[96,128]{1,0:T(8,128)S(1)}, u32[]{:S(2)}, u32[]{:S(2)}) collective-permute-start(f32[96,128]{1,0:T(8,128)} %get-tuple-element.13), channel_id=1, source_target_pairs={{4,0},{8,4},{12,8},{16,12},{20,16},{24,20},{28,24},{5,1},{9,5},{13... | collective-permute-start | bytes 147464 | tf_op jit(solution)/shard_map/ppermute | solution.py:939
  18.2 0.7 %collective-permute-done.below_ref = f32[96,128]{1,0:T(8,128)S(1)} collective-permute-done((f32[96,128]{1,0:T(8,128)}, f32[96,128]{1,0:T(8,128)S(1)}, u32[]{:S(2)}, u32[]{:S(2)}) %collective-permute-start) | collective-permute-done | bytes 49184 | tf_op jit(solution)/shard_map/ppermute | solution.py:938
  18.9 4.1 %collective-permute-done.1.above_ref = f32[96,128]{1,0:T(8,128)S(1)} collective-permute-done((f32[96,128]{1,0:T(8,128)}, f32[96,128]{1,0:T(8,128)S(1)}, u32[]{:S(2)}, u32[]{:S(2)}) %collective-permute-start.1) | collective-permute-done | bytes 49184 | tf_op jit(solution)/shard_map/ppermute | solution.py:939
  23.1 2.8 %all-to-all-done = f32[8,104,128]{2,1,0:T(8,128)S(1)} async-done(((f32[8,104,128]{2,1,0:T(8,128)}), f32[8,104,128]{2,1,0:T(8,128)S(1)}, u32[]{:S(2)}, u32[]{:S(2)}) %all-to-all-start) | async-done | bytes 426016 | tf_op jit(solution)/shard_map/all_to_all | solution.py:874
  25.9 0.0 collective-permute-start.4
  25.9 1.6 %collective-permute-start.3 = (f32[80,128]{1,0:T(8,128)S(1)}, f32[80,128]{1,0:T(8,128)S(1)}, u32[]{:S(2)}, u32[]{:S(2)}) collective-permute-start(f32[80,128]{1,0:T(8,128)S(1)} %shard_map.115.refs_0_), channel_id=1, source_target_pairs={{0,2},{1,3},{2,0},{3,1},{4,6},{5,7},{6,4},{7,5},{8,10},{9,11},{10,... | collective-permute-start | bytes 122888 | tf_op jit(solution)/shard_map/ppermute | solution.py:960
  27.4 0.3 collective-permute-start.2
  27.7 0.2 shard_map.114
  27.9 1.7 %collective-permute-done.4.refs_3_ = f32[80,128]{1,0:T(8,128)S(1)} collective-permute-done((f32[80,128]{1,0:T(8,128)S(1)}, f32[80,128]{1,0:T(8,128)S(1)}, u32[]{:S(2)}, u32[]{:S(2)}) %collective-permute-start.4) | collective-permute-done | bytes 40992 | tf_op jit(solution)/shard_map/ppermute | solution.py:960
  29.7 0.6 %collective-permute-done.3.refs_2_ = f32[80,128]{1,0:T(8,128)S(1)} collective-permute-done((f32[80,128]{1,0:T(8,128)S(1)}, f32[80,128]{1,0:T(8,128)S(1)}, u32[]{:S(2)}, u32[]{:S(2)}) %collective-permute-start.3) | collective-permute-done | bytes 40992 | tf_op jit(solution)/shard_map/ppermute | solution.py:960
  30.2 0.0 collective-permute-done.2.refs_1_
  30.2 1.6 %shard_map.116 = f32[384,128]{1,0:T(8,128)} custom-call(f32[832,128]{1,0:T(8,128)S(1)} %bitcast.6, f32[320,128]{1,0:T(8,128)S(1)} %get-tuple-element.15.rest_ref, f32[256,128]{1,0:T(8,128)S(1)} %get-tuple-element.16.chain_ref, f32[80,128]{1,0:T(8,128)S(1)} %shard_map.115.refs_0_, f32[80,128]{1,0:T(8,128)S(1)} %collective-permute-done.2.refs_1_, ...), custom_call_target="tpu_custom_call" | custom-call | tf_op jit(solution)/shard_map/pallas_call | solution.py:863
  31.9 4.1 %all-to-all-start.1 = ((f32[8,48,128]{2,1,0:T(8,128)}), f32[8,48,128]{2,1,0:T(8,128)S(1)}, u32[]{:S(2)}, u32[]{:S(2)}) async-start(f32[8,48,128]{2,1,0:T(8,128)} %bitcast.2), calls=%async_computation.1 | async-start | bytes 393216 | tf_op jit(solution)/shard_map/all_to_all | solution.py:874
  36.0 0.0 copy-done.2
  36.0 0.0 copy-done
  36.0 0.0 copy-done.1
  36.0 0.8 %shard_map.117.ready_ref = f32[4544,128]{1,0:T(8,128)S(1)} custom-call(f32[1664,128]{1,0:T(8,128)S(1)} %copy-done.1, s32[16,2304]{1,0:T(8,128)S(1)} %copy-done.2, f32[5,16,2304]{2,1,0:T(8,128)S(1)} %copy-done), custom_call_target="tpu_custom_call" | custom-call | tf_op jit(solution)/shard_map/pallas_call | solution.py:863
  36.8 2.2 %shard_map.118.done_ref = f32[4252,128]{1,0:T(8,128)S(1)} custom-call(f32[4544,128]{1,0:T(8,128)S(1)} %shard_map.117.ready_ref, f32[96,128]{1,0:T(8,128)S(1)} %collective-permute-done.below_ref, f32[96,128]{1,0:T(8,128)S(1)} %collective-permute-done.1.above_ref, f32[80,128]{1,0:T(8,128)S(1)} %shard_map.115.refs_0_, ...), custom_call_target="tpu_custom_call" | custom-call | tf_op jit(solution)/shard_map/pallas_call | solution.py:863
  39.0 5.2 %all-to-all-done.1 = f32[8,48,128]{2,1,0:T(8,128)S(1)} async-done(((f32[8,48,128]{2,1,0:T(8,128)}), f32[8,48,128]{2,1,0:T(8,128)S(1)}, u32[]{:S(2)}, u32[]{:S(2)}) %all-to-all-start.1) | async-done | bytes 196640 | tf_op jit(solution)/shard_map/all_to_all | solution.py:874
  44.2 1.3 %shard_map.119 = (f32[5,16,2304]{2,1,0:T(8,128)}, f32[5,16,2304]{2,1,0:T(8,128)}) custom-call(f32[384,128]{1,0:T(8,128)S(1)} %bitcast.7, f32[4252,128]{1,0:T(8,128)S(1)} %shard_map.118.done_ref), custom_call_target="tpu_custom_call" | custom-call | tf_op jit(solution)/shard_map/pallas_call | solution.py:863
  (1 shorter events, 0.0 us)
Async XLA Ops:
  0.6 35.3 %copy-start.2 = (s32[16,2304]{1,0:T(8,128)S(1)}, s32[16,2304]{1,0:T(8,128)}, u32[]{:S(2)}) copy-start(s32[16,2304]{1,0:T(8,128)} %mask_ref.1) | copy-start | bytes 442372
  0.6 35.3 %copy-start = (f32[5,16,2304]{2,1,0:T(8,128)S(1)}, f32[5,16,2304]{2,1,0:T(8,128)}, u32[]{:S(2)}) copy-start(f32[5,16,2304]{2,1,0:T(8,128)} %state_ref.1) | copy-start | bytes 2211844
  5.5 30.5 %copy-start.1 = (f32[1664,128]{1,0:T(8,128)S(1)}, f32[1664,128]{1,0:T(8,128)}, u32[]{:S(2)}) copy-start(f32[1664,128]{1,0:T(8,128)} %get-tuple-element.17.stay_ref) | copy-start | bytes 2555908
  5.5 20.3 %all-to-all-start = ((f32[8,104,128]{2,1,0:T(8,128)}), f32[8,104,128]{2,1,0:T(8,128)S(1)}, u32[]{:S(2)}, u32[]{:S(2)}) async-start(f32[8,104,128]{2,1,0:T(8,128)} %bitcast.8), calls=%async_computation | async-start | bytes 851968 | tf_op jit(solution)/shard_map/all_to_all | solution.py:874
  12.9 6.0 %collective-permute-start = (f32[96,128]{1,0:T(8,128)}, f32[96,128]{1,0:T(8,128)S(1)}, u32[]{:S(2)}, u32[]{:S(2)}) collective-permute-start(f32[96,128]{1,0:T(8,128)} %get-tuple-element.12), channel_id=1, source_target_pairs={{0,4},{4,8},{8,12},{12,16},{16,20},{20,24},{24,28},{1,5},{5,9},{9,... | collective-permute-start | bytes 147464 | tf_op jit(solution)/shard_map/ppermute | solution.py:938
  16.9 6.2 %collective-permute-start.1 = (f32[96,128]{1,0:T(8,128)}, f32[96,128]{1,0:T(8,128)S(1)}, u32[]{:S(2)}, u32[]{:S(2)}) collective-permute-start(f32[96,128]{1,0:T(8,128)} %get-tuple-element.13), channel_id=1, source_target_pairs={{4,0},{8,4},{12,8},{16,12},{20,16},{24,20},{28,24},{5,1},{9,5},{13... | collective-permute-start | bytes 147464 | tf_op jit(solution)/shard_map/ppermute | solution.py:939
  25.9 3.8 %collective-permute-start.4 = (f32[80,128]{1,0:T(8,128)S(1)}, f32[80,128]{1,0:T(8,128)S(1)}, u32[]{:S(2)}, u32[]{:S(2)}) collective-permute-start(f32[80,128]{1,0:T(8,128)S(1)} %shard_map.115.refs_0_), channel_id=1, source_target_pairs={{0,3},{1,2},{2,1},{3,0},{4,7},{5,6},{6,5},{7,4},{8,11},{9,10},{10,... | collective-permute-start | bytes 122888 | tf_op jit(solution)/shard_map/ppermute | solution.py:960
  25.9 4.4 %collective-permute-start.3 = (f32[80,128]{1,0:T(8,128)S(1)}, f32[80,128]{1,0:T(8,128)S(1)}, u32[]{:S(2)}, u32[]{:S(2)}) collective-permute-start(f32[80,128]{1,0:T(8,128)S(1)} %shard_map.115.refs_0_), channel_id=1, source_target_pairs={{0,2},{1,3},{2,0},{3,1},{4,6},{5,7},{6,4},{7,5},{8,10},{9,11},{10,... | collective-permute-start | bytes 122888 | tf_op jit(solution)/shard_map/ppermute | solution.py:960
  27.4 2.8 %collective-permute-start.2 = (f32[80,128]{1,0:T(8,128)S(1)}, f32[80,128]{1,0:T(8,128)S(1)}, u32[]{:S(2)}, u32[]{:S(2)}) collective-permute-start(f32[80,128]{1,0:T(8,128)S(1)} %shard_map.115.refs_0_), channel_id=1, source_target_pairs={{0,1},{1,0},{2,3},{3,2},{4,5},{5,4},{6,7},{7,6},{8,9},{9,8},{10,11... | collective-permute-start | bytes 122888 | tf_op jit(solution)/shard_map/ppermute | solution.py:960
  31.9 12.3 %all-to-all-start.1 = ((f32[8,48,128]{2,1,0:T(8,128)}), f32[8,48,128]{2,1,0:T(8,128)S(1)}, u32[]{:S(2)}, u32[]{:S(2)}) async-start(f32[8,48,128]{2,1,0:T(8,128)} %bitcast.2), calls=%async_computation.1 | async-start | bytes 393216 | tf_op jit(solution)/shard_map/all_to_all | solution.py:874

commit v6 on v5

--- a/solution.py
+++ b/solution.py
@@ -937,7 +937,6 @@
     forward = [(i, i + 1) for i in range(slabs - 1)]
     below = lax.ppermute(up, "pipe", forward)
     above = lax.ppermute(down, "pipe", [(j, i) for i, j in forward])
-    message, below, above = lax.optimization_barrier((message, below, above))
     (ready,) = call(
         own_kernel,
         [ready],
@@ -961,12 +960,13 @@
         for u in range(1, cross)
     ]
 
+    factored, below, above = lax.optimization_barrier((message, below, above))
     rest, chain = call(
         functools.partial(chain_kernel, slices),
         [(slabs * max(slices.groups, 1) * slices.per, LANES), (2 * slabs * 16, LANES)],
         [],
         [],
-        (message,),
+        (factored,),
         near=(0,),
         limit=24,
     )

time: 45.8 us -> 45.8 us (level)
    all_to_all x2, waiting for transfers between devices: 7.96 us -> 12.8 us  [exchange(): return lax.all_to_all(message, axes, 0, 0, tiled=True)]
    ppermute x1, waiting for transfers between devices: 4.15 us -> 0.01 us  [local(): above = lax.ppermute(down, 'pipe', [(j, i) for i, j in forward])]
    ppermute x1, waiting for transfers between devices: 0.75 us -> 0.01 us  [local(): below = lax.ppermute(up, 'pipe', forward)]
  transfers between devices with their start and end apart: 7 -> 7, of which waited for: 6 -> 4; matrix products, arithmetic and copies ran while one was open for 0% -> 0% of each run, Pallas kernels for 7% -> 7%
where the time goes in v6:
time: 45.8 us; the launch traced here: 45.5 us
  starting transfers between devices  18.6 us (41%)
  waiting for transfers between devices  15.1 us (33%)
  Pallas kernels  11 us (24%)
  between operations  0.74 us (2%)
    all_to_all x2, waiting for transfers between devices, exchange(): return lax.all_to_all(message, axes, 0, 0, tiled=True)  12.8 us
    all_to_all x2, starting transfers between devices, exchange(): return lax.all_to_all(message, axes, 0, 0, tiled=True)  11.5 us
    pallas_call x7, Pallas kernels, call(): pl.pallas_call(kernel, out_shape=[jax.ShapeDtypeStruct(shape, jnp.float32...  11 us
    ppermute x1, starting transfers between devices, local(): below = lax.ppermute(up, 'pipe', forward)  3.91 us
    ppermute x3, waiting for transfers between devices, local(): lax.ppermute(image_values, 'cross', [(i, i ^ u) for i in range(cross)])  2.29 us
    ppermute x3, starting transfers between devices, local(): lax.ppermute(image_values, 'cross', [(i, i ^ u) for i in range(cross)])  1.85 us
    ppermute x1, starting transfers between devices, local(): above = lax.ppermute(down, 'pipe', [(j, i) for i, j in forward])  1.29 us
  transfers between devices with their start and end apart: 7, of which 4 were waited for; matrix products, arithmetic and copies ran while one was open for 0% of the time, Pallas kernels for 7%

profile of v6, /device:TPU:0, one launch (start us, length us, event | category | flops | bytes accessed | tf_op | source)
XLA Modules:
  0.0 45.5 jit_solution(9734899470398473168)
XLA Ops:
  0.6 0.0 copy-start.2
  0.6 0.0 copy-start
  0.7 4.8 %shard_map.113 = (f32[832,128]{1,0:T(8,128)}, f32[1664,128]{1,0:T(8,128)}, f32[96,128]{1,0:T(8,128)}, f32[96,128]{1,0:T(8,128)}) custom-call(f32[16,2304]{1,0:T(8,128)} %face_hbm.1, f32[16,2304]{1,0:T(8,128)} %courant_hbm.1, f32[8,192,128]{2,1,0:T(8,128)} %constant.2.clone.tables_hbm, s32[128]{0:T(128)} %cell_hbm.1, s32[128]{0:T(128)} %owner_hbm.1, ...), custom_call_target="tpu_custom_call" | custom-call | tf_op jit(solution)/shard_map/pallas_call | solution.py:863
  5.5 0.0 copy-start.1
  5.5 7.4 %all-to-all-start = ((f32[8,104,128]{2,1,0:T(8,128)}), f32[8,104,128]{2,1,0:T(8,128)S(1)}, u32[]{:S(2)}, u32[]{:S(2)}) async-start(f32[8,104,128]{2,1,0:T(8,128)} %bitcast.8), calls=%async_computation | async-start | bytes 851968 | tf_op jit(solution)/shard_map/all_to_all | solution.py:874
  12.9 3.9 %collective-permute-start = (f32[96,128]{1,0:T(8,128)}, f32[96,128]{1,0:T(8,128)S(1)}, u32[]{:S(2)}, u32[]{:S(2)}) collective-permute-start(f32[96,128]{1,0:T(8,128)} %get-tuple-element.12), channel_id=1, source_target_pairs={{0,4},{4,8},{8,12},{12,16},{16,20},{20,24},{24,28},{1,5},{5,9},{9,... | collective-permute-start | bytes 147464 | tf_op jit(solution)/shard_map/ppermute | solution.py:938
  16.9 1.3 %collective-permute-start.1 = (f32[96,128]{1,0:T(8,128)}, f32[96,128]{1,0:T(8,128)S(1)}, u32[]{:S(2)}, u32[]{:S(2)}) collective-permute-start(f32[96,128]{1,0:T(8,128)} %get-tuple-element.13), channel_id=1, source_target_pairs={{4,0},{8,4},{12,8},{16,12},{20,16},{24,20},{28,24},{5,1},{9,5},{13... | collective-permute-start | bytes 147464 | tf_op jit(solution)/shard_map/ppermute | solution.py:939
  18.2 7.7 %all-to-all-done = f32[8,104,128]{2,1,0:T(8,128)S(1)} async-done(((f32[8,104,128]{2,1,0:T(8,128)}), f32[8,104,128]{2,1,0:T(8,128)S(1)}, u32[]{:S(2)}, u32[]{:S(2)}) %all-to-all-start) | async-done | bytes 426016 | tf_op jit(solution)/shard_map/all_to_all | solution.py:874
  25.9 0.0 collective-permute-start.4
  25.9 1.6 %collective-permute-start.3 = (f32[80,128]{1,0:T(8,128)S(1)}, f32[80,128]{1,0:T(8,128)S(1)}, u32[]{:S(2)}, u32[]{:S(2)}) collective-permute-start(f32[80,128]{1,0:T(8,128)S(1)} %shard_map.115.refs_0_), channel_id=1, source_target_pairs={{0,2},{1,3},{2,0},{3,1},{4,6},{5,7},{6,4},{7,5},{8,10},{9,11},{10,... | collective-permute-start | bytes 122888 | tf_op jit(solution)/shard_map/ppermute | solution.py:959
  27.4 0.3 collective-permute-start.2
  27.7 0.0 collective-permute-done.below_ref
  27.7 0.0 collective-permute-done.1.above_ref
  27.7 0.2 shard_map.114
  28.0 1.7 %collective-permute-done.4.refs_3_ = f32[80,128]{1,0:T(8,128)S(1)} collective-permute-done((f32[80,128]{1,0:T(8,128)S(1)}, f32[80,128]{1,0:T(8,128)S(1)}, u32[]{:S(2)}, u32[]{:S(2)}) %collective-permute-start.4) | collective-permute-done | bytes 40992 | tf_op jit(solution)/shard_map/ppermute | solution.py:959
  29.7 0.6 %collective-permute-done.3.refs_2_ = f32[80,128]{1,0:T(8,128)S(1)} collective-permute-done((f32[80,128]{1,0:T(8,128)S(1)}, f32[80,128]{1,0:T(8,128)S(1)}, u32[]{:S(2)}, u32[]{:S(2)}) %collective-permute-start.3) | collective-permute-done | bytes 40992 | tf_op jit(solution)/shard_map/ppermute | solution.py:959
  30.2 0.0 collective-permute-done.2.refs_1_
  30.2 1.6 %shard_map.116 = f32[384,128]{1,0:T(8,128)} custom-call(f32[832,128]{1,0:T(8,128)S(1)} %bitcast.6, f32[320,128]{1,0:T(8,128)S(1)} %get-tuple-element.15.rest_ref, f32[256,128]{1,0:T(8,128)S(1)} %get-tuple-element.16.chain_ref, f32[80,128]{1,0:T(8,128)S(1)} %shard_map.115.refs_0_, f32[80,128]{1,0:T(8,128)S(1)} %collective-permute-done.2.refs_1_, ...), custom_call_target="tpu_custom_call" | custom-call | tf_op jit(solution)/shard_map/pallas_call | solution.py:863
  31.9 4.1 %all-to-all-start.1 = ((f32[8,48,128]{2,1,0:T(8,128)}), f32[8,48,128]{2,1,0:T(8,128)S(1)}, u32[]{:S(2)}, u32[]{:S(2)}) async-start(f32[8,48,128]{2,1,0:T(8,128)} %bitcast.2), calls=%async_computation.1 | async-start | bytes 393216 | tf_op jit(solution)/shard_map/all_to_all | solution.py:874
  36.0 0.0 copy-done.2
  36.0 0.0 copy-done
  36.0 0.0 copy-done.1
  36.0 0.8 %shard_map.117.ready_ref = f32[4544,128]{1,0:T(8,128)S(1)} custom-call(f32[1664,128]{1,0:T(8,128)S(1)} %copy-done.1, s32[16,2304]{1,0:T(8,128)S(1)} %copy-done.2, f32[5,16,2304]{2,1,0:T(8,128)S(1)} %copy-done), custom_call_target="tpu_custom_call" | custom-call | tf_op jit(solution)/shard_map/pallas_call | solution.py:863
  36.8 2.2 %shard_map.118.done_ref = f32[4252,128]{1,0:T(8,128)S(1)} custom-call(f32[4544,128]{1,0:T(8,128)S(1)} %shard_map.117.ready_ref, f32[96,128]{1,0:T(8,128)S(1)} %collective-permute-done.below_ref, f32[96,128]{1,0:T(8,128)S(1)} %collective-permute-done.1.above_ref, f32[80,128]{1,0:T(8,128)S(1)} %shard_map.115.refs_0_, ...), custom_call_target="tpu_custom_call" | custom-call | tf_op jit(solution)/shard_map/pallas_call | solution.py:863
  39.0 5.2 %all-to-all-done.1 = f32[8,48,128]{2,1,0:T(8,128)S(1)} async-done(((f32[8,48,128]{2,1,0:T(8,128)}), f32[8,48,128]{2,1,0:T(8,128)S(1)}, u32[]{:S(2)}, u32[]{:S(2)}) %all-to-all-start.1) | async-done | bytes 196640 | tf_op jit(solution)/shard_map/all_to_all | solution.py:874
  44.2 1.3 %shard_map.119 = (f32[5,16,2304]{2,1,0:T(8,128)}, f32[5,16,2304]{2,1,0:T(8,128)}) custom-call(f32[384,128]{1,0:T(8,128)S(1)} %bitcast.7, f32[4252,128]{1,0:T(8,128)S(1)} %shard_map.118.done_ref), custom_call_target="tpu_custom_call" | custom-call | tf_op jit(solution)/shard_map/pallas_call | solution.py:863
  (1 shorter events, 0.0 us)
Async XLA Ops:
  0.6 35.3 %copy-start.2 = (s32[16,2304]{1,0:T(8,128)S(1)}, s32[16,2304]{1,0:T(8,128)}, u32[]{:S(2)}) copy-start(s32[16,2304]{1,0:T(8,128)} %mask_ref.1) | copy-start | bytes 442372
  0.6 35.3 %copy-start = (f32[5,16,2304]{2,1,0:T(8,128)S(1)}, f32[5,16,2304]{2,1,0:T(8,128)}, u32[]{:S(2)}) copy-start(f32[5,16,2304]{2,1,0:T(8,128)} %state_ref.1) | copy-start | bytes 2211844
  5.5 30.5 %copy-start.1 = (f32[1664,128]{1,0:T(8,128)S(1)}, f32[1664,128]{1,0:T(8,128)}, u32[]{:S(2)}) copy-start(f32[1664,128]{1,0:T(8,128)} %get-tuple-element.17.stay_ref) | copy-start | bytes 2555908
  5.5 20.3 %all-to-all-start = ((f32[8,104,128]{2,1,0:T(8,128)}), f32[8,104,128]{2,1,0:T(8,128)S(1)}, u32[]{:S(2)}, u32[]{:S(2)}) async-start(f32[8,104,128]{2,1,0:T(8,128)} %bitcast.8), calls=%async_computation | async-start | bytes 851968 | tf_op jit(solution)/shard_map/all_to_all | solution.py:874
  12.9 14.8 %collective-permute-start = (f32[96,128]{1,0:T(8,128)}, f32[96,128]{1,0:T(8,128)S(1)}, u32[]{:S(2)}, u32[]{:S(2)}) collective-permute-start(f32[96,128]{1,0:T(8,128)} %get-tuple-element.12), channel_id=1, source_target_pairs={{0,4},{4,8},{8,12},{12,16},{16,20},{20,24},{24,28},{1,5},{5,9},{9,... | collective-permute-start | bytes 147464 | tf_op jit(solution)/shard_map/ppermute | solution.py:938
  16.9 10.9 %collective-permute-start.1 = (f32[96,128]{1,0:T(8,128)}, f32[96,128]{1,0:T(8,128)S(1)}, u32[]{:S(2)}, u32[]{:S(2)}) collective-permute-start(f32[96,128]{1,0:T(8,128)} %get-tuple-element.13), channel_id=1, source_target_pairs={{4,0},{8,4},{12,8},{16,12},{20,16},{24,20},{28,24},{5,1},{9,5},{13... | collective-permute-start | bytes 147464 | tf_op jit(solution)/shard_map/ppermute | solution.py:939
  25.9 3.8 %collective-permute-start.4 = (f32[80,128]{1,0:T(8,128)S(1)}, f32[80,128]{1,0:T(8,128)S(1)}, u32[]{:S(2)}, u32[]{:S(2)}) collective-permute-start(f32[80,128]{1,0:T(8,128)S(1)} %shard_map.115.refs_0_), channel_id=1, source_target_pairs={{0,3},{1,2},{2,1},{3,0},{4,7},{5,6},{6,5},{7,4},{8,11},{9,10},{10,... | collective-permute-start | bytes 122888 | tf_op jit(solution)/shard_map/ppermute | solution.py:959
  25.9 4.4 %collective-permute-start.3 = (f32[80,128]{1,0:T(8,128)S(1)}, f32[80,128]{1,0:T(8,128)S(1)}, u32[]{:S(2)}, u32[]{:S(2)}) collective-permute-start(f32[80,128]{1,0:T(8,128)S(1)} %shard_map.115.refs_0_), channel_id=1, source_target_pairs={{0,2},{1,3},{2,0},{3,1},{4,6},{5,7},{6,4},{7,5},{8,10},{9,11},{10,... | collective-permute-start | bytes 122888 | tf_op jit(solution)/shard_map/ppermute | solution.py:959
  27.4 2.8 %collective-permute-start.2 = (f32[80,128]{1,0:T(8,128)S(1)}, f32[80,128]{1,0:T(8,128)S(1)}, u32[]{:S(2)}, u32[]{:S(2)}) collective-permute-start(f32[80,128]{1,0:T(8,128)S(1)} %shard_map.115.refs_0_), channel_id=1, source_target_pairs={{0,1},{1,0},{2,3},{3,2},{4,5},{5,4},{6,7},{7,6},{8,9},{9,8},{10,11... | collective-permute-start | bytes 122888 | tf_op jit(solution)/shard_map/ppermute | solution.py:959
  31.9 12.3 %all-to-all-start.1 = ((f32[8,48,128]{2,1,0:T(8,128)}), f32[8,48,128]{2,1,0:T(8,128)S(1)}, u32[]{:S(2)}, u32[]{:S(2)}) async-start(f32[8,48,128]{2,1,0:T(8,128)} %bitcast.2), calls=%async_computation.1 | async-start | bytes 393216 | tf_op jit(solution)/shard_map/all_to_all | solution.py:874

commit v7 on v6

--- a/solution.py
+++ b/solution.py
@@ -171,9 +171,15 @@
     return copies
 
 
+def middle_first(slabs):
+    return sorted(range(slabs), key=lambda p: (abs(2 * p - slabs + 1), p))
+
+
 class Slices:
     def __init__(self, slabs, count, cross, var_count, images):
         rest = count % slabs
+        order = middle_first(slabs)
+        self.place = [order.index(p) for p in range(slabs)]
         self.slabs, self.count, self.cross, self.var_count = slabs, count, cross, var_count
         self.image_rows = var_count * images // LANES
         shared = rest > 0 and slabs % rest == 0 and LANES % (slabs // rest) == 0
@@ -518,7 +524,7 @@
     height, per, width = slices.height, slices.per, slices.width
     if slices.rest:
         for p in range(slabs):
-            start = p * height + slices.packed_at
+            start = slices.place[p] * height + slices.packed_at
             packed = message_ref[start : start + slices.groups, :]
             for k in range(per):
                 rest_ref[pl.ds(p * slices.groups * per + k, slices.groups, stride=per), :] = (
@@ -528,7 +534,7 @@
         rest_ref[...] = jnp.zeros_like(rest_ref)
 
     def sent(p, which):
-        start = p * height + slices.coefficient_row(which, 0)
+        start = slices.place[p] * height + slices.coefficient_row(which, 0)
         slab = message_ref[start : start + full, :]
         if slices.rest:
             start = p * slices.groups * per + 6 * slices.var_count + which
@@ -552,10 +558,11 @@
     *blocks, back_ref, ghost_ref, back_rest_ref = refs
     slabs, var_count, chunk, full = slices.slabs, slices.var_count, slices.chunk, slices.full
     height, per, width = slices.height, slices.per, slices.width
-    me = lax.axis_index("pipe")
+    along = lax.axis_index("pipe")
+    me = sum(jnp.where(along == p, slices.place[p], 0) for p in range(slabs))
 
     def meta(p, k):
-        start = p * height + slices.meta_at + k
+        start = slices.place[p] * height + slices.meta_at + k
         return message_ref[start : start + 1, :]
 
     def meta_all(k):
@@ -602,7 +609,7 @@
 
         def value(p, functional):
             if t < full:
-                start = p * height + slices.row(functional, t)
+                start = slices.place[p] * height + slices.row(functional, t)
                 sent = message_ref[start : start + var_count, :]
             else:
                 start = p * slices.groups * per + functional * var_count
@@ -612,14 +619,14 @@
 
         def coefficient(p, which):
             if t < full:
-                start = p * height + slices.coefficient_row(which, t)
+                start = slices.place[p] * height + slices.coefficient_row(which, t)
                 return message_ref[start : start + 1, :]
             start = p * slices.groups * per + 6 * var_count + which
             return rest_ref[start : start + 1, :]
 
         def give(p, functional, block):
             if t < full:
-                start = p * slices.back_height + slices.row(functional, t)
+                start = slices.place[p] * slices.back_height + slices.row(functional, t)
                 back_ref[start : start + var_count, :] = block
             else:
                 start = p * slices.back_groups * per + functional * var_count
@@ -669,14 +676,14 @@
                 lined = back_rest_ref[pl.ds(p * groups * per + k, groups, stride=per), :]
                 moved = moved_lanes(lined, k * width)
                 packed = moved if k == 0 else jnp.where(block == k, moved, packed)
-            start = p * slices.back_height + slices.back_packed_at
+            start = slices.place[p] * slices.back_height + slices.back_packed_at
             back_ref[start : start + groups, :] = packed
 
 
 def pick_kernel(slices, message_ref, values_ref):
     size = slices.image_rows
     for p in range(slices.slabs):
-        start = p * slices.height + slices.images_at
+        start = slices.place[p] * slices.height + slices.images_at
         values_ref[p * size : (p + 1) * size, :] = message_ref[start : start + size, :]
 
 
@@ -870,8 +877,9 @@
     )(*args)
 
 
-def exchange(message, axes):
-    return lax.all_to_all(message, axes, 0, 0, tiled=True)
+def exchange(message, axis):
+    groups = [middle_first(lax.axis_size(axis))]
+    return lax.all_to_all(message, axis, 0, 0, axis_index_groups=groups, tiled=True)
 
 
 def local(

time: 45.8 us -> 42.4 us (0.926)
  waiting for transfers between devices: 15.1 us -> 12.5 us
  starting transfers between devices: 18.6 us -> 17.8 us
    all_to_all x2, waiting for transfers between devices: 12.8 us -> 10.2 us  [exchange(): lax.all_to_all(message, axis, 0, 0, axis_index_groups=groups, tiled=True)]
    ppermute x1, starting transfers between devices: 3.91 us -> 2.46 us  [local(): below = lax.ppermute(up, 'pipe', forward)]
    all_to_all x2, starting transfers between devices: 11.5 us -> 12.2 us  [exchange(): lax.all_to_all(message, axis, 0, 0, axis_index_groups=groups, tiled=True)]
  transfers between devices with their start and end apart: 7 -> 7, of which waited for: 4 -> 4; matrix products, arithmetic and copies ran while one was open for 0% -> 0% of each run, Pallas kernels for 7% -> 8%
where the time goes in v7:
time: 42.4 us; the launch traced here: 42 us
  starting transfers between devices  17.8 us (42%)
  waiting for transfers between devices  12.5 us (29%)
  Pallas kernels  11 us (26%)
  between operations  0.73 us (2%)
    all_to_all x2, starting transfers between devices, exchange(): lax.all_to_all(message, axis, 0, 0, axis_index_groups=groups, tiled=True)  12.2 us
    pallas_call x7, Pallas kernels, call(): pl.pallas_call(kernel, out_shape=[jax.ShapeDtypeStruct(shape, jnp.float32...  11 us
    all_to_all x2, waiting for transfers between devices, exchange(): lax.all_to_all(message, axis, 0, 0, axis_index_groups=groups, tiled=True)  10.2 us
    ppermute x1, starting transfers between devices, local(): below = lax.ppermute(up, 'pipe', forward)  2.46 us
    ppermute x3, waiting for transfers between devices, local(): lax.ppermute(image_values, 'cross', [(i, i ^ u) for i in range(cross)])  2.29 us
    ppermute x3, starting transfers between devices, local(): lax.ppermute(image_values, 'cross', [(i, i ^ u) for i in range(cross)])  1.85 us
    ppermute x1, starting transfers between devices, local(): above = lax.ppermute(down, 'pipe', [(j, i) for i, j in forward])  1.29 us
  transfers between devices with their start and end apart: 7, of which 4 were waited for; matrix products, arithmetic and copies ran while one was open for 0% of the time, Pallas kernels for 8%

profile of v7, /device:TPU:0, one launch (start us, length us, event | category | flops | bytes accessed | tf_op | source)
XLA Modules:
  0.0 42.0 jit_solution(3746277858214829183)
XLA Ops:
  0.6 0.0 copy-start.2
  0.6 0.0 copy-start
  0.7 4.8 %shard_map.113 = (f32[832,128]{1,0:T(8,128)}, f32[1664,128]{1,0:T(8,128)}, f32[96,128]{1,0:T(8,128)}, f32[96,128]{1,0:T(8,128)}) custom-call(f32[16,2304]{1,0:T(8,128)} %face_hbm.1, f32[16,2304]{1,0:T(8,128)} %courant_hbm.1, f32[8,192,128]{2,1,0:T(8,128)} %constant.2.clone.tables_hbm, s32[128]{0:T(128)} %cell_hbm.1, s32[128]{0:T(128)} %owner_hbm.1, ...), custom_call_target="tpu_custom_call" | custom-call | tf_op jit(solution)/shard_map/pallas_call | solution.py:870
  5.5 0.0 copy-start.1
  5.5 8.0 %all-to-all-start = ((f32[8,104,128]{2,1,0:T(8,128)}), f32[8,104,128]{2,1,0:T(8,128)S(1)}, u32[]{:S(2)}, u32[]{:S(2)}) async-start(f32[8,104,128]{2,1,0:T(8,128)} %bitcast.8), calls=%async_computation | async-start | bytes 851968 | tf_op jit(solution)/shard_map/all_to_all | solution.py:882
  13.5 2.5 %collective-permute-start = (f32[96,128]{1,0:T(8,128)}, f32[96,128]{1,0:T(8,128)S(1)}, u32[]{:S(2)}, u32[]{:S(2)}) collective-permute-start(f32[96,128]{1,0:T(8,128)} %get-tuple-element.12), channel_id=1, source_target_pairs={{0,4},{4,8},{8,12},{12,16},{16,20},{20,24},{24,28},{1,5},{5,9},{9,... | collective-permute-start | bytes 147464 | tf_op jit(solution)/shard_map/ppermute | solution.py:946
  16.0 1.3 %collective-permute-start.1 = (f32[96,128]{1,0:T(8,128)}, f32[96,128]{1,0:T(8,128)S(1)}, u32[]{:S(2)}, u32[]{:S(2)}) collective-permute-start(f32[96,128]{1,0:T(8,128)} %get-tuple-element.13), channel_id=1, source_target_pairs={{4,0},{8,4},{12,8},{16,12},{20,16},{24,20},{28,24},{5,1},{9,5},{13... | collective-permute-start | bytes 147464 | tf_op jit(solution)/shard_map/ppermute | solution.py:947
  17.3 7.1 %all-to-all-done = f32[8,104,128]{2,1,0:T(8,128)S(1)} async-done(((f32[8,104,128]{2,1,0:T(8,128)}), f32[8,104,128]{2,1,0:T(8,128)S(1)}, u32[]{:S(2)}, u32[]{:S(2)}) %all-to-all-start) | async-done | bytes 426016 | tf_op jit(solution)/shard_map/all_to_all | solution.py:882
  24.4 0.0 collective-permute-start.4
  24.4 1.6 %collective-permute-start.3 = (f32[80,128]{1,0:T(8,128)S(1)}, f32[80,128]{1,0:T(8,128)S(1)}, u32[]{:S(2)}, u32[]{:S(2)}) collective-permute-start(f32[80,128]{1,0:T(8,128)S(1)} %shard_map.115.refs_0_), channel_id=1, source_target_pairs={{0,2},{1,3},{2,0},{3,1},{4,6},{5,7},{6,4},{7,5},{8,10},{9,11},{10,... | collective-permute-start | bytes 122888 | tf_op jit(solution)/shard_map/ppermute | solution.py:967
  26.0 0.3 collective-permute-start.2
  26.3 0.0 collective-permute-done.below_ref
  26.3 0.0 collective-permute-done.1.above_ref
  26.3 0.2 shard_map.114
  26.5 1.7 %collective-permute-done.4.refs_3_ = f32[80,128]{1,0:T(8,128)S(1)} collective-permute-done((f32[80,128]{1,0:T(8,128)S(1)}, f32[80,128]{1,0:T(8,128)S(1)}, u32[]{:S(2)}, u32[]{:S(2)}) %collective-permute-start.4) | collective-permute-done | bytes 40992 | tf_op jit(solution)/shard_map/ppermute | solution.py:967
  28.2 0.6 %collective-permute-done.3.refs_2_ = f32[80,128]{1,0:T(8,128)S(1)} collective-permute-done((f32[80,128]{1,0:T(8,128)S(1)}, f32[80,128]{1,0:T(8,128)S(1)}, u32[]{:S(2)}, u32[]{:S(2)}) %collective-permute-start.3) | collective-permute-done | bytes 40992 | tf_op jit(solution)/shard_map/ppermute | solution.py:967
  28.8 0.0 collective-permute-done.2.refs_1_
  28.8 1.7 %shard_map.116 = f32[384,128]{1,0:T(8,128)} custom-call(f32[832,128]{1,0:T(8,128)S(1)} %bitcast.6, f32[320,128]{1,0:T(8,128)S(1)} %get-tuple-element.15.rest_ref, f32[256,128]{1,0:T(8,128)S(1)} %get-tuple-element.16.chain_ref, f32[80,128]{1,0:T(8,128)S(1)} %shard_map.115.refs_0_, f32[80,128]{1,0:T(8,128)S(1)} %collective-permute-done.2.refs_1_, ...), custom_call_target="tpu_custom_call" | custom-call | tf_op jit(solution)/shard_map/pallas_call | solution.py:870
  30.4 4.2 %all-to-all-start.1 = ((f32[8,48,128]{2,1,0:T(8,128)}), f32[8,48,128]{2,1,0:T(8,128)S(1)}, u32[]{:S(2)}, u32[]{:S(2)}) async-start(f32[8,48,128]{2,1,0:T(8,128)} %bitcast.2), calls=%async_computation.1 | async-start | bytes 393216 | tf_op jit(solution)/shard_map/all_to_all | solution.py:882
  34.6 0.0 copy-done.2
  34.6 0.0 copy-done
  34.6 0.0 copy-done.1
  34.6 0.8 %shard_map.117.ready_ref = f32[4544,128]{1,0:T(8,128)S(1)} custom-call(f32[1664,128]{1,0:T(8,128)S(1)} %copy-done.1, s32[16,2304]{1,0:T(8,128)S(1)} %copy-done.2, f32[5,16,2304]{2,1,0:T(8,128)S(1)} %copy-done), custom_call_target="tpu_custom_call" | custom-call | tf_op jit(solution)/shard_map/pallas_call | solution.py:870
  35.4 2.2 %shard_map.118.done_ref = f32[4252,128]{1,0:T(8,128)S(1)} custom-call(f32[4544,128]{1,0:T(8,128)S(1)} %shard_map.117.ready_ref, f32[96,128]{1,0:T(8,128)S(1)} %collective-permute-done.below_ref, f32[96,128]{1,0:T(8,128)S(1)} %collective-permute-done.1.above_ref, f32[80,128]{1,0:T(8,128)S(1)} %shard_map.115.refs_0_, ...), custom_call_target="tpu_custom_call" | custom-call | tf_op jit(solution)/shard_map/pallas_call | solution.py:870
  37.7 3.1 %all-to-all-done.1 = f32[8,48,128]{2,1,0:T(8,128)S(1)} async-done(((f32[8,48,128]{2,1,0:T(8,128)}), f32[8,48,128]{2,1,0:T(8,128)S(1)}, u32[]{:S(2)}, u32[]{:S(2)}) %all-to-all-start.1) | async-done | bytes 196640 | tf_op jit(solution)/shard_map/all_to_all | solution.py:882
  40.7 1.3 %shard_map.119 = (f32[5,16,2304]{2,1,0:T(8,128)}, f32[5,16,2304]{2,1,0:T(8,128)}) custom-call(f32[384,128]{1,0:T(8,128)S(1)} %bitcast.7, f32[4252,128]{1,0:T(8,128)S(1)} %shard_map.118.done_ref), custom_call_target="tpu_custom_call" | custom-call | tf_op jit(solution)/shard_map/pallas_call | solution.py:870
  (1 shorter events, 0.0 us)
Async XLA Ops:
  0.6 34.0 %copy-start.2 = (s32[16,2304]{1,0:T(8,128)S(1)}, s32[16,2304]{1,0:T(8,128)}, u32[]{:S(2)}) copy-start(s32[16,2304]{1,0:T(8,128)} %mask_ref.1) | copy-start | bytes 442372
  0.6 34.0 %copy-start = (f32[5,16,2304]{2,1,0:T(8,128)S(1)}, f32[5,16,2304]{2,1,0:T(8,128)}, u32[]{:S(2)}) copy-start(f32[5,16,2304]{2,1,0:T(8,128)} %state_ref.1) | copy-start | bytes 2211844
  5.5 29.1 %copy-start.1 = (f32[1664,128]{1,0:T(8,128)S(1)}, f32[1664,128]{1,0:T(8,128)}, u32[]{:S(2)}) copy-start(f32[1664,128]{1,0:T(8,128)} %get-tuple-element.17.stay_ref) | copy-start | bytes 2555908
  5.5 18.9 %all-to-all-start = ((f32[8,104,128]{2,1,0:T(8,128)}), f32[8,104,128]{2,1,0:T(8,128)S(1)}, u32[]{:S(2)}, u32[]{:S(2)}) async-start(f32[8,104,128]{2,1,0:T(8,128)} %bitcast.8), calls=%async_computation | async-start | bytes 851968 | tf_op jit(solution)/shard_map/all_to_all | solution.py:882
  13.5 12.7 %collective-permute-start = (f32[96,128]{1,0:T(8,128)}, f32[96,128]{1,0:T(8,128)S(1)}, u32[]{:S(2)}, u32[]{:S(2)}) collective-permute-start(f32[96,128]{1,0:T(8,128)} %get-tuple-element.12), channel_id=1, source_target_pairs={{0,4},{4,8},{8,12},{12,16},{16,20},{20,24},{24,28},{1,5},{5,9},{9,... | collective-permute-start | bytes 147464 | tf_op jit(solution)/shard_map/ppermute | solution.py:946
  16.0 10.3 %collective-permute-start.1 = (f32[96,128]{1,0:T(8,128)}, f32[96,128]{1,0:T(8,128)S(1)}, u32[]{:S(2)}, u32[]{:S(2)}) collective-permute-start(f32[96,128]{1,0:T(8,128)} %get-tuple-element.13), channel_id=1, source_target_pairs={{4,0},{8,4},{12,8},{16,12},{20,16},{24,20},{28,24},{5,1},{9,5},{13... | collective-permute-start | bytes 147464 | tf_op jit(solution)/shard_map/ppermute | solution.py:947
  24.4 3.8 %collective-permute-start.4 = (f32[80,128]{1,0:T(8,128)S(1)}, f32[80,128]{1,0:T(8,128)S(1)}, u32[]{:S(2)}, u32[]{:S(2)}) collective-permute-start(f32[80,128]{1,0:T(8,128)S(1)} %shard_map.115.refs_0_), channel_id=1, source_target_pairs={{0,3},{1,2},{2,1},{3,0},{4,7},{5,6},{6,5},{7,4},{8,11},{9,10},{10,... | collective-permute-start | bytes 122888 | tf_op jit(solution)/shard_map/ppermute | solution.py:967
  24.4 4.4 %collective-permute-start.3 = (f32[80,128]{1,0:T(8,128)S(1)}, f32[80,128]{1,0:T(8,128)S(1)}, u32[]{:S(2)}, u32[]{:S(2)}) collective-permute-start(f32[80,128]{1,0:T(8,128)S(1)} %shard_map.115.refs_0_), channel_id=1, source_target_pairs={{0,2},{1,3},{2,0},{3,1},{4,6},{5,7},{6,4},{7,5},{8,10},{9,11},{10,... | collective-permute-start | bytes 122888 | tf_op jit(solution)/shard_map/ppermute | solution.py:967
  26.0 2.8 %collective-permute-start.2 = (f32[80,128]{1,0:T(8,128)S(1)}, f32[80,128]{1,0:T(8,128)S(1)}, u32[]{:S(2)}, u32[]{:S(2)}) collective-permute-start(f32[80,128]{1,0:T(8,128)S(1)} %shard_map.115.refs_0_), channel_id=1, source_target_pairs={{0,1},{1,0},{2,3},{3,2},{4,5},{5,4},{6,7},{7,6},{8,9},{9,8},{10,11... | collective-permute-start | bytes 122888 | tf_op jit(solution)/shard_map/ppermute | solution.py:967
  30.4 10.3 %all-to-all-start.1 = ((f32[8,48,128]{2,1,0:T(8,128)}), f32[8,48,128]{2,1,0:T(8,128)S(1)}, u32[]{:S(2)}, u32[]{:S(2)}) async-start(f32[8,48,128]{2,1,0:T(8,128)} %bitcast.2), calls=%async_computation.1 | async-start | bytes 393216 | tf_op jit(solution)/shard_map/all_to_all | solution.py:882

commit v8 on v7

--- a/solution.py
+++ b/solution.py
@@ -171,14 +171,19 @@
     return copies
 
 
-def middle_first(slabs):
-    return sorted(range(slabs), key=lambda p: (abs(2 * p - slabs + 1), p))
+def exchange_order(slabs):
+    near = sorted(range(slabs), key=lambda p: (abs(p - (slabs * 5) // 8), p))
+    upper = [p for p in near if p >= slabs // 2]
+    lower = [p for p in reversed(range(slabs // 2))]
+    if slabs == 8:
+        upper, lower = [5, 4, 6, 7], [2, 3, 1, 0]
+    return [p for pair in zip(upper, lower) for p in pair]
 
 
 class Slices:
     def __init__(self, slabs, count, cross, var_count, images):
         rest = count % slabs
-        order = middle_first(slabs)
+        order = exchange_order(slabs)
         self.place = [order.index(p) for p in range(slabs)]
         self.slabs, self.count, self.cross, self.var_count = slabs, count, cross, var_count
         self.image_rows = var_count * images // LANES
@@ -878,7 +883,7 @@
 
 
 def exchange(message, axis):
-    groups = [middle_first(lax.axis_size(axis))]
+    groups = [exchange_order(lax.axis_size(axis))]
     return lax.all_to_all(message, axis, 0, 0, axis_index_groups=groups, tiled=True)
 
 

time: 42.4 us -> 42.9 us (1.012)
  starting transfers between devices: 17.8 us -> 19.9 us
  waiting for transfers between devices: 12.5 us -> 10.8 us
    all_to_all x2, starting transfers between devices: 12.2 us -> 14.3 us  [exchange(): lax.all_to_all(message, axis, 0, 0, axis_index_groups=groups, tiled=True)]
    all_to_all x2, waiting for transfers between devices: 10.2 us -> 8.54 us  [exchange(): lax.all_to_all(message, axis, 0, 0, axis_index_groups=groups, tiled=True)]
where the time goes in v8:
time: 42.9 us; the launch traced here: 42.5 us
  starting transfers between devices  19.9 us (46%)
  Pallas kernels  11 us (26%)
  waiting for transfers between devices  10.8 us (25%)
  between operations  0.73 us (2%)
    all_to_all x2, starting transfers between devices, exchange(): lax.all_to_all(message, axis, 0, 0, axis_index_groups=groups, tiled=True)  14.3 us
    pallas_call x7, Pallas kernels, call(): pl.pallas_call(kernel, out_shape=[jax.ShapeDtypeStruct(shape, jnp.float32...  11 us
    all_to_all x2, waiting for transfers between devices, exchange(): lax.all_to_all(message, axis, 0, 0, axis_index_groups=groups, tiled=True)  8.54 us
    ppermute x1, starting transfers between devices, local(): below = lax.ppermute(up, 'pipe', forward)  2.44 us
    ppermute x3, waiting for transfers between devices, local(): lax.ppermute(image_values, 'cross', [(i, i ^ u) for i in range(cross)])  2.29 us
    ppermute x3, starting transfers between devices, local(): lax.ppermute(image_values, 'cross', [(i, i ^ u) for i in range(cross)])  1.85 us
    ppermute x1, starting transfers between devices, local(): above = lax.ppermute(down, 'pipe', [(j, i) for i, j in forward])  1.29 us
  transfers between devices with their start and end apart: 7, of which 4 were waited for; matrix products, arithmetic and copies ran while one was open for 0% of the time, Pallas kernels for 8%

profile of v8, /device:TPU:0, one launch (start us, length us, event | category | flops | bytes accessed | tf_op | source)
XLA Modules:
  0.0 42.5 jit_solution(8426468684484408326)
XLA Ops:
  0.6 0.0 copy-start.2
  0.6 0.0 copy-start
  0.7 4.8 %shard_map.113 = (f32[832,128]{1,0:T(8,128)}, f32[1664,128]{1,0:T(8,128)}, f32[96,128]{1,0:T(8,128)}, f32[96,128]{1,0:T(8,128)}) custom-call(f32[16,2304]{1,0:T(8,128)} %face_hbm.1, f32[16,2304]{1,0:T(8,128)} %courant_hbm.1, f32[8,192,128]{2,1,0:T(8,128)} %constant.2.clone.tables_hbm, s32[128]{0:T(128)} %cell_hbm.1, s32[128]{0:T(128)} %owner_hbm.1, ...), custom_call_target="tpu_custom_call" | custom-call | tf_op jit(solution)/shard_map/pallas_call | solution.py:875
  5.5 0.0 copy-start.1
  5.5 8.5 %all-to-all-start = ((f32[8,104,128]{2,1,0:T(8,128)}), f32[8,104,128]{2,1,0:T(8,128)S(1)}, u32[]{:S(2)}, u32[]{:S(2)}) async-start(f32[8,104,128]{2,1,0:T(8,128)} %bitcast.8), calls=%async_computation | async-start | bytes 851968 | tf_op jit(solution)/shard_map/all_to_all | solution.py:887
  14.1 2.4 %collective-permute-start = (f32[96,128]{1,0:T(8,128)}, f32[96,128]{1,0:T(8,128)S(1)}, u32[]{:S(2)}, u32[]{:S(2)}) collective-permute-start(f32[96,128]{1,0:T(8,128)} %get-tuple-element.12), channel_id=1, source_target_pairs={{0,4},{4,8},{8,12},{12,16},{16,20},{20,24},{24,28},{1,5},{5,9},{9,... | collective-permute-start | bytes 147464 | tf_op jit(solution)/shard_map/ppermute | solution.py:951
  16.5 1.3 %collective-permute-start.1 = (f32[96,128]{1,0:T(8,128)}, f32[96,128]{1,0:T(8,128)S(1)}, u32[]{:S(2)}, u32[]{:S(2)}) collective-permute-start(f32[96,128]{1,0:T(8,128)} %get-tuple-element.13), channel_id=1, source_target_pairs={{4,0},{8,4},{12,8},{16,12},{20,16},{24,20},{28,24},{5,1},{9,5},{13... | collective-permute-start | bytes 147464 | tf_op jit(solution)/shard_map/ppermute | solution.py:952
  17.8 6.4 %all-to-all-done = f32[8,104,128]{2,1,0:T(8,128)S(1)} async-done(((f32[8,104,128]{2,1,0:T(8,128)}), f32[8,104,128]{2,1,0:T(8,128)S(1)}, u32[]{:S(2)}, u32[]{:S(2)}) %all-to-all-start) | async-done | bytes 426016 | tf_op jit(solution)/shard_map/all_to_all | solution.py:887
  24.2 0.0 collective-permute-start.4
  24.2 1.6 %collective-permute-start.3 = (f32[80,128]{1,0:T(8,128)S(1)}, f32[80,128]{1,0:T(8,128)S(1)}, u32[]{:S(2)}, u32[]{:S(2)}) collective-permute-start(f32[80,128]{1,0:T(8,128)S(1)} %shard_map.115.refs_0_), channel_id=1, source_target_pairs={{0,2},{1,3},{2,0},{3,1},{4,6},{5,7},{6,4},{7,5},{8,10},{9,11},{10,... | collective-permute-start | bytes 122888 | tf_op jit(solution)/shard_map/ppermute | solution.py:972
  25.8 0.3 collective-permute-start.2
  26.1 0.0 collective-permute-done.below_ref
  26.1 0.0 collective-permute-done.1.above_ref
  26.1 0.2 shard_map.114
  26.3 1.7 %collective-permute-done.4.refs_3_ = f32[80,128]{1,0:T(8,128)S(1)} collective-permute-done((f32[80,128]{1,0:T(8,128)S(1)}, f32[80,128]{1,0:T(8,128)S(1)}, u32[]{:S(2)}, u32[]{:S(2)}) %collective-permute-start.4) | collective-permute-done | bytes 40992 | tf_op jit(solution)/shard_map/ppermute | solution.py:972
  28.0 0.6 %collective-permute-done.3.refs_2_ = f32[80,128]{1,0:T(8,128)S(1)} collective-permute-done((f32[80,128]{1,0:T(8,128)S(1)}, f32[80,128]{1,0:T(8,128)S(1)}, u32[]{:S(2)}, u32[]{:S(2)}) %collective-permute-start.3) | collective-permute-done | bytes 40992 | tf_op jit(solution)/shard_map/ppermute | solution.py:972
  28.6 0.0 collective-permute-done.2.refs_1_
  28.6 1.7 %shard_map.116 = f32[384,128]{1,0:T(8,128)} custom-call(f32[832,128]{1,0:T(8,128)S(1)} %bitcast.6, f32[320,128]{1,0:T(8,128)S(1)} %get-tuple-element.15.rest_ref, f32[256,128]{1,0:T(8,128)S(1)} %get-tuple-element.16.chain_ref, f32[80,128]{1,0:T(8,128)S(1)} %shard_map.115.refs_0_, f32[80,128]{1,0:T(8,128)S(1)} %collective-permute-done.2.refs_1_, ...), custom_call_target="tpu_custom_call" | custom-call | tf_op jit(solution)/shard_map/pallas_call | solution.py:875
  30.3 5.8 %all-to-all-start.1 = ((f32[8,48,128]{2,1,0:T(8,128)}), f32[8,48,128]{2,1,0:T(8,128)S(1)}, u32[]{:S(2)}, u32[]{:S(2)}) async-start(f32[8,48,128]{2,1,0:T(8,128)} %bitcast.2), calls=%async_computation.1 | async-start | bytes 393216 | tf_op jit(solution)/shard_map/all_to_all | solution.py:887
  36.1 0.0 copy-done.2
  36.1 0.0 copy-done
  36.1 0.0 copy-done.1
  36.1 0.8 %shard_map.117.ready_ref = f32[4544,128]{1,0:T(8,128)S(1)} custom-call(f32[1664,128]{1,0:T(8,128)S(1)} %copy-done.1, s32[16,2304]{1,0:T(8,128)S(1)} %copy-done.2, f32[5,16,2304]{2,1,0:T(8,128)S(1)} %copy-done), custom_call_target="tpu_custom_call" | custom-call | tf_op jit(solution)/shard_map/pallas_call | solution.py:875
  36.9 2.2 %shard_map.118.done_ref = f32[4252,128]{1,0:T(8,128)S(1)} custom-call(f32[4544,128]{1,0:T(8,128)S(1)} %shard_map.117.ready_ref, f32[96,128]{1,0:T(8,128)S(1)} %collective-permute-done.below_ref, f32[96,128]{1,0:T(8,128)S(1)} %collective-permute-done.1.above_ref, f32[80,128]{1,0:T(8,128)S(1)} %shard_map.115.refs_0_, ...), custom_call_target="tpu_custom_call" | custom-call | tf_op jit(solution)/shard_map/pallas_call | solution.py:875
  39.1 2.1 %all-to-all-done.1 = f32[8,48,128]{2,1,0:T(8,128)S(1)} async-done(((f32[8,48,128]{2,1,0:T(8,128)}), f32[8,48,128]{2,1,0:T(8,128)S(1)}, u32[]{:S(2)}, u32[]{:S(2)}) %all-to-all-start.1) | async-done | bytes 196640 | tf_op jit(solution)/shard_map/all_to_all | solution.py:887
  41.2 1.3 %shard_map.119 = (f32[5,16,2304]{2,1,0:T(8,128)}, f32[5,16,2304]{2,1,0:T(8,128)}) custom-call(f32[384,128]{1,0:T(8,128)S(1)} %bitcast.7, f32[4252,128]{1,0:T(8,128)S(1)} %shard_map.118.done_ref), custom_call_target="tpu_custom_call" | custom-call | tf_op jit(solution)/shard_map/pallas_call | solution.py:875
  (1 shorter events, 0.0 us)
Async XLA Ops:
  0.6 35.4 %copy-start.2 = (s32[16,2304]{1,0:T(8,128)S(1)}, s32[16,2304]{1,0:T(8,128)}, u32[]{:S(2)}) copy-start(s32[16,2304]{1,0:T(8,128)} %mask_ref.1) | copy-start | bytes 442372
  0.6 35.4 %copy-start = (f32[5,16,2304]{2,1,0:T(8,128)S(1)}, f32[5,16,2304]{2,1,0:T(8,128)}, u32[]{:S(2)}) copy-start(f32[5,16,2304]{2,1,0:T(8,128)} %state_ref.1) | copy-start | bytes 2211844
  5.5 30.6 %copy-start.1 = (f32[1664,128]{1,0:T(8,128)S(1)}, f32[1664,128]{1,0:T(8,128)}, u32[]{:S(2)}) copy-start(f32[1664,128]{1,0:T(8,128)} %get-tuple-element.17.stay_ref) | copy-start | bytes 2555908
  5.5 18.7 %all-to-all-start = ((f32[8,104,128]{2,1,0:T(8,128)}), f32[8,104,128]{2,1,0:T(8,128)S(1)}, u32[]{:S(2)}, u32[]{:S(2)}) async-start(f32[8,104,128]{2,1,0:T(8,128)} %bitcast.8), calls=%async_computation | async-start | bytes 851968 | tf_op jit(solution)/shard_map/all_to_all | solution.py:887
  14.1 12.0 %collective-permute-start = (f32[96,128]{1,0:T(8,128)}, f32[96,128]{1,0:T(8,128)S(1)}, u32[]{:S(2)}, u32[]{:S(2)}) collective-permute-start(f32[96,128]{1,0:T(8,128)} %get-tuple-element.12), channel_id=1, source_target_pairs={{0,4},{4,8},{8,12},{12,16},{16,20},{20,24},{24,28},{1,5},{5,9},{9,... | collective-permute-start | bytes 147464 | tf_op jit(solution)/shard_map/ppermute | solution.py:951
  16.5 9.6 %collective-permute-start.1 = (f32[96,128]{1,0:T(8,128)}, f32[96,128]{1,0:T(8,128)S(1)}, u32[]{:S(2)}, u32[]{:S(2)}) collective-permute-start(f32[96,128]{1,0:T(8,128)} %get-tuple-element.13), channel_id=1, source_target_pairs={{4,0},{8,4},{12,8},{16,12},{20,16},{24,20},{28,24},{5,1},{9,5},{13... | collective-permute-start | bytes 147464 | tf_op jit(solution)/shard_map/ppermute | solution.py:952
  24.2 3.8 %collective-permute-start.4 = (f32[80,128]{1,0:T(8,128)S(1)}, f32[80,128]{1,0:T(8,128)S(1)}, u32[]{:S(2)}, u32[]{:S(2)}) collective-permute-start(f32[80,128]{1,0:T(8,128)S(1)} %shard_map.115.refs_0_), channel_id=1, source_target_pairs={{0,3},{1,2},{2,1},{3,0},{4,7},{5,6},{6,5},{7,4},{8,11},{9,10},{10,... | collective-permute-start | bytes 122888 | tf_op jit(solution)/shard_map/ppermute | solution.py:972
  24.2 4.4 %collective-permute-start.3 = (f32[80,128]{1,0:T(8,128)S(1)}, f32[80,128]{1,0:T(8,128)S(1)}, u32[]{:S(2)}, u32[]{:S(2)}) collective-permute-start(f32[80,128]{1,0:T(8,128)S(1)} %shard_map.115.refs_0_), channel_id=1, source_target_pairs={{0,2},{1,3},{2,0},{3,1},{4,6},{5,7},{6,4},{7,5},{8,10},{9,11},{10,... | collective-permute-start | bytes 122888 | tf_op jit(solution)/shard_map/ppermute | solution.py:972
  25.8 2.8 %collective-permute-start.2 = (f32[80,128]{1,0:T(8,128)S(1)}, f32[80,128]{1,0:T(8,128)S(1)}, u32[]{:S(2)}, u32[]{:S(2)}) collective-permute-start(f32[80,128]{1,0:T(8,128)S(1)} %shard_map.115.refs_0_), channel_id=1, source_target_pairs={{0,1},{1,0},{2,3},{3,2},{4,5},{5,4},{6,7},{7,6},{8,9},{9,8},{10,11... | collective-permute-start | bytes 122888 | tf_op jit(solution)/shard_map/ppermute | solution.py:972
  30.3 11.0 %all-to-all-start.1 = ((f32[8,48,128]{2,1,0:T(8,128)}), f32[8,48,128]{2,1,0:T(8,128)S(1)}, u32[]{:S(2)}, u32[]{:S(2)}) async-start(f32[8,48,128]{2,1,0:T(8,128)} %bitcast.2), calls=%async_computation.1 | async-start | bytes 393216 | tf_op jit(solution)/shard_map/all_to_all | solution.py:887

commit v9 on v7

--- a/solution.py
+++ b/solution.py
@@ -106,7 +106,14 @@
 
 
 def full_dot(a, b):
-    return jnp.dot(a, b, precision=lax.Precision.HIGHEST, preferred_element_type=jnp.float32)
+    size = a.shape[0]
+    stacked = jnp.concatenate(split(a, 3), axis=0)
+    terms = []
+    for k, part in enumerate(split(b, 3)):
+        found = jnp.dot(stacked[: (3 - k) * size], part, preferred_element_type=jnp.float32)
+        terms += [found[i * size : (i + 1) * size] for i in range(3 - k)]
+    largest, ab, ac, ba, bb, ca = terms
+    return largest + ((ab + ba) + (bb + (ac + ca)))
 
 
 def marks(shape, axis, values):
@@ -224,11 +231,15 @@
     row_at = lax.broadcasted_iota(jnp.int32, (rows, images), 0)
     lower, upper = row_at == row, row_at == row + 1
     total = [jnp.zeros((rows, images), jnp.float32) for _ in range(var_count)]
+    cells = var_count * rows
     pieces = jnp.concatenate(split(x, 2), axis=0)
-    for corner, shift in enumerate((0, 1, LINE, LINE + 1)):
-        moved = pieces if shift == 0 else pltpu.roll(pieces, pencils - shift, 1)
-        found = jnp.dot(moved, pick_ref[...], preferred_element_type=jnp.float32)
-        found = found[: var_count * rows] + found[var_count * rows :]
+    moved = [pieces] + [pltpu.roll(pieces, pencils - s, 1) for s in (1, LINE, LINE + 1)]
+    all_found = jnp.dot(
+        jnp.concatenate(moved, axis=0), pick_ref[...], preferred_element_type=jnp.float32
+    )
+    for corner in range(4):
+        start = 2 * corner * cells
+        found = all_found[start : start + cells] + all_found[start + cells : start + 2 * cells]
         weight = jnp.where(lower, weight_ref[corner : corner + 1], 0.0) + jnp.where(
             upper, weight_ref[corner + 4 : corner + 5], 0.0
         )

time: 42.4 us -> 42.7 us (level)
  no operation moved by 1% of the time
where the time goes in v9:
time: 42.7 us; the launch traced here: 42.3 us
  starting transfers between devices  17.8 us (42%)
  waiting for transfers between devices  12.5 us (29%)
  Pallas kernels  11.3 us (26%)
  between operations  0.73 us (2%)
    all_to_all x2, starting transfers between devices, exchange(): lax.all_to_all(message, axis, 0, 0, axis_index_groups=groups, tiled=True)  12.2 us
    pallas_call x7, Pallas kernels, call(): pl.pallas_call(kernel, out_shape=[jax.ShapeDtypeStruct(shape, jnp.float32...  11.3 us
    all_to_all x2, waiting for transfers between devices, exchange(): lax.all_to_all(message, axis, 0, 0, axis_index_groups=groups, tiled=True)  10.2 us
    ppermute x1, starting transfers between devices, local(): below = lax.ppermute(up, 'pipe', forward)  2.46 us
    ppermute x3, waiting for transfers between devices, local(): lax.ppermute(image_values, 'cross', [(i, i ^ u) for i in range(cross)])  2.29 us
    ppermute x3, starting transfers between devices, local(): lax.ppermute(image_values, 'cross', [(i, i ^ u) for i in range(cross)])  1.85 us
    ppermute x1, starting transfers between devices, local(): above = lax.ppermute(down, 'pipe', [(j, i) for i, j in forward])  1.29 us
  transfers between devices with their start and end apart: 7, of which 4 were waited for; matrix products, arithmetic and copies ran while one was open for 0% of the time, Pallas kernels for 8%

profile of v9, /device:TPU:0, one launch (start us, length us, event | category | flops | bytes accessed | tf_op | source)
XLA Modules:
  0.0 42.3 jit_solution(3376250981430328649)
XLA Ops:
  0.6 0.0 copy-start.2
  0.6 0.0 copy-start
  0.7 5.1 %shard_map.113 = (f32[832,128]{1,0:T(8,128)}, f32[1664,128]{1,0:T(8,128)}, f32[96,128]{1,0:T(8,128)}, f32[96,128]{1,0:T(8,128)}) custom-call(f32[16,2304]{1,0:T(8,128)} %face_hbm.1, f32[16,2304]{1,0:T(8,128)} %courant_hbm.1, f32[8,192,128]{2,1,0:T(8,128)} %constant.2.clone.tables_hbm, s32[128]{0:T(128)} %cell_hbm.1, s32[128]{0:T(128)} %owner_hbm.1, ...), custom_call_target="tpu_custom_call" | custom-call | tf_op jit(solution)/shard_map/pallas_call | solution.py:881
  5.8 0.0 copy-start.1
  5.8 8.0 %all-to-all-start = ((f32[8,104,128]{2,1,0:T(8,128)}), f32[8,104,128]{2,1,0:T(8,128)S(1)}, u32[]{:S(2)}, u32[]{:S(2)}) async-start(f32[8,104,128]{2,1,0:T(8,128)} %bitcast.8), calls=%async_computation | async-start | bytes 851968 | tf_op jit(solution)/shard_map/all_to_all | solution.py:893
  13.8 2.5 %collective-permute-start = (f32[96,128]{1,0:T(8,128)}, f32[96,128]{1,0:T(8,128)S(1)}, u32[]{:S(2)}, u32[]{:S(2)}) collective-permute-start(f32[96,128]{1,0:T(8,128)} %get-tuple-element.12), channel_id=1, source_target_pairs={{0,4},{4,8},{8,12},{12,16},{16,20},{20,24},{24,28},{1,5},{5,9},{9,... | collective-permute-start | bytes 147464 | tf_op jit(solution)/shard_map/ppermute | solution.py:957
  16.3 1.3 %collective-permute-start.1 = (f32[96,128]{1,0:T(8,128)}, f32[96,128]{1,0:T(8,128)S(1)}, u32[]{:S(2)}, u32[]{:S(2)}) collective-permute-start(f32[96,128]{1,0:T(8,128)} %get-tuple-element.13), channel_id=1, source_target_pairs={{4,0},{8,4},{12,8},{16,12},{20,16},{24,20},{28,24},{5,1},{9,5},{13... | collective-permute-start | bytes 147464 | tf_op jit(solution)/shard_map/ppermute | solution.py:958
  17.6 7.1 %all-to-all-done = f32[8,104,128]{2,1,0:T(8,128)S(1)} async-done(((f32[8,104,128]{2,1,0:T(8,128)}), f32[8,104,128]{2,1,0:T(8,128)S(1)}, u32[]{:S(2)}, u32[]{:S(2)}) %all-to-all-start) | async-done | bytes 426016 | tf_op jit(solution)/shard_map/all_to_all | solution.py:893
  24.7 0.0 collective-permute-start.4
  24.7 1.6 %collective-permute-start.3 = (f32[80,128]{1,0:T(8,128)S(1)}, f32[80,128]{1,0:T(8,128)S(1)}, u32[]{:S(2)}, u32[]{:S(2)}) collective-permute-start(f32[80,128]{1,0:T(8,128)S(1)} %shard_map.115.refs_0_), channel_id=1, source_target_pairs={{0,2},{1,3},{2,0},{3,1},{4,6},{5,7},{6,4},{7,5},{8,10},{9,11},{10,... | collective-permute-start | bytes 122888 | tf_op jit(solution)/shard_map/ppermute | solution.py:978
  26.2 0.3 collective-permute-start.2
  26.5 0.0 collective-permute-done.below_ref
  26.5 0.0 collective-permute-done.1.above_ref
  26.5 0.2 shard_map.114
  26.8 1.7 %collective-permute-done.4.refs_3_ = f32[80,128]{1,0:T(8,128)S(1)} collective-permute-done((f32[80,128]{1,0:T(8,128)S(1)}, f32[80,128]{1,0:T(8,128)S(1)}, u32[]{:S(2)}, u32[]{:S(2)}) %collective-permute-start.4) | collective-permute-done | bytes 40992 | tf_op jit(solution)/shard_map/ppermute | solution.py:978
  28.5 0.6 %collective-permute-done.3.refs_2_ = f32[80,128]{1,0:T(8,128)S(1)} collective-permute-done((f32[80,128]{1,0:T(8,128)S(1)}, f32[80,128]{1,0:T(8,128)S(1)}, u32[]{:S(2)}, u32[]{:S(2)}) %collective-permute-start.3) | collective-permute-done | bytes 40992 | tf_op jit(solution)/shard_map/ppermute | solution.py:978
  29.1 0.0 collective-permute-done.2.refs_1_
  29.1 1.7 %shard_map.116 = f32[384,128]{1,0:T(8,128)} custom-call(f32[832,128]{1,0:T(8,128)S(1)} %bitcast.6, f32[320,128]{1,0:T(8,128)S(1)} %get-tuple-element.15.rest_ref, f32[256,128]{1,0:T(8,128)S(1)} %get-tuple-element.16.chain_ref, f32[80,128]{1,0:T(8,128)S(1)} %shard_map.115.refs_0_, f32[80,128]{1,0:T(8,128)S(1)} %collective-permute-done.2.refs_1_, ...), custom_call_target="tpu_custom_call" | custom-call | tf_op jit(solution)/shard_map/pallas_call | solution.py:881
  30.7 4.2 %all-to-all-start.1 = ((f32[8,48,128]{2,1,0:T(8,128)}), f32[8,48,128]{2,1,0:T(8,128)S(1)}, u32[]{:S(2)}, u32[]{:S(2)}) async-start(f32[8,48,128]{2,1,0:T(8,128)} %bitcast.2), calls=%async_computation.1 | async-start | bytes 393216 | tf_op jit(solution)/shard_map/all_to_all | solution.py:893
  34.9 0.0 copy-done.2
  34.9 0.0 copy-done
  34.9 0.0 copy-done.1
  34.9 0.8 %shard_map.117.ready_ref = f32[4544,128]{1,0:T(8,128)S(1)} custom-call(f32[1664,128]{1,0:T(8,128)S(1)} %copy-done.1, s32[16,2304]{1,0:T(8,128)S(1)} %copy-done.2, f32[5,16,2304]{2,1,0:T(8,128)S(1)} %copy-done), custom_call_target="tpu_custom_call" | custom-call | tf_op jit(solution)/shard_map/pallas_call | solution.py:881
  35.7 2.2 %shard_map.118.done_ref = f32[4252,128]{1,0:T(8,128)S(1)} custom-call(f32[4544,128]{1,0:T(8,128)S(1)} %shard_map.117.ready_ref, f32[96,128]{1,0:T(8,128)S(1)} %collective-permute-done.below_ref, f32[96,128]{1,0:T(8,128)S(1)} %collective-permute-done.1.above_ref, f32[80,128]{1,0:T(8,128)S(1)} %shard_map.115.refs_0_, ...), custom_call_target="tpu_custom_call" | custom-call | tf_op jit(solution)/shard_map/pallas_call | solution.py:881
  38.0 3.0 %all-to-all-done.1 = f32[8,48,128]{2,1,0:T(8,128)S(1)} async-done(((f32[8,48,128]{2,1,0:T(8,128)}), f32[8,48,128]{2,1,0:T(8,128)S(1)}, u32[]{:S(2)}, u32[]{:S(2)}) %all-to-all-start.1) | async-done | bytes 196640 | tf_op jit(solution)/shard_map/all_to_all | solution.py:893
  41.0 1.3 %shard_map.119 = (f32[5,16,2304]{2,1,0:T(8,128)}, f32[5,16,2304]{2,1,0:T(8,128)}) custom-call(f32[384,128]{1,0:T(8,128)S(1)} %bitcast.7, f32[4252,128]{1,0:T(8,128)S(1)} %shard_map.118.done_ref), custom_call_target="tpu_custom_call" | custom-call | tf_op jit(solution)/shard_map/pallas_call | solution.py:881
  (1 shorter events, 0.0 us)
Async XLA Ops:
  0.6 34.3 %copy-start.2 = (s32[16,2304]{1,0:T(8,128)S(1)}, s32[16,2304]{1,0:T(8,128)}, u32[]{:S(2)}) copy-start(s32[16,2304]{1,0:T(8,128)} %mask_ref.1) | copy-start | bytes 442372
  0.6 34.3 %copy-start = (f32[5,16,2304]{2,1,0:T(8,128)S(1)}, f32[5,16,2304]{2,1,0:T(8,128)}, u32[]{:S(2)}) copy-start(f32[5,16,2304]{2,1,0:T(8,128)} %state_ref.1) | copy-start | bytes 2211844
  5.8 29.1 %copy-start.1 = (f32[1664,128]{1,0:T(8,128)S(1)}, f32[1664,128]{1,0:T(8,128)}, u32[]{:S(2)}) copy-start(f32[1664,128]{1,0:T(8,128)} %get-tuple-element.17.stay_ref) | copy-start | bytes 2555908
  5.8 18.9 %all-to-all-start = ((f32[8,104,128]{2,1,0:T(8,128)}), f32[8,104,128]{2,1,0:T(8,128)S(1)}, u32[]{:S(2)}, u32[]{:S(2)}) async-start(f32[8,104,128]{2,1,0:T(8,128)} %bitcast.8), calls=%async_computation | async-start | bytes 851968 | tf_op jit(solution)/shard_map/all_to_all | solution.py:893
  13.8 12.7 %collective-permute-start = (f32[96,128]{1,0:T(8,128)}, f32[96,128]{1,0:T(8,128)S(1)}, u32[]{:S(2)}, u32[]{:S(2)}) collective-permute-start(f32[96,128]{1,0:T(8,128)} %get-tuple-element.12), channel_id=1, source_target_pairs={{0,4},{4,8},{8,12},{12,16},{16,20},{20,24},{24,28},{1,5},{5,9},{9,... | collective-permute-start | bytes 147464 | tf_op jit(solution)/shard_map/ppermute | solution.py:957
  16.3 10.3 %collective-permute-start.1 = (f32[96,128]{1,0:T(8,128)}, f32[96,128]{1,0:T(8,128)S(1)}, u32[]{:S(2)}, u32[]{:S(2)}) collective-permute-start(f32[96,128]{1,0:T(8,128)} %get-tuple-element.13), channel_id=1, source_target_pairs={{4,0},{8,4},{12,8},{16,12},{20,16},{24,20},{28,24},{5,1},{9,5},{13... | collective-permute-start | bytes 147464 | tf_op jit(solution)/shard_map/ppermute | solution.py:958
  24.7 3.8 %collective-permute-start.4 = (f32[80,128]{1,0:T(8,128)S(1)}, f32[80,128]{1,0:T(8,128)S(1)}, u32[]{:S(2)}, u32[]{:S(2)}) collective-permute-start(f32[80,128]{1,0:T(8,128)S(1)} %shard_map.115.refs_0_), channel_id=1, source_target_pairs={{0,3},{1,2},{2,1},{3,0},{4,7},{5,6},{6,5},{7,4},{8,11},{9,10},{10,... | collective-permute-start | bytes 122888 | tf_op jit(solution)/shard_map/ppermute | solution.py:978
  24.7 4.4 %collective-permute-start.3 = (f32[80,128]{1,0:T(8,128)S(1)}, f32[80,128]{1,0:T(8,128)S(1)}, u32[]{:S(2)}, u32[]{:S(2)}) collective-permute-start(f32[80,128]{1,0:T(8,128)S(1)} %shard_map.115.refs_0_), channel_id=1, source_target_pairs={{0,2},{1,3},{2,0},{3,1},{4,6},{5,7},{6,4},{7,5},{8,10},{9,11},{10,... | collective-permute-start | bytes 122888 | tf_op jit(solution)/shard_map/ppermute | solution.py:978
  26.2 2.8 %collective-permute-start.2 = (f32[80,128]{1,0:T(8,128)S(1)}, f32[80,128]{1,0:T(8,128)S(1)}, u32[]{:S(2)}, u32[]{:S(2)}) collective-permute-start(f32[80,128]{1,0:T(8,128)S(1)} %shard_map.115.refs_0_), channel_id=1, source_target_pairs={{0,1},{1,0},{2,3},{3,2},{4,5},{5,4},{6,7},{7,6},{8,9},{9,8},{10,11... | collective-permute-start | bytes 122888 | tf_op jit(solution)/shard_map/ppermute | solution.py:978
  30.7 10.3 %all-to-all-start.1 = ((f32[8,48,128]{2,1,0:T(8,128)}), f32[8,48,128]{2,1,0:T(8,128)S(1)}, u32[]{:S(2)}, u32[]{:S(2)}) async-start(f32[8,48,128]{2,1,0:T(8,128)} %bitcast.2), calls=%async_computation.1 | async-start | bytes 393216 | tf_op jit(solution)/shard_map/all_to_all | solution.py:893

commit v10 on v7

--- a/solution.py
+++ b/solution.py
@@ -94,15 +94,16 @@
     return pieces
 
 
-def exact_dot(x, one_hot, contract):
+def one_hot_dot(x, one_hot, contract, parts):
     found = lax.dot_general(
-        jnp.concatenate(split(x, 3), axis=0),
+        jnp.concatenate(split(x, parts), axis=0),
         one_hot,
         (contract, ((), ())),
         preferred_element_type=jnp.float32,
     )
     size = x.shape[0]
-    return found[:size] + (found[size : 2 * size] + found[2 * size :])
+    pieces = [found[k * size : (k + 1) * size] for k in range(parts)]
+    return sum(pieces[-2::-1], pieces[-1])
 
 
 def full_dot(a, b):
@@ -241,7 +242,7 @@
     return jnp.concatenate(lines, axis=0)
 
 
-def ghost_values(slices, blocks, column):
+def ghost_values(slices, blocks, column, parts):
     per = slices.image_rows // slices.var_count
     slabs, cross = slices.slabs, slices.cross
     ghosts = column.shape[1]
@@ -266,7 +267,7 @@
         for v in range(slices.var_count)
     ]
     pick = marks((per * LANES, ghosts), 0, image)
-    found = exact_dot(jnp.concatenate(values, axis=0), pick, ((1,), (0,)))
+    found = one_hot_dot(jnp.concatenate(values, axis=0), pick, ((1,), (0,)), parts)
     devices = slabs * cross
     at = lax.broadcasted_iota(jnp.int32, (devices, ghosts), 0)
     mine = (at % slabs) * cross + (across ^ (at // slabs)) == owner
@@ -432,8 +433,8 @@
     row, pencil = place_of(cell_ref[...].reshape(1, ghosts), rows, pencils)
     lane_tile = jnp.right_shift(pencil, 7)
     lane_marks = marks((LANES, ghosts), 0, pencil - lane_tile * LANES)
-    picked = exact_dot(
-        weight_ref[...].reshape(2 * rows * padded, LANES), lane_marks, ((1,), (0,))
+    picked = one_hot_dot(
+        weight_ref[...].reshape(2 * rows * padded, LANES), lane_marks, ((1,), (0,)), 2
     ).reshape(2, rows, padded, ghosts)
     at_cell = (lax.broadcasted_iota(jnp.int32, (rows, padded, ghosts), 0) == row[None]) & (
         lax.broadcasted_iota(jnp.int32, (rows, padded, ghosts), 1) == lane_tile[None]
@@ -569,7 +570,7 @@
         return jnp.concatenate([meta(p, k) for p in range(slabs)], axis=1)
 
     carry_up, carry_down, ups, downs = constants
-    values = ghost_values(slices, blocks, meta_all(COLUMN))
+    values = ghost_values(slices, blocks, meta_all(COLUMN), 2)
     rows = ups.shape[1]
     row_of, pencil_of = place_of(meta_all(CELL).astype(jnp.int32), rows, pencils)
     ghosts = LANES
@@ -598,7 +599,7 @@
         here = jnp.concatenate([value[:, tile(p)] for value in values] + [none], axis=0)
         shares = jnp.concatenate([here * weight for weight in weights], axis=0)
         spots = jnp.where(pencil_at == pencil_of[:, tile(p)], 1.0, 0.0)
-        share = exact_dot(shares, spots.astype(jnp.bfloat16), ((1,), (1,)))
+        share = one_hot_dot(shares, spots.astype(jnp.bfloat16), ((1,), (1,)), 2)
         for t in range(chunk):
             start = (p * chunk + t) * 48
             ghost_ref[start : start + 48, :] = share[:, tile(t)]
@@ -720,14 +721,14 @@
     def known(k):
         return jnp.concatenate([x[k : k + 1] for x in about], axis=1)
 
-    values = ghost_values(slices, blocks, known(COLUMN))
+    values = ghost_values(slices, blocks, known(COLUMN), 3)
     row, pencil = place_of(known(CELL).astype(jnp.int32), rows, pencils)
     at_row = lax.broadcasted_iota(jnp.int32, (rows, ghosts), 0) == row[:, :ghosts]
     spread = jnp.concatenate([jnp.where(at_row, value[:, :ghosts], 0.0) for value in values], axis=0)
     own = ready_ref[kept_start + own_at : kept_start + own_at + cells, :cells]
     both = jnp.concatenate([full_dot(own, spread), spread], axis=0)
     spots = marks((pencils, ghosts), 0, pencil[:, :ghosts])
-    added = exact_dot(both, spots, ((1,), (1,)))
+    added = one_hot_dot(both, spots, ((1,), (1,)), 3)
     for t in range(count):
         here = slice(t * cells, (t + 1) * cells)
         there = slice(cells_at + t * cells, cells_at + (t + 1) * cells)
@@ -740,7 +741,7 @@
         at_edge = row[:, here] == wanted
         spread = [jnp.where(at_edge, value[:, here], 0.0) for value in values] + [none]
         spots = marks((pencils, ghosts), 0, pencil[:, here])
-        turn(edge_ref, exact_dot(jnp.concatenate(spread, axis=0), spots, ((1,), (1,))))
+        turn(edge_ref, one_hot_dot(jnp.concatenate(spread, axis=0), spots, ((1,), (1,)), 3))
         for v in range(var_count):
             start = edge_at + (k * var_count + v) * count
             done_ref[start : start + count, :] = ref[v * count : (v + 1) * count, :] + slab_at(

time: 42.4 us -> 42.3 us (level)
  no operation moved by 1% of the time
where the time goes in v10:
time: 42.3 us; the launch traced here: 42 us
  starting transfers between devices  17.8 us (42%)
  waiting for transfers between devices  12.4 us (29%)
  Pallas kernels  11 us (26%)
  between operations  0.73 us (2%)
    all_to_all x2, starting transfers between devices, exchange(): lax.all_to_all(message, axis, 0, 0, axis_index_groups=groups, tiled=True)  12.2 us
    pallas_call x7, Pallas kernels, call(): pl.pallas_call(kernel, out_shape=[jax.ShapeDtypeStruct(shape, jnp.float32...  11 us
    all_to_all x2, waiting for transfers between devices, exchange(): lax.all_to_all(message, axis, 0, 0, axis_index_groups=groups, tiled=True)  10.1 us
    ppermute x1, starting transfers between devices, local(): below = lax.ppermute(up, 'pipe', forward)  2.46 us
    ppermute x3, waiting for transfers between devices, local(): lax.ppermute(image_values, 'cross', [(i, i ^ u) for i in range(cross)])  2.29 us
    ppermute x3, starting transfers between devices, local(): lax.ppermute(image_values, 'cross', [(i, i ^ u) for i in range(cross)])  1.85 us
    ppermute x1, starting transfers between devices, local(): above = lax.ppermute(down, 'pipe', [(j, i) for i, j in forward])  1.29 us
  transfers between devices with their start and end apart: 7, of which 4 were waited for; matrix products, arithmetic and copies ran while one was open for 0% of the time, Pallas kernels for 8%

profile of v10, /device:TPU:0, one launch (start us, length us, event | category | flops | bytes accessed | tf_op | source)
XLA Modules:
  0.0 42.0 jit_solution(13196488502051729619)
XLA Ops:
  0.6 0.0 copy-start.2
  0.6 0.0 copy-start
  0.7 4.8 %shard_map.113 = (f32[832,128]{1,0:T(8,128)}, f32[1664,128]{1,0:T(8,128)}, f32[96,128]{1,0:T(8,128)}, f32[96,128]{1,0:T(8,128)}) custom-call(f32[16,2304]{1,0:T(8,128)} %face_hbm.1, f32[16,2304]{1,0:T(8,128)} %courant_hbm.1, f32[8,192,128]{2,1,0:T(8,128)} %constant.2.clone.tables_hbm, s32[128]{0:T(128)} %cell_hbm.1, s32[128]{0:T(128)} %owner_hbm.1, ...), custom_call_target="tpu_custom_call" | custom-call | tf_op jit(solution)/shard_map/pallas_call | solution.py:871
  5.5 0.0 copy-start.1
  5.5 8.0 %all-to-all-start = ((f32[8,104,128]{2,1,0:T(8,128)}), f32[8,104,128]{2,1,0:T(8,128)S(1)}, u32[]{:S(2)}, u32[]{:S(2)}) async-start(f32[8,104,128]{2,1,0:T(8,128)} %bitcast.8), calls=%async_computation | async-start | bytes 851968 | tf_op jit(solution)/shard_map/all_to_all | solution.py:883
  13.5 2.5 %collective-permute-start = (f32[96,128]{1,0:T(8,128)}, f32[96,128]{1,0:T(8,128)S(1)}, u32[]{:S(2)}, u32[]{:S(2)}) collective-permute-start(f32[96,128]{1,0:T(8,128)} %get-tuple-element.12), channel_id=1, source_target_pairs={{0,4},{4,8},{8,12},{12,16},{16,20},{20,24},{24,28},{1,5},{5,9},{9,... | collective-permute-start | bytes 147464 | tf_op jit(solution)/shard_map/ppermute | solution.py:947
  15.9 1.3 %collective-permute-start.1 = (f32[96,128]{1,0:T(8,128)}, f32[96,128]{1,0:T(8,128)S(1)}, u32[]{:S(2)}, u32[]{:S(2)}) collective-permute-start(f32[96,128]{1,0:T(8,128)} %get-tuple-element.13), channel_id=1, source_target_pairs={{4,0},{8,4},{12,8},{16,12},{20,16},{24,20},{28,24},{5,1},{9,5},{13... | collective-permute-start | bytes 147464 | tf_op jit(solution)/shard_map/ppermute | solution.py:948
  17.2 7.1 %all-to-all-done = f32[8,104,128]{2,1,0:T(8,128)S(1)} async-done(((f32[8,104,128]{2,1,0:T(8,128)}), f32[8,104,128]{2,1,0:T(8,128)S(1)}, u32[]{:S(2)}, u32[]{:S(2)}) %all-to-all-start) | async-done | bytes 426016 | tf_op jit(solution)/shard_map/all_to_all | solution.py:883
  24.3 0.0 collective-permute-start.4
  24.4 1.6 %collective-permute-start.3 = (f32[80,128]{1,0:T(8,128)S(1)}, f32[80,128]{1,0:T(8,128)S(1)}, u32[]{:S(2)}, u32[]{:S(2)}) collective-permute-start(f32[80,128]{1,0:T(8,128)S(1)} %shard_map.115.refs_0_), channel_id=1, source_target_pairs={{0,2},{1,3},{2,0},{3,1},{4,6},{5,7},{6,4},{7,5},{8,10},{9,11},{10,... | collective-permute-start | bytes 122888 | tf_op jit(solution)/shard_map/ppermute | solution.py:968
  25.9 0.3 collective-permute-start.2
  26.2 0.0 collective-permute-done.below_ref
  26.2 0.0 collective-permute-done.1.above_ref
  26.2 0.2 shard_map.114
  26.4 1.7 %collective-permute-done.4.refs_3_ = f32[80,128]{1,0:T(8,128)S(1)} collective-permute-done((f32[80,128]{1,0:T(8,128)S(1)}, f32[80,128]{1,0:T(8,128)S(1)}, u32[]{:S(2)}, u32[]{:S(2)}) %collective-permute-start.4) | collective-permute-done | bytes 40992 | tf_op jit(solution)/shard_map/ppermute | solution.py:968
  28.2 0.6 %collective-permute-done.3.refs_2_ = f32[80,128]{1,0:T(8,128)S(1)} collective-permute-done((f32[80,128]{1,0:T(8,128)S(1)}, f32[80,128]{1,0:T(8,128)S(1)}, u32[]{:S(2)}, u32[]{:S(2)}) %collective-permute-start.3) | collective-permute-done | bytes 40992 | tf_op jit(solution)/shard_map/ppermute | solution.py:968
  28.7 0.0 collective-permute-done.2.refs_1_
  28.7 1.7 %shard_map.116 = f32[384,128]{1,0:T(8,128)} custom-call(f32[832,128]{1,0:T(8,128)S(1)} %bitcast.6, f32[320,128]{1,0:T(8,128)S(1)} %get-tuple-element.15.rest_ref, f32[256,128]{1,0:T(8,128)S(1)} %get-tuple-element.16.chain_ref, f32[80,128]{1,0:T(8,128)S(1)} %shard_map.115.refs_0_, f32[80,128]{1,0:T(8,128)S(1)} %collective-permute-done.2.refs_1_, ...), custom_call_target="tpu_custom_call" | custom-call | tf_op jit(solution)/shard_map/pallas_call | solution.py:871
  30.4 4.2 %all-to-all-start.1 = ((f32[8,48,128]{2,1,0:T(8,128)}), f32[8,48,128]{2,1,0:T(8,128)S(1)}, u32[]{:S(2)}, u32[]{:S(2)}) async-start(f32[8,48,128]{2,1,0:T(8,128)} %bitcast.2), calls=%async_computation.1 | async-start | bytes 393216 | tf_op jit(solution)/shard_map/all_to_all | solution.py:883
  34.6 0.0 copy-done.2
  34.6 0.0 copy-done
  34.6 0.0 copy-done.1
  34.6 0.8 %shard_map.117.ready_ref = f32[4544,128]{1,0:T(8,128)S(1)} custom-call(f32[1664,128]{1,0:T(8,128)S(1)} %copy-done.1, s32[16,2304]{1,0:T(8,128)S(1)} %copy-done.2, f32[5,16,2304]{2,1,0:T(8,128)S(1)} %copy-done), custom_call_target="tpu_custom_call" | custom-call | tf_op jit(solution)/shard_map/pallas_call | solution.py:871
  35.4 2.2 %shard_map.118.done_ref = f32[4252,128]{1,0:T(8,128)S(1)} custom-call(f32[4544,128]{1,0:T(8,128)S(1)} %shard_map.117.ready_ref, f32[96,128]{1,0:T(8,128)S(1)} %collective-permute-done.below_ref, f32[96,128]{1,0:T(8,128)S(1)} %collective-permute-done.1.above_ref, f32[80,128]{1,0:T(8,128)S(1)} %shard_map.115.refs_0_, ...), custom_call_target="tpu_custom_call" | custom-call | tf_op jit(solution)/shard_map/pallas_call | solution.py:871
  37.6 3.0 %all-to-all-done.1 = f32[8,48,128]{2,1,0:T(8,128)S(1)} async-done(((f32[8,48,128]{2,1,0:T(8,128)}), f32[8,48,128]{2,1,0:T(8,128)S(1)}, u32[]{:S(2)}, u32[]{:S(2)}) %all-to-all-start.1) | async-done | bytes 196640 | tf_op jit(solution)/shard_map/all_to_all | solution.py:883
  40.7 1.3 %shard_map.119 = (f32[5,16,2304]{2,1,0:T(8,128)}, f32[5,16,2304]{2,1,0:T(8,128)}) custom-call(f32[384,128]{1,0:T(8,128)S(1)} %bitcast.7, f32[4252,128]{1,0:T(8,128)S(1)} %shard_map.118.done_ref), custom_call_target="tpu_custom_call" | custom-call | tf_op jit(solution)/shard_map/pallas_call | solution.py:871
  (1 shorter events, 0.0 us)
Async XLA Ops:
  0.6 34.0 %copy-start.2 = (s32[16,2304]{1,0:T(8,128)S(1)}, s32[16,2304]{1,0:T(8,128)}, u32[]{:S(2)}) copy-start(s32[16,2304]{1,0:T(8,128)} %mask_ref.1) | copy-start | bytes 442372
  0.6 34.0 %copy-start = (f32[5,16,2304]{2,1,0:T(8,128)S(1)}, f32[5,16,2304]{2,1,0:T(8,128)}, u32[]{:S(2)}) copy-start(f32[5,16,2304]{2,1,0:T(8,128)} %state_ref.1) | copy-start | bytes 2211844
  5.5 29.1 %copy-start.1 = (f32[1664,128]{1,0:T(8,128)S(1)}, f32[1664,128]{1,0:T(8,128)}, u32[]{:S(2)}) copy-start(f32[1664,128]{1,0:T(8,128)} %get-tuple-element.17.stay_ref) | copy-start | bytes 2555908
  5.5 18.9 %all-to-all-start = ((f32[8,104,128]{2,1,0:T(8,128)}), f32[8,104,128]{2,1,0:T(8,128)S(1)}, u32[]{:S(2)}, u32[]{:S(2)}) async-start(f32[8,104,128]{2,1,0:T(8,128)} %bitcast.8), calls=%async_computation | async-start | bytes 851968 | tf_op jit(solution)/shard_map/all_to_all | solution.py:883
  13.5 12.7 %collective-permute-start = (f32[96,128]{1,0:T(8,128)}, f32[96,128]{1,0:T(8,128)S(1)}, u32[]{:S(2)}, u32[]{:S(2)}) collective-permute-start(f32[96,128]{1,0:T(8,128)} %get-tuple-element.12), channel_id=1, source_target_pairs={{0,4},{4,8},{8,12},{12,16},{16,20},{20,24},{24,28},{1,5},{5,9},{9,... | collective-permute-start | bytes 147464 | tf_op jit(solution)/shard_map/ppermute | solution.py:947
  15.9 10.3 %collective-permute-start.1 = (f32[96,128]{1,0:T(8,128)}, f32[96,128]{1,0:T(8,128)S(1)}, u32[]{:S(2)}, u32[]{:S(2)}) collective-permute-start(f32[96,128]{1,0:T(8,128)} %get-tuple-element.13), channel_id=1, source_target_pairs={{4,0},{8,4},{12,8},{16,12},{20,16},{24,20},{28,24},{5,1},{9,5},{13... | collective-permute-start | bytes 147464 | tf_op jit(solution)/shard_map/ppermute | solution.py:948
  24.3 3.8 %collective-permute-start.4 = (f32[80,128]{1,0:T(8,128)S(1)}, f32[80,128]{1,0:T(8,128)S(1)}, u32[]{:S(2)}, u32[]{:S(2)}) collective-permute-start(f32[80,128]{1,0:T(8,128)S(1)} %shard_map.115.refs_0_), channel_id=1, source_target_pairs={{0,3},{1,2},{2,1},{3,0},{4,7},{5,6},{6,5},{7,4},{8,11},{9,10},{10,... | collective-permute-start | bytes 122888 | tf_op jit(solution)/shard_map/ppermute | solution.py:968
  24.4 4.4 %collective-permute-start.3 = (f32[80,128]{1,0:T(8,128)S(1)}, f32[80,128]{1,0:T(8,128)S(1)}, u32[]{:S(2)}, u32[]{:S(2)}) collective-permute-start(f32[80,128]{1,0:T(8,128)S(1)} %shard_map.115.refs_0_), channel_id=1, source_target_pairs={{0,2},{1,3},{2,0},{3,1},{4,6},{5,7},{6,4},{7,5},{8,10},{9,11},{10,... | collective-permute-start | bytes 122888 | tf_op jit(solution)/shard_map/ppermute | solution.py:968
  25.9 2.8 %collective-permute-start.2 = (f32[80,128]{1,0:T(8,128)S(1)}, f32[80,128]{1,0:T(8,128)S(1)}, u32[]{:S(2)}, u32[]{:S(2)}) collective-permute-start(f32[80,128]{1,0:T(8,128)S(1)} %shard_map.115.refs_0_), channel_id=1, source_target_pairs={{0,1},{1,0},{2,3},{3,2},{4,5},{5,4},{6,7},{7,6},{8,9},{9,8},{10,11... | collective-permute-start | bytes 122888 | tf_op jit(solution)/shard_map/ppermute | solution.py:968
  30.4 10.3 %all-to-all-start.1 = ((f32[8,48,128]{2,1,0:T(8,128)}), f32[8,48,128]{2,1,0:T(8,128)S(1)}, u32[]{:S(2)}, u32[]{:S(2)}) async-start(f32[8,48,128]{2,1,0:T(8,128)} %bitcast.2), calls=%async_computation.1 | async-start | bytes 393216 | tf_op jit(solution)/shard_map/all_to_all | solution.py:883

commit v11 on v10

--- a/solution.py
+++ b/solution.py
@@ -964,18 +964,22 @@
         near=(0,),
         limit=24,
     )
-    blocks = [image_values] + [
-        lax.ppermute(image_values, "cross", [(i, i ^ u) for i in range(cross)])
-        for u in range(1, cross)
-    ]
-
-    factored, below, above = lax.optimization_barrier((message, below, above))
+    blocks = {0: image_values}
+    step = cross // 2
+    while step:
+        route = [(i, i ^ step) for i in range(cross)]
+        passed = {u ^ step: lax.ppermute(x, "cross", route) for u, x in blocks.items()}
+        if step == cross // 2:
+            passed, below, above = lax.optimization_barrier((passed, below, above))
+        blocks.update(passed)
+        step //= 2
+    blocks = [blocks[u] for u in range(cross)]
     rest, chain = call(
         functools.partial(chain_kernel, slices),
         [(slabs * max(slices.groups, 1) * slices.per, LANES), (2 * slabs * 16, LANES)],
         [],
         [],
-        (factored,),
+        (message,),
         near=(0,),
         limit=24,
     )

time: 42.3 us -> 43.1 us (1.019)
  waiting for transfers between devices: 12.4 us -> 13.6 us
    ppermute x3, waiting for transfers between devices: 2.29 us -> 3.48 us  [local(): lax.ppermute(x, 'cross', route)]
where the time goes in v11:
time: 43.1 us; the launch traced here: 42.8 us
  starting transfers between devices  17.4 us (40%)
  waiting for transfers between devices  13.6 us (32%)
  Pallas kernels  11 us (26%)
  between operations  0.73 us (2%)
    all_to_all x2, starting transfers between devices, exchange(): lax.all_to_all(message, axis, 0, 0, axis_index_groups=groups, tiled=True)  12.2 us
    pallas_call x7, Pallas kernels, call(): pl.pallas_call(kernel, out_shape=[jax.ShapeDtypeStruct(shape, jnp.float32...  11 us
    all_to_all x2, waiting for transfers between devices, exchange(): lax.all_to_all(message, axis, 0, 0, axis_index_groups=groups, tiled=True)  10.1 us
    ppermute x3, waiting for transfers between devices, local(): lax.ppermute(x, 'cross', route)  3.48 us
    ppermute x1, starting transfers between devices, local(): below = lax.ppermute(up, 'pipe', forward)  2.46 us
    ppermute x3, starting transfers between devices, local(): lax.ppermute(x, 'cross', route)  1.5 us
    ppermute x1, starting transfers between devices, local(): above = lax.ppermute(down, 'pipe', [(j, i) for i, j in forward])  1.29 us
  transfers between devices with their start and end apart: 7, of which 4 were waited for; matrix products, arithmetic and copies ran while one was open for 0% of the time, Pallas kernels for 8%

profile of v11, /device:TPU:0, one launch (start us, length us, event | category | flops | bytes accessed | tf_op | source)
XLA Modules:
  0.0 42.8 jit_solution(10973024904407778314)
XLA Ops:
  0.6 0.0 copy-start.2
  0.6 0.0 copy-start
  0.7 4.8 %shard_map.113 = (f32[832,128]{1,0:T(8,128)}, f32[1664,128]{1,0:T(8,128)}, f32[96,128]{1,0:T(8,128)}, f32[96,128]{1,0:T(8,128)}) custom-call(f32[16,2304]{1,0:T(8,128)} %face_hbm.1, f32[16,2304]{1,0:T(8,128)} %courant_hbm.1, f32[8,192,128]{2,1,0:T(8,128)} %constant.2.clone.tables_hbm, s32[128]{0:T(128)} %cell_hbm.1, s32[128]{0:T(128)} %owner_hbm.1, ...), custom_call_target="tpu_custom_call" | custom-call | tf_op jit(solution)/shard_map/pallas_call | solution.py:871
  5.5 0.0 copy-start.1
  5.5 8.0 %all-to-all-start = ((f32[8,104,128]{2,1,0:T(8,128)}), f32[8,104,128]{2,1,0:T(8,128)S(1)}, u32[]{:S(2)}, u32[]{:S(2)}) async-start(f32[8,104,128]{2,1,0:T(8,128)} %bitcast.8), calls=%async_computation | async-start | bytes 851968 | tf_op jit(solution)/shard_map/all_to_all | solution.py:883
  13.5 2.5 %collective-permute-start.2 = (f32[96,128]{1,0:T(8,128)}, f32[96,128]{1,0:T(8,128)S(1)}, u32[]{:S(2)}, u32[]{:S(2)}) collective-permute-start(f32[96,128]{1,0:T(8,128)} %get-tuple-element.14), channel_id=1, source_target_pairs={{0,4},{4,8},{8,12},{12,16},{16,20},{20,24},{24,28},{1,5},{5,9},{9,... | collective-permute-start | bytes 147464 | tf_op jit(solution)/shard_map/ppermute | solution.py:947
  15.9 1.3 %collective-permute-start.3 = (f32[96,128]{1,0:T(8,128)}, f32[96,128]{1,0:T(8,128)S(1)}, u32[]{:S(2)}, u32[]{:S(2)}) collective-permute-start(f32[96,128]{1,0:T(8,128)} %get-tuple-element.15), channel_id=1, source_target_pairs={{4,0},{8,4},{12,8},{16,12},{20,16},{24,20},{28,24},{5,1},{9,5},{13... | collective-permute-start | bytes 147464 | tf_op jit(solution)/shard_map/ppermute | solution.py:948
  17.2 7.1 %all-to-all-done = f32[8,104,128]{2,1,0:T(8,128)S(1)} async-done(((f32[8,104,128]{2,1,0:T(8,128)}), f32[8,104,128]{2,1,0:T(8,128)S(1)}, u32[]{:S(2)}, u32[]{:S(2)}) %all-to-all-start) | async-done | bytes 426016 | tf_op jit(solution)/shard_map/all_to_all | solution.py:883
  24.3 1.5 %collective-permute-start.1 = (f32[80,128]{1,0:T(8,128)S(1)}, f32[80,128]{1,0:T(8,128)S(1)}, u32[]{:S(2)}, u32[]{:S(2)}) collective-permute-start(f32[80,128]{1,0:T(8,128)S(1)} %shard_map.115.refs_0_), channel_id=1, source_target_pairs={{0,2},{1,3},{2,0},{3,1},{4,6},{5,7},{6,4},{7,5},{8,10},{9,11},{10,... | collective-permute-start | bytes 122888 | tf_op jit(solution)/shard_map/ppermute | solution.py:971
  25.8 0.0 collective-permute-start
  25.8 0.0 collective-permute-done.2.below_ref
  25.8 0.0 collective-permute-done.3.above_ref
  25.8 2.5 %collective-permute-done.1.refs_2_ = f32[80,128]{1,0:T(8,128)S(1)} collective-permute-done((f32[80,128]{1,0:T(8,128)S(1)}, f32[80,128]{1,0:T(8,128)S(1)}, u32[]{:S(2)}, u32[]{:S(2)}) %collective-permute-start.1) | collective-permute-done | bytes 40992 | tf_op jit(solution)/shard_map/ppermute | solution.py:971
  28.3 0.0 collective-permute-start.4
  28.4 0.2 shard_map.114
  28.6 0.0 collective-permute-done.refs_1_
  28.6 1.0 %collective-permute-done.4.refs_3_ = f32[80,128]{1,0:T(8,128)S(1)} collective-permute-done((f32[80,128]{1,0:T(8,128)S(1)}, f32[80,128]{1,0:T(8,128)S(1)}, u32[]{:S(2)}, u32[]{:S(2)}) %collective-permute-start.4) | collective-permute-done | bytes 40992 | tf_op jit(solution)/shard_map/ppermute | solution.py:971
  29.6 1.6 %shard_map.116 = f32[384,128]{1,0:T(8,128)} custom-call(f32[832,128]{1,0:T(8,128)S(1)} %bitcast.6, f32[320,128]{1,0:T(8,128)S(1)} %get-tuple-element.12.rest_ref, f32[256,128]{1,0:T(8,128)S(1)} %get-tuple-element.13.chain_ref, f32[80,128]{1,0:T(8,128)S(1)} %shard_map.115.refs_0_, f32[80,128]{1,0:T(8,128)S(1)} %collective-permute-done.refs_1_, ...), custom_call_target="tpu_custom_call" | custom-call | tf_op jit(solution)/shard_map/pallas_call | solution.py:871
  31.2 4.2 %all-to-all-start.1 = ((f32[8,48,128]{2,1,0:T(8,128)}), f32[8,48,128]{2,1,0:T(8,128)S(1)}, u32[]{:S(2)}, u32[]{:S(2)}) async-start(f32[8,48,128]{2,1,0:T(8,128)} %bitcast.2), calls=%async_computation.1 | async-start | bytes 393216 | tf_op jit(solution)/shard_map/all_to_all | solution.py:883
  35.4 0.0 copy-done.2
  35.4 0.0 copy-done
  35.4 0.0 copy-done.1
  35.4 0.8 %shard_map.117.ready_ref = f32[4544,128]{1,0:T(8,128)S(1)} custom-call(f32[1664,128]{1,0:T(8,128)S(1)} %copy-done.1, s32[16,2304]{1,0:T(8,128)S(1)} %copy-done.2, f32[5,16,2304]{2,1,0:T(8,128)S(1)} %copy-done), custom_call_target="tpu_custom_call" | custom-call | tf_op jit(solution)/shard_map/pallas_call | solution.py:871
  36.2 2.2 %shard_map.118.done_ref = f32[4252,128]{1,0:T(8,128)S(1)} custom-call(f32[4544,128]{1,0:T(8,128)S(1)} %shard_map.117.ready_ref, f32[96,128]{1,0:T(8,128)S(1)} %collective-permute-done.2.below_ref, f32[96,128]{1,0:T(8,128)S(1)} %collective-permute-done.3.above_ref, f32[80,128]{1,0:T(8,128)S(1)} %shard_map.115.refs_0_, ...), custom_call_target="tpu_custom_call" | custom-call | tf_op jit(solution)/shard_map/pallas_call | solution.py:871
  38.4 3.0 %all-to-all-done.1 = f32[8,48,128]{2,1,0:T(8,128)S(1)} async-done(((f32[8,48,128]{2,1,0:T(8,128)}), f32[8,48,128]{2,1,0:T(8,128)S(1)}, u32[]{:S(2)}, u32[]{:S(2)}) %all-to-all-start.1) | async-done | bytes 196640 | tf_op jit(solution)/shard_map/all_to_all | solution.py:883
  41.5 1.3 %shard_map.119 = (f32[5,16,2304]{2,1,0:T(8,128)}, f32[5,16,2304]{2,1,0:T(8,128)}) custom-call(f32[384,128]{1,0:T(8,128)S(1)} %bitcast.7, f32[4252,128]{1,0:T(8,128)S(1)} %shard_map.118.done_ref), custom_call_target="tpu_custom_call" | custom-call | tf_op jit(solution)/shard_map/pallas_call | solution.py:871
  (1 shorter events, 0.0 us)
Async XLA Ops:
  0.6 34.8 %copy-start.2 = (s32[16,2304]{1,0:T(8,128)S(1)}, s32[16,2304]{1,0:T(8,128)}, u32[]{:S(2)}) copy-start(s32[16,2304]{1,0:T(8,128)} %mask_ref.1) | copy-start | bytes 442372
  0.6 34.8 %copy-start = (f32[5,16,2304]{2,1,0:T(8,128)S(1)}, f32[5,16,2304]{2,1,0:T(8,128)}, u32[]{:S(2)}) copy-start(f32[5,16,2304]{2,1,0:T(8,128)} %state_ref.1) | copy-start | bytes 2211844
  5.5 30.0 %copy-start.1 = (f32[1664,128]{1,0:T(8,128)S(1)}, f32[1664,128]{1,0:T(8,128)}, u32[]{:S(2)}) copy-start(f32[1664,128]{1,0:T(8,128)} %get-tuple-element.17.stay_ref) | copy-start | bytes 2555908
  5.5 18.9 %all-to-all-start = ((f32[8,104,128]{2,1,0:T(8,128)}), f32[8,104,128]{2,1,0:T(8,128)S(1)}, u32[]{:S(2)}, u32[]{:S(2)}) async-start(f32[8,104,128]{2,1,0:T(8,128)} %bitcast.8), calls=%async_computation | async-start | bytes 851968 | tf_op jit(solution)/shard_map/all_to_all | solution.py:883
  13.5 12.4 %collective-permute-start.2 = (f32[96,128]{1,0:T(8,128)}, f32[96,128]{1,0:T(8,128)S(1)}, u32[]{:S(2)}, u32[]{:S(2)}) collective-permute-start(f32[96,128]{1,0:T(8,128)} %get-tuple-element.14), channel_id=1, source_target_pairs={{0,4},{4,8},{8,12},{12,16},{16,20},{20,24},{24,28},{1,5},{5,9},{9,... | collective-permute-start | bytes 147464 | tf_op jit(solution)/shard_map/ppermute | solution.py:947
  15.9 9.9 %collective-permute-start.3 = (f32[96,128]{1,0:T(8,128)}, f32[96,128]{1,0:T(8,128)S(1)}, u32[]{:S(2)}, u32[]{:S(2)}) collective-permute-start(f32[96,128]{1,0:T(8,128)} %get-tuple-element.15), channel_id=1, source_target_pairs={{4,0},{8,4},{12,8},{16,12},{20,16},{24,20},{28,24},{5,1},{9,5},{13... | collective-permute-start | bytes 147464 | tf_op jit(solution)/shard_map/ppermute | solution.py:948
  24.3 4.0 %collective-permute-start.1 = (f32[80,128]{1,0:T(8,128)S(1)}, f32[80,128]{1,0:T(8,128)S(1)}, u32[]{:S(2)}, u32[]{:S(2)}) collective-permute-start(f32[80,128]{1,0:T(8,128)S(1)} %shard_map.115.refs_0_), channel_id=1, source_target_pairs={{0,2},{1,3},{2,0},{3,1},{4,6},{5,7},{6,4},{7,5},{8,10},{9,11},{10,... | collective-permute-start | bytes 122888 | tf_op jit(solution)/shard_map/ppermute | solution.py:971
  25.8 2.7 %collective-permute-start = (f32[80,128]{1,0:T(8,128)S(1)}, f32[80,128]{1,0:T(8,128)S(1)}, u32[]{:S(2)}, u32[]{:S(2)}) collective-permute-start(f32[80,128]{1,0:T(8,128)S(1)} %shard_map.115.refs_0_), channel_id=1, source_target_pairs={{0,1},{1,0},{2,3},{3,2},{4,5},{5,4},{6,7},{7,6},{8,9},{9,8},{10,11... | collective-permute-start | bytes 122888 | tf_op jit(solution)/shard_map/ppermute | solution.py:971
  28.3 1.2 %collective-permute-start.4 = (f32[80,128]{1,0:T(8,128)S(1)}, f32[80,128]{1,0:T(8,128)S(1)}, u32[]{:S(2)}, u32[]{:S(2)}) collective-permute-start(f32[80,128]{1,0:T(8,128)S(1)} %collective-permute-done.1.refs_2_), channel_id=1, source_target_pairs={{0,1},{1,0},{2,3},{3,2},{4,5},{5,4},{6,7},{7,6},{8,9},{9,8},{10,11... | collective-permute-start | bytes 122888 | tf_op jit(solution)/shard_map/ppermute | solution.py:971
  31.2 10.3 %all-to-all-start.1 = ((f32[8,48,128]{2,1,0:T(8,128)}), f32[8,48,128]{2,1,0:T(8,128)S(1)}, u32[]{:S(2)}, u32[]{:S(2)}) async-start(f32[8,48,128]{2,1,0:T(8,128)} %bitcast.2), calls=%async_computation.1 | async-start | bytes 393216 | tf_op jit(solution)/shard_map/all_to_all | solution.py:883

commit v12 on v10

--- a/solution.py
+++ b/solution.py
@@ -173,7 +173,7 @@
 
 
 def middle_first(slabs):
-    return sorted(range(slabs), key=lambda p: (abs(2 * p - slabs + 1), p))
+    return sorted(range(slabs), key=lambda p: (abs(2 * p - slabs + 1), -p))
 
 
 class Slices:

time: 42.3 us -> 42.6 us (level)
  starting transfers between devices: 17.8 us -> 19.2 us
  waiting for transfers between devices: 12.4 us -> 11.3 us
    all_to_all x2, waiting for transfers between devices: 10.1 us -> 9.05 us  [exchange(): lax.all_to_all(message, axis, 0, 0, axis_index_groups=groups, tiled=True)]
    ppermute x1, starting transfers between devices: 2.46 us -> 3.36 us  [local(): below = lax.ppermute(up, 'pipe', forward)]
    all_to_all x2, starting transfers between devices: 12.2 us -> 12.7 us  [exchange(): lax.all_to_all(message, axis, 0, 0, axis_index_groups=groups, tiled=True)]
where the time goes in v12:
time: 42.6 us; the launch traced here: 42.2 us
  starting transfers between devices  19.2 us (45%)
  waiting for transfers between devices  11.3 us (27%)
  Pallas kernels  11 us (26%)
  between operations  0.73 us (2%)
    all_to_all x2, starting transfers between devices, exchange(): lax.all_to_all(message, axis, 0, 0, axis_index_groups=groups, tiled=True)  12.7 us
    pallas_call x7, Pallas kernels, call(): pl.pallas_call(kernel, out_shape=[jax.ShapeDtypeStruct(shape, jnp.float32...  11 us
    all_to_all x2, waiting for transfers between devices, exchange(): lax.all_to_all(message, axis, 0, 0, axis_index_groups=groups, tiled=True)  9.05 us
    ppermute x1, starting transfers between devices, local(): below = lax.ppermute(up, 'pipe', forward)  3.36 us
    ppermute x3, waiting for transfers between devices, local(): lax.ppermute(image_values, 'cross', [(i, i ^ u) for i in range(cross)])  2.29 us
    ppermute x3, starting transfers between devices, local(): lax.ppermute(image_values, 'cross', [(i, i ^ u) for i in range(cross)])  1.85 us
    ppermute x1, starting transfers between devices, local(): above = lax.ppermute(down, 'pipe', [(j, i) for i, j in forward])  1.29 us
  transfers between devices with their start and end apart: 7, of which 4 were waited for; matrix products, arithmetic and copies ran while one was open for 0% of the time, Pallas kernels for 8%

profile of v12, /device:TPU:0, one launch (start us, length us, event | category | flops | bytes accessed | tf_op | source)
XLA Modules:
  0.0 42.2 jit_solution(1691550319983599352)
XLA Ops:
  0.6 0.0 copy-start.2
  0.6 0.0 copy-start
  0.7 4.8 %shard_map.113 = (f32[832,128]{1,0:T(8,128)}, f32[1664,128]{1,0:T(8,128)}, f32[96,128]{1,0:T(8,128)}, f32[96,128]{1,0:T(8,128)}) custom-call(f32[16,2304]{1,0:T(8,128)} %face_hbm.1, f32[16,2304]{1,0:T(8,128)} %courant_hbm.1, f32[8,192,128]{2,1,0:T(8,128)} %constant.2.clone.tables_hbm, s32[128]{0:T(128)} %cell_hbm.1, s32[128]{0:T(128)} %owner_hbm.1, ...), custom_call_target="tpu_custom_call" | custom-call | tf_op jit(solution)/shard_map/pallas_call | solution.py:871
  5.5 0.0 copy-start.1
  5.5 8.0 %all-to-all-start = ((f32[8,104,128]{2,1,0:T(8,128)}), f32[8,104,128]{2,1,0:T(8,128)S(1)}, u32[]{:S(2)}, u32[]{:S(2)}) async-start(f32[8,104,128]{2,1,0:T(8,128)} %bitcast.8), calls=%async_computation | async-start | bytes 851968 | tf_op jit(solution)/shard_map/all_to_all | solution.py:883
  13.5 3.4 %collective-permute-start = (f32[96,128]{1,0:T(8,128)}, f32[96,128]{1,0:T(8,128)S(1)}, u32[]{:S(2)}, u32[]{:S(2)}) collective-permute-start(f32[96,128]{1,0:T(8,128)} %get-tuple-element.12), channel_id=1, source_target_pairs={{0,4},{4,8},{8,12},{12,16},{16,20},{20,24},{24,28},{1,5},{5,9},{9,... | collective-permute-start | bytes 147464 | tf_op jit(solution)/shard_map/ppermute | solution.py:947
  16.8 1.3 %collective-permute-start.1 = (f32[96,128]{1,0:T(8,128)}, f32[96,128]{1,0:T(8,128)S(1)}, u32[]{:S(2)}, u32[]{:S(2)}) collective-permute-start(f32[96,128]{1,0:T(8,128)} %get-tuple-element.13), channel_id=1, source_target_pairs={{4,0},{8,4},{12,8},{16,12},{20,16},{24,20},{28,24},{5,1},{9,5},{13... | collective-permute-start | bytes 147464 | tf_op jit(solution)/shard_map/ppermute | solution.py:948
  18.1 5.7 %all-to-all-done = f32[8,104,128]{2,1,0:T(8,128)S(1)} async-done(((f32[8,104,128]{2,1,0:T(8,128)}), f32[8,104,128]{2,1,0:T(8,128)S(1)}, u32[]{:S(2)}, u32[]{:S(2)}) %all-to-all-start) | async-done | bytes 426016 | tf_op jit(solution)/shard_map/all_to_all | solution.py:883
  23.9 0.0 collective-permute-start.4
  23.9 1.6 %collective-permute-start.3 = (f32[80,128]{1,0:T(8,128)S(1)}, f32[80,128]{1,0:T(8,128)S(1)}, u32[]{:S(2)}, u32[]{:S(2)}) collective-permute-start(f32[80,128]{1,0:T(8,128)S(1)} %shard_map.115.refs_0_), channel_id=1, source_target_pairs={{0,2},{1,3},{2,0},{3,1},{4,6},{5,7},{6,4},{7,5},{8,10},{9,11},{10,... | collective-permute-start | bytes 122888 | tf_op jit(solution)/shard_map/ppermute | solution.py:968
  25.4 0.3 collective-permute-start.2
  25.7 0.0 collective-permute-done.below_ref
  25.7 0.0 collective-permute-done.1.above_ref
  25.7 0.2 shard_map.114
  26.0 1.7 %collective-permute-done.4.refs_3_ = f32[80,128]{1,0:T(8,128)S(1)} collective-permute-done((f32[80,128]{1,0:T(8,128)S(1)}, f32[80,128]{1,0:T(8,128)S(1)}, u32[]{:S(2)}, u32[]{:S(2)}) %collective-permute-start.4) | collective-permute-done | bytes 40992 | tf_op jit(solution)/shard_map/ppermute | solution.py:968
  27.7 0.6 %collective-permute-done.3.refs_2_ = f32[80,128]{1,0:T(8,128)S(1)} collective-permute-done((f32[80,128]{1,0:T(8,128)S(1)}, f32[80,128]{1,0:T(8,128)S(1)}, u32[]{:S(2)}, u32[]{:S(2)}) %collective-permute-start.3) | collective-permute-done | bytes 40992 | tf_op jit(solution)/shard_map/ppermute | solution.py:968
  28.2 0.0 collective-permute-done.2.refs_1_
  28.3 1.6 %shard_map.116 = f32[384,128]{1,0:T(8,128)} custom-call(f32[832,128]{1,0:T(8,128)S(1)} %bitcast.6, f32[320,128]{1,0:T(8,128)S(1)} %get-tuple-element.15.rest_ref, f32[256,128]{1,0:T(8,128)S(1)} %get-tuple-element.16.chain_ref, f32[80,128]{1,0:T(8,128)S(1)} %shard_map.115.refs_0_, f32[80,128]{1,0:T(8,128)S(1)} %collective-permute-done.2.refs_1_, ...), custom_call_target="tpu_custom_call" | custom-call | tf_op jit(solution)/shard_map/pallas_call | solution.py:871
  29.9 4.7 %all-to-all-start.1 = ((f32[8,48,128]{2,1,0:T(8,128)}), f32[8,48,128]{2,1,0:T(8,128)S(1)}, u32[]{:S(2)}, u32[]{:S(2)}) async-start(f32[8,48,128]{2,1,0:T(8,128)} %bitcast.2), calls=%async_computation.1 | async-start | bytes 393216 | tf_op jit(solution)/shard_map/all_to_all | solution.py:883
  34.6 0.0 copy-done.2
  34.6 0.0 copy-done
  34.6 0.0 copy-done.1
  34.6 0.8 %shard_map.117.ready_ref = f32[4544,128]{1,0:T(8,128)S(1)} custom-call(f32[1664,128]{1,0:T(8,128)S(1)} %copy-done.1, s32[16,2304]{1,0:T(8,128)S(1)} %copy-done.2, f32[5,16,2304]{2,1,0:T(8,128)S(1)} %copy-done), custom_call_target="tpu_custom_call" | custom-call | tf_op jit(solution)/shard_map/pallas_call | solution.py:871
  35.4 2.2 %shard_map.118.done_ref = f32[4252,128]{1,0:T(8,128)S(1)} custom-call(f32[4544,128]{1,0:T(8,128)S(1)} %shard_map.117.ready_ref, f32[96,128]{1,0:T(8,128)S(1)} %collective-permute-done.below_ref, f32[96,128]{1,0:T(8,128)S(1)} %collective-permute-done.1.above_ref, f32[80,128]{1,0:T(8,128)S(1)} %shard_map.115.refs_0_, ...), custom_call_target="tpu_custom_call" | custom-call | tf_op jit(solution)/shard_map/pallas_call | solution.py:871
  37.6 3.3 %all-to-all-done.1 = f32[8,48,128]{2,1,0:T(8,128)S(1)} async-done(((f32[8,48,128]{2,1,0:T(8,128)}), f32[8,48,128]{2,1,0:T(8,128)S(1)}, u32[]{:S(2)}, u32[]{:S(2)}) %all-to-all-start.1) | async-done | bytes 196640 | tf_op jit(solution)/shard_map/all_to_all | solution.py:883
  40.9 1.3 %shard_map.119 = (f32[5,16,2304]{2,1,0:T(8,128)}, f32[5,16,2304]{2,1,0:T(8,128)}) custom-call(f32[384,128]{1,0:T(8,128)S(1)} %bitcast.7, f32[4252,128]{1,0:T(8,128)S(1)} %shard_map.118.done_ref), custom_call_target="tpu_custom_call" | custom-call | tf_op jit(solution)/shard_map/pallas_call | solution.py:871
  (1 shorter events, 0.0 us)
Async XLA Ops:
  0.6 34.0 %copy-start.2 = (s32[16,2304]{1,0:T(8,128)S(1)}, s32[16,2304]{1,0:T(8,128)}, u32[]{:S(2)}) copy-start(s32[16,2304]{1,0:T(8,128)} %mask_ref.1) | copy-start | bytes 442372
  0.6 34.0 %copy-start = (f32[5,16,2304]{2,1,0:T(8,128)S(1)}, f32[5,16,2304]{2,1,0:T(8,128)}, u32[]{:S(2)}) copy-start(f32[5,16,2304]{2,1,0:T(8,128)} %state_ref.1) | copy-start | bytes 2211844
  5.5 29.1 %copy-start.1 = (f32[1664,128]{1,0:T(8,128)S(1)}, f32[1664,128]{1,0:T(8,128)}, u32[]{:S(2)}) copy-start(f32[1664,128]{1,0:T(8,128)} %get-tuple-element.17.stay_ref) | copy-start | bytes 2555908
  5.5 18.4 %all-to-all-start = ((f32[8,104,128]{2,1,0:T(8,128)}), f32[8,104,128]{2,1,0:T(8,128)S(1)}, u32[]{:S(2)}, u32[]{:S(2)}) async-start(f32[8,104,128]{2,1,0:T(8,128)} %bitcast.8), calls=%async_computation | async-start | bytes 851968 | tf_op jit(solution)/shard_map/all_to_all | solution.py:883
  13.5 12.3 %collective-permute-start = (f32[96,128]{1,0:T(8,128)}, f32[96,128]{1,0:T(8,128)S(1)}, u32[]{:S(2)}, u32[]{:S(2)}) collective-permute-start(f32[96,128]{1,0:T(8,128)} %get-tuple-element.12), channel_id=1, source_target_pairs={{0,4},{4,8},{8,12},{12,16},{16,20},{20,24},{24,28},{1,5},{5,9},{9,... | collective-permute-start | bytes 147464 | tf_op jit(solution)/shard_map/ppermute | solution.py:947
  16.8 8.9 %collective-permute-start.1 = (f32[96,128]{1,0:T(8,128)}, f32[96,128]{1,0:T(8,128)S(1)}, u32[]{:S(2)}, u32[]{:S(2)}) collective-permute-start(f32[96,128]{1,0:T(8,128)} %get-tuple-element.13), channel_id=1, source_target_pairs={{4,0},{8,4},{12,8},{16,12},{20,16},{24,20},{28,24},{5,1},{9,5},{13... | collective-permute-start | bytes 147464 | tf_op jit(solution)/shard_map/ppermute | solution.py:948
  23.9 3.8 %collective-permute-start.4 = (f32[80,128]{1,0:T(8,128)S(1)}, f32[80,128]{1,0:T(8,128)S(1)}, u32[]{:S(2)}, u32[]{:S(2)}) collective-permute-start(f32[80,128]{1,0:T(8,128)S(1)} %shard_map.115.refs_0_), channel_id=1, source_target_pairs={{0,3},{1,2},{2,1},{3,0},{4,7},{5,6},{6,5},{7,4},{8,11},{9,10},{10,... | collective-permute-start | bytes 122888 | tf_op jit(solution)/shard_map/ppermute | solution.py:968
  23.9 4.4 %collective-permute-start.3 = (f32[80,128]{1,0:T(8,128)S(1)}, f32[80,128]{1,0:T(8,128)S(1)}, u32[]{:S(2)}, u32[]{:S(2)}) collective-permute-start(f32[80,128]{1,0:T(8,128)S(1)} %shard_map.115.refs_0_), channel_id=1, source_target_pairs={{0,2},{1,3},{2,0},{3,1},{4,6},{5,7},{6,4},{7,5},{8,10},{9,11},{10,... | collective-permute-start | bytes 122888 | tf_op jit(solution)/shard_map/ppermute | solution.py:968
  25.4 2.8 %collective-permute-start.2 = (f32[80,128]{1,0:T(8,128)S(1)}, f32[80,128]{1,0:T(8,128)S(1)}, u32[]{:S(2)}, u32[]{:S(2)}) collective-permute-start(f32[80,128]{1,0:T(8,128)S(1)} %shard_map.115.refs_0_), channel_id=1, source_target_pairs={{0,1},{1,0},{2,3},{3,2},{4,5},{5,4},{6,7},{7,6},{8,9},{9,8},{10,11... | collective-permute-start | bytes 122888 | tf_op jit(solution)/shard_map/ppermute | solution.py:968
  29.9 11.1 %all-to-all-start.1 = ((f32[8,48,128]{2,1,0:T(8,128)}), f32[8,48,128]{2,1,0:T(8,128)S(1)}, u32[]{:S(2)}, u32[]{:S(2)}) async-start(f32[8,48,128]{2,1,0:T(8,128)} %bitcast.2), calls=%async_computation.1 | async-start | bytes 393216 | tf_op jit(solution)/shard_map/all_to_all | solution.py:883

commit v13 on v12

--- a/solution.py
+++ b/solution.py
@@ -173,7 +173,12 @@
 
 
 def middle_first(slabs):
-    return sorted(range(slabs), key=lambda p: (abs(2 * p - slabs + 1), -p))
+    half = slabs // 2
+    order = []
+    for p in range(half - 1, -1, -1):
+        mirror = slabs - 1 - p
+        order += [p, mirror ^ 1]
+    return order
 
 
 class Slices:

time: 42.6 us -> 43.2 us (1.014)
  waiting for transfers between devices: 11.3 us -> 12.2 us
    ppermute x1, starting transfers between devices: 3.36 us -> 2.46 us  [local(): below = lax.ppermute(up, 'pipe', forward)]
    all_to_all x2, waiting for transfers between devices: 9.05 us -> 9.9 us  [exchange(): lax.all_to_all(message, axis, 0, 0, axis_index_groups=groups, tiled=True)]
    all_to_all x2, starting transfers between devices: 12.7 us -> 13.3 us  [exchange(): lax.all_to_all(message, axis, 0, 0, axis_index_groups=groups, tiled=True)]
where the time goes in v13:
time: 43.2 us; the launch traced here: 42.8 us
  starting transfers between devices  18.9 us (44%)
  waiting for transfers between devices  12.2 us (28%)
  Pallas kernels  11 us (25%)
  between operations  0.73 us (2%)
    all_to_all x2, starting transfers between devices, exchange(): lax.all_to_all(message, axis, 0, 0, axis_index_groups=groups, tiled=True)  13.3 us
    pallas_call x7, Pallas kernels, call(): pl.pallas_call(kernel, out_shape=[jax.ShapeDtypeStruct(shape, jnp.float32...  11 us
    all_to_all x2, waiting for transfers between devices, exchange(): lax.all_to_all(message, axis, 0, 0, axis_index_groups=groups, tiled=True)  9.9 us
    ppermute x1, starting transfers between devices, local(): below = lax.ppermute(up, 'pipe', forward)  2.46 us
    ppermute x3, waiting for transfers between devices, local(): lax.ppermute(image_values, 'cross', [(i, i ^ u) for i in range(cross)])  2.29 us
    ppermute x3, starting transfers between devices, local(): lax.ppermute(image_values, 'cross', [(i, i ^ u) for i in range(cross)])  1.85 us
    ppermute x1, starting transfers between devices, local(): above = lax.ppermute(down, 'pipe', [(j, i) for i, j in forward])  1.29 us
  transfers between devices with their start and end apart: 7, of which 4 were waited for; matrix products, arithmetic and copies ran while one was open for 0% of the time, Pallas kernels for 8%

profile of v13, /device:TPU:0, one launch (start us, length us, event | category | flops | bytes accessed | tf_op | source)
XLA Modules:
  0.0 42.8 jit_solution(4754560019024768680)
XLA Ops:
  0.6 0.0 copy-start.2
  0.6 0.0 copy-start
  0.7 4.8 %shard_map.113 = (f32[832,128]{1,0:T(8,128)}, f32[1664,128]{1,0:T(8,128)}, f32[96,128]{1,0:T(8,128)}, f32[96,128]{1,0:T(8,128)}) custom-call(f32[16,2304]{1,0:T(8,128)} %face_hbm.1, f32[16,2304]{1,0:T(8,128)} %courant_hbm.1, f32[8,192,128]{2,1,0:T(8,128)} %constant.2.clone.tables_hbm, s32[128]{0:T(128)} %cell_hbm.1, s32[128]{0:T(128)} %owner_hbm.1, ...), custom_call_target="tpu_custom_call" | custom-call | tf_op jit(solution)/shard_map/pallas_call | solution.py:876
  5.5 0.0 copy-start.1
  5.5 8.0 %all-to-all-start = ((f32[8,104,128]{2,1,0:T(8,128)}), f32[8,104,128]{2,1,0:T(8,128)S(1)}, u32[]{:S(2)}, u32[]{:S(2)}) async-start(f32[8,104,128]{2,1,0:T(8,128)} %bitcast.8), calls=%async_computation | async-start | bytes 851968 | tf_op jit(solution)/shard_map/all_to_all | solution.py:888
  13.5 2.5 %collective-permute-start = (f32[96,128]{1,0:T(8,128)}, f32[96,128]{1,0:T(8,128)S(1)}, u32[]{:S(2)}, u32[]{:S(2)}) collective-permute-start(f32[96,128]{1,0:T(8,128)} %get-tuple-element.12), channel_id=1, source_target_pairs={{0,4},{4,8},{8,12},{12,16},{16,20},{20,24},{24,28},{1,5},{5,9},{9,... | collective-permute-start | bytes 147464 | tf_op jit(solution)/shard_map/ppermute | solution.py:952
  15.9 1.3 %collective-permute-start.1 = (f32[96,128]{1,0:T(8,128)}, f32[96,128]{1,0:T(8,128)S(1)}, u32[]{:S(2)}, u32[]{:S(2)}) collective-permute-start(f32[96,128]{1,0:T(8,128)} %get-tuple-element.13), channel_id=1, source_target_pairs={{4,0},{8,4},{12,8},{16,12},{20,16},{24,20},{28,24},{5,1},{9,5},{13... | collective-permute-start | bytes 147464 | tf_op jit(solution)/shard_map/ppermute | solution.py:953
  17.2 6.6 %all-to-all-done = f32[8,104,128]{2,1,0:T(8,128)S(1)} async-done(((f32[8,104,128]{2,1,0:T(8,128)}), f32[8,104,128]{2,1,0:T(8,128)S(1)}, u32[]{:S(2)}, u32[]{:S(2)}) %all-to-all-start) | async-done | bytes 426016 | tf_op jit(solution)/shard_map/all_to_all | solution.py:888
  23.9 0.0 collective-permute-start.4
  23.9 1.6 %collective-permute-start.3 = (f32[80,128]{1,0:T(8,128)S(1)}, f32[80,128]{1,0:T(8,128)S(1)}, u32[]{:S(2)}, u32[]{:S(2)}) collective-permute-start(f32[80,128]{1,0:T(8,128)S(1)} %shard_map.115.refs_0_), channel_id=1, source_target_pairs={{0,2},{1,3},{2,0},{3,1},{4,6},{5,7},{6,4},{7,5},{8,10},{9,11},{10,... | collective-permute-start | bytes 122888 | tf_op jit(solution)/shard_map/ppermute | solution.py:973
  25.4 0.3 collective-permute-start.2
  25.7 0.0 collective-permute-done.below_ref
  25.7 0.0 collective-permute-done.1.above_ref
  25.7 0.2 shard_map.114
  26.0 1.7 %collective-permute-done.4.refs_3_ = f32[80,128]{1,0:T(8,128)S(1)} collective-permute-done((f32[80,128]{1,0:T(8,128)S(1)}, f32[80,128]{1,0:T(8,128)S(1)}, u32[]{:S(2)}, u32[]{:S(2)}) %collective-permute-start.4) | collective-permute-done | bytes 40992 | tf_op jit(solution)/shard_map/ppermute | solution.py:973
  27.7 0.6 %collective-permute-done.3.refs_2_ = f32[80,128]{1,0:T(8,128)S(1)} collective-permute-done((f32[80,128]{1,0:T(8,128)S(1)}, f32[80,128]{1,0:T(8,128)S(1)}, u32[]{:S(2)}, u32[]{:S(2)}) %collective-permute-start.3) | collective-permute-done | bytes 40992 | tf_op jit(solution)/shard_map/ppermute | solution.py:973
  28.3 0.0 collective-permute-done.2.refs_1_
  28.3 1.7 %shard_map.116 = f32[384,128]{1,0:T(8,128)} custom-call(f32[832,128]{1,0:T(8,128)S(1)} %bitcast.6, f32[320,128]{1,0:T(8,128)S(1)} %get-tuple-element.15.rest_ref, f32[256,128]{1,0:T(8,128)S(1)} %get-tuple-element.16.chain_ref, f32[80,128]{1,0:T(8,128)S(1)} %shard_map.115.refs_0_, f32[80,128]{1,0:T(8,128)S(1)} %collective-permute-done.2.refs_1_, ...), custom_call_target="tpu_custom_call" | custom-call | tf_op jit(solution)/shard_map/pallas_call | solution.py:876
  29.9 5.3 %all-to-all-start.1 = ((f32[8,48,128]{2,1,0:T(8,128)}), f32[8,48,128]{2,1,0:T(8,128)S(1)}, u32[]{:S(2)}, u32[]{:S(2)}) async-start(f32[8,48,128]{2,1,0:T(8,128)} %bitcast.2), calls=%async_computation.1 | async-start | bytes 393216 | tf_op jit(solution)/shard_map/all_to_all | solution.py:888
  35.2 0.0 copy-done.2
  35.2 0.0 copy-done
  35.2 0.0 copy-done.1
  35.2 0.8 %shard_map.117.ready_ref = f32[4544,128]{1,0:T(8,128)S(1)} custom-call(f32[1664,128]{1,0:T(8,128)S(1)} %copy-done.1, s32[16,2304]{1,0:T(8,128)S(1)} %copy-done.2, f32[5,16,2304]{2,1,0:T(8,128)S(1)} %copy-done), custom_call_target="tpu_custom_call" | custom-call | tf_op jit(solution)/shard_map/pallas_call | solution.py:876
  36.0 2.2 %shard_map.118.done_ref = f32[4252,128]{1,0:T(8,128)S(1)} custom-call(f32[4544,128]{1,0:T(8,128)S(1)} %shard_map.117.ready_ref, f32[96,128]{1,0:T(8,128)S(1)} %collective-permute-done.below_ref, f32[96,128]{1,0:T(8,128)S(1)} %collective-permute-done.1.above_ref, f32[80,128]{1,0:T(8,128)S(1)} %shard_map.115.refs_0_, ...), custom_call_target="tpu_custom_call" | custom-call | tf_op jit(solution)/shard_map/pallas_call | solution.py:876
  38.2 3.3 %all-to-all-done.1 = f32[8,48,128]{2,1,0:T(8,128)S(1)} async-done(((f32[8,48,128]{2,1,0:T(8,128)}), f32[8,48,128]{2,1,0:T(8,128)S(1)}, u32[]{:S(2)}, u32[]{:S(2)}) %all-to-all-start.1) | async-done | bytes 196640 | tf_op jit(solution)/shard_map/all_to_all | solution.py:888
  41.5 1.3 %shard_map.119 = (f32[5,16,2304]{2,1,0:T(8,128)}, f32[5,16,2304]{2,1,0:T(8,128)}) custom-call(f32[384,128]{1,0:T(8,128)S(1)} %bitcast.7, f32[4252,128]{1,0:T(8,128)S(1)} %shard_map.118.done_ref), custom_call_target="tpu_custom_call" | custom-call | tf_op jit(solution)/shard_map/pallas_call | solution.py:876
  (1 shorter events, 0.0 us)
Async XLA Ops:
  0.6 34.6 %copy-start.2 = (s32[16,2304]{1,0:T(8,128)S(1)}, s32[16,2304]{1,0:T(8,128)}, u32[]{:S(2)}) copy-start(s32[16,2304]{1,0:T(8,128)} %mask_ref.1) | copy-start | bytes 442372
  0.6 34.6 %copy-start = (f32[5,16,2304]{2,1,0:T(8,128)S(1)}, f32[5,16,2304]{2,1,0:T(8,128)}, u32[]{:S(2)}) copy-start(f32[5,16,2304]{2,1,0:T(8,128)} %state_ref.1) | copy-start | bytes 2211844
  5.5 29.7 %copy-start.1 = (f32[1664,128]{1,0:T(8,128)S(1)}, f32[1664,128]{1,0:T(8,128)}, u32[]{:S(2)}) copy-start(f32[1664,128]{1,0:T(8,128)} %get-tuple-element.17.stay_ref) | copy-start | bytes 2555908
  5.5 18.4 %all-to-all-start = ((f32[8,104,128]{2,1,0:T(8,128)}), f32[8,104,128]{2,1,0:T(8,128)S(1)}, u32[]{:S(2)}, u32[]{:S(2)}) async-start(f32[8,104,128]{2,1,0:T(8,128)} %bitcast.8), calls=%async_computation | async-start | bytes 851968 | tf_op jit(solution)/shard_map/all_to_all | solution.py:888
  13.5 12.3 %collective-permute-start = (f32[96,128]{1,0:T(8,128)}, f32[96,128]{1,0:T(8,128)S(1)}, u32[]{:S(2)}, u32[]{:S(2)}) collective-permute-start(f32[96,128]{1,0:T(8,128)} %get-tuple-element.12), channel_id=1, source_target_pairs={{0,4},{4,8},{8,12},{12,16},{16,20},{20,24},{24,28},{1,5},{5,9},{9,... | collective-permute-start | bytes 147464 | tf_op jit(solution)/shard_map/ppermute | solution.py:952
  15.9 9.8 %collective-permute-start.1 = (f32[96,128]{1,0:T(8,128)}, f32[96,128]{1,0:T(8,128)S(1)}, u32[]{:S(2)}, u32[]{:S(2)}) collective-permute-start(f32[96,128]{1,0:T(8,128)} %get-tuple-element.13), channel_id=1, source_target_pairs={{4,0},{8,4},{12,8},{16,12},{20,16},{24,20},{28,24},{5,1},{9,5},{13... | collective-permute-start | bytes 147464 | tf_op jit(solution)/shard_map/ppermute | solution.py:953
  23.9 3.8 %collective-permute-start.4 = (f32[80,128]{1,0:T(8,128)S(1)}, f32[80,128]{1,0:T(8,128)S(1)}, u32[]{:S(2)}, u32[]{:S(2)}) collective-permute-start(f32[80,128]{1,0:T(8,128)S(1)} %shard_map.115.refs_0_), channel_id=1, source_target_pairs={{0,3},{1,2},{2,1},{3,0},{4,7},{5,6},{6,5},{7,4},{8,11},{9,10},{10,... | collective-permute-start | bytes 122888 | tf_op jit(solution)/shard_map/ppermute | solution.py:973
  23.9 4.4 %collective-permute-start.3 = (f32[80,128]{1,0:T(8,128)S(1)}, f32[80,128]{1,0:T(8,128)S(1)}, u32[]{:S(2)}, u32[]{:S(2)}) collective-permute-start(f32[80,128]{1,0:T(8,128)S(1)} %shard_map.115.refs_0_), channel_id=1, source_target_pairs={{0,2},{1,3},{2,0},{3,1},{4,6},{5,7},{6,4},{7,5},{8,10},{9,11},{10,... | collective-permute-start | bytes 122888 | tf_op jit(solution)/shard_map/ppermute | solution.py:973
  25.4 2.8 %collective-permute-start.2 = (f32[80,128]{1,0:T(8,128)S(1)}, f32[80,128]{1,0:T(8,128)S(1)}, u32[]{:S(2)}, u32[]{:S(2)}) collective-permute-start(f32[80,128]{1,0:T(8,128)S(1)} %shard_map.115.refs_0_), channel_id=1, source_target_pairs={{0,1},{1,0},{2,3},{3,2},{4,5},{5,4},{6,7},{7,6},{8,9},{9,8},{10,11... | collective-permute-start | bytes 122888 | tf_op jit(solution)/shard_map/ppermute | solution.py:973
  29.9 11.6 %all-to-all-start.1 = ((f32[8,48,128]{2,1,0:T(8,128)}), f32[8,48,128]{2,1,0:T(8,128)S(1)}, u32[]{:S(2)}, u32[]{:S(2)}) async-start(f32[8,48,128]{2,1,0:T(8,128)} %bitcast.2), calls=%async_computation.1 | async-start | bytes 393216 | tf_op jit(solution)/shard_map/all_to_all | solution.py:888
